TPU v7x, 512 devices: a whole 4x4x16 slice. The times are simulated.
512 devices in a mesh: wall: 16 (over y, x_lo, core), stream: 32 (over z, x_hi).
Axes of the slice: x: 4 (x_hi: 2, x_lo: 2; x = x_hi * 2 + x_lo), y: 4, z: 16, core: 2. Of those that a mesh axis runs over, the one named last changes fastest.
Arguments:
- concentration: float32 [2, 256, 128, 512], P(None, 'stream', 'wall'), may hold values from 0.2 to 2
- velocity: float32 [3, 256, 128, 512], P(None, 'stream', 'wall'), may hold values from -5 to 5
- potential: float32 [256, 128, 512], P('stream', 'wall'), may hold values from -6 to 6
Outputs:
- updated: float32 [2, 256, 128, 512], P(None, 'stream', 'wall')
All inputs are finite; a program needn't handle non-finite values.
Results may differ from a plain program's by a relative error of at most 0.0003.
Values sent between devices are 32-bit elements; how exact they have to be, the bound alone decides.
No kernel may reach another device: no remote copies, remote signals or barrier semaphores. Data moves between devices by JAX's collectives and lax.ppermute only.
A program may use at most 64 MiB of HBM per device.

v0:
```python
import jax
import jax.numpy as jnp
from jax import lax
from jax.sharding import PartitionSpec as P

ADVECT_STEP = 0.2
DRIFT_RATES = (1.0, -0.5)


def padded(x, sides, width, wrap):
    for axis, dim in sides:
        peers, length = (lax.axis_size(axis), x.shape[dim])
        up = [(i, (i + 1) % peers) for i in range(peers if wrap else peers - 1)]
        down = [(j, i) for i, j in up]
        last = lax.slice_in_dim(x, length - width, length, axis=dim)
        leading = lax.slice_in_dim(x, 0, width, axis=dim)
        before = lax.ppermute(last, axis, up)
        after = lax.ppermute(leading, axis, down)
        x = jnp.concatenate([before, x, after], axis=dim)
    return x


def face_divergence(conc_pad, speed_pad, volt_pad, dimension):
    face_count = speed_pad.shape[dimension] - 1
    face_speed = 0.5 * (
        lax.slice_in_dim(speed_pad, 0, face_count, axis=dimension)
        + lax.slice_in_dim(speed_pad, 1, face_count + 1, axis=dimension)
    )
    voltage_step = lax.slice_in_dim(volt_pad, 1, face_count + 1, axis=dimension) - lax.slice_in_dim(
        volt_pad, 0, face_count, axis=dimension
    )
    drift_rate = jnp.array(DRIFT_RATES, jnp.float32).reshape((2,) + (1,) * face_speed.ndim)
    mean_conc = 0.5 * (
        lax.slice_in_dim(conc_pad, 0, face_count, axis=dimension + 1)
        + lax.slice_in_dim(conc_pad, 1, face_count + 1, axis=dimension + 1)
    )
    face_flux = mean_conc * (face_speed[None] - drift_rate * voltage_step[None])
    return lax.slice_in_dim(face_flux, 1, face_count, axis=dimension + 1) - lax.slice_in_dim(
        face_flux, 0, face_count - 1, axis=dimension + 1
    )


def block_inverse(line_length, rates):
    rate_row = jnp.array(rates, jnp.float32)[:, None]
    filled = jnp.ones((2, line_length), jnp.float32)
    indices = jnp.arange(line_length)[None, :]
    below_diag = jnp.where(indices == 0, 0.0, -rate_row * filled)
    above_diag = jnp.where(indices == line_length - 1, 0.0, -rate_row * filled)
    middle = (1.0 + 2.0 * rate_row) * filled
    identity = jnp.broadcast_to(
        jnp.eye(line_length, dtype=jnp.float32), (2, line_length, line_length)
    )
    return lax.linalg.tridiagonal_solve(below_diag, middle, above_diag, identity)


def sweep(leading, trailing, corner, across, start_value, finish_value):

    def forward(carry, ends):
        levels, weight = carry
        top_end, bottom_end = ends
        divisor = 1.0 - corner * weight
        leader = (top_end + corner * levels) / divisor
        factor = across / divisor
        level_next = bottom_end + across * levels + across * weight * leader
        weight_next = corner + across * weight * factor
        return ((level_next, weight_next), (leader, factor, level_next, weight_next))

    level_start = jnp.zeros_like(leading[0]) + start_value
    weight_start = jnp.zeros_like(leading[0])
    closing, (leaders, factors, level_all, weight_all) = lax.scan(
        forward, (level_start, weight_start), (leading, trailing)
    )

    def backward(following, terms):
        leader, factor, levels, weight = terms
        solved = leader + factor * following
        return (solved, (levels + weight * following, solved))

    opening, (last_values, first_values) = lax.scan(
        backward,
        jnp.zeros_like(leading[0]) + finish_value,
        (leaders, factors, level_all, weight_all),
        reverse=True,
    )
    return (last_values, first_values)


def open_links(leading, trailing, corner, across):
    last_values, first_values = sweep(leading, trailing, corner, across, 0.0, 0.0)
    nothing = jnp.zeros_like(leading[:1])
    return (
        jnp.concatenate([nothing, last_values[:-1]], 0),
        jnp.concatenate([first_values[1:], nothing], 0),
    )


def closed_links(leading, trailing, corner, across):
    last_values, first_values = sweep(leading, trailing, corner, across, 0.0, 0.0)
    unit_data = jnp.zeros((leading.shape[0],) + corner.shape, jnp.float32)
    lasts_entry, firsts_entry = sweep(unit_data, unit_data, corner, across, 1.0, 0.0)
    lasts_leave, firsts_leave = sweep(unit_data, unit_data, corner, across, 0.0, 1.0)
    top_left = 1.0 - lasts_entry[-1]
    top_right = -lasts_leave[-1]
    low_left = -firsts_entry[0]
    low_right = 1.0 - firsts_leave[0]
    determinant = top_left * low_right - top_right * low_left
    entering = (last_values[-1] * low_right - top_right * first_values[0]) / determinant
    leaving = (top_left * first_values[0] - low_left * last_values[-1]) / determinant
    last_values = last_values + entering * lasts_entry + leaving * lasts_leave
    first_values = first_values + entering * firsts_entry + leaving * firsts_leave
    return (
        jnp.concatenate([entering[None], last_values[:-1]], 0),
        jnp.concatenate([first_values[1:], leaving[None]], 0),
    )


def per_device(concentration, velocity, potential):
    width = concentration.shape[1]
    depth = concentration.shape[2]
    stream_pad = padded(
        jnp.stack([concentration[0], concentration[1], velocity[0], potential]),
        (("stream", 1),),
        1,
        True,
    )
    divergence = face_divergence(stream_pad[0:2], stream_pad[2], stream_pad[3], 0)
    wall_pad = padded(
        jnp.stack([concentration[0], concentration[1], velocity[1], potential]),
        (("wall", 2),),
        1,
        False,
    )
    divergence = divergence + face_divergence(wall_pad[0:2], wall_pad[2], wall_pad[3], 1)
    spanwise = jnp.stack([concentration[0], concentration[1], velocity[2], potential])
    span_pad = jnp.concatenate([spanwise[..., -1:], spanwise, spanwise[..., :1]], axis=3)
    divergence = divergence + face_divergence(span_pad[0:2], span_pad[2], span_pad[3], 2)
    predicted = concentration - ADVECT_STEP * divergence
    stream_total = width * lax.axis_size("stream")
    rates_stream = (4.0 * width * width, float(stream_total * stream_total // 25))
    inverse_x = block_inverse(width, rates_stream)
    rate_x = jnp.array(rates_stream, jnp.float32)
    corner_x = (rate_x * inverse_x[:, 0, 0]).reshape(2, 1, 1)
    across_x = (rate_x * inverse_x[:, 0, width - 1]).reshape(2, 1, 1)
    spike_low_x = rate_x[:, None] * inverse_x[:, :, 0]
    spike_high_x = rate_x[:, None] * inverse_x[:, :, width - 1]
    blocked = jnp.einsum("sij,sjzy->sizy", inverse_x, predicted, precision=lax.Precision.HIGHEST)
    leading, trailing = (
        lax.all_gather(blocked[:, 0][None], "stream", axis=0, tiled=True),
        lax.all_gather(blocked[:, width - 1][None], "stream", axis=0, tiled=True),
    )
    prior_all, next_all = closed_links(leading, trailing, corner_x, across_x)
    position = lax.axis_index("stream")
    prior_link = lax.dynamic_index_in_dim(prior_all, position, 0, keepdims=False)
    next_link = lax.dynamic_index_in_dim(next_all, position, 0, keepdims=False)
    streamwise = (
        blocked
        + prior_link[:, None] * spike_low_x[:, :, None, None]
        + next_link[:, None] * spike_high_x[:, :, None, None]
    )
    wall_total = depth * lax.axis_size("wall")
    rates_wall = (4.0 * depth * depth, float(wall_total * wall_total // 16))
    inverse_z = block_inverse(depth, rates_wall)
    rate_z = jnp.array(rates_wall, jnp.float32)
    corner_flat = rate_z * inverse_z[:, 0, 0]
    across_flat = rate_z * inverse_z[:, 0, depth - 1]
    corner_z = corner_flat.reshape(2, 1, 1)
    across_z = across_flat.reshape(2, 1, 1)
    spike_low_z = rate_z[:, None] * inverse_z[:, :, 0]
    spike_high_z = rate_z[:, None] * inverse_z[:, :, depth - 1]
    blocked_z = jnp.einsum("sij,sxjy->sxiy", inverse_z, streamwise, precision=lax.Precision.HIGHEST)
    upper_end = blocked_z[:, :, 0]
    lower_end = blocked_z[:, :, depth - 1]
    leading, trailing = (
        lax.all_gather(upper_end[None], "wall", axis=0, tiled=True),
        lax.all_gather(lower_end[None], "wall", axis=0, tiled=True),
    )
    prior_all, next_all = open_links(leading, trailing, corner_z, across_z)
    position = lax.axis_index("wall")
    prior_link = lax.dynamic_index_in_dim(prior_all, position, 0, keepdims=False)
    next_link = lax.dynamic_index_in_dim(next_all, position, 0, keepdims=False)
    return (
        blocked_z
        + prior_link[:, :, None] * spike_low_z[:, None, :, None]
        + next_link[:, :, None] * spike_high_z[:, None, :, None]
    )


def solution(mesh):
    return jax.shard_map(
        per_device,
        mesh=mesh,
        in_specs=(
            P(None, "stream", "wall", None),
            P(None, "stream", "wall", None),
            P("stream", "wall", None),
        ),
        out_specs=P(None, "stream", "wall", None),
        check_vma=False,
    )
```

profile of v0, /device:TPU:1, one launch (start us, length us, event | category | flops | bytes accessed | tf_op | source)
XLA Modules:
  0.0 457.4 jit_solution(6365256254505280338)
XLA Ops:
  8.0 4.5 collective-permute-start.2
  12.6 5.6 %collective-permute-start.3 = (f32[4,8,1,512]{3,2,1,0:T(1,128)S(1)}, f32[4,8,1,512]{3,2,1,0:T(1,128)S(1)}, u32[]{:S(2)}, u32[]{:S(2)}) collective-permute-start(f32[4,8,1,512]{3,2,1,0:T(1,128)S(1)} %get-tuple-element.1534), channel_id=1, source_target_pairs={{32,0},{64,32},{96,64},{128,96},{160,128},{192,160},{224,192},{256... | collective-permute-start | bytes 196616 | tf_op jit(solution)/shard_map/ppermute | solution.py:18
  18.2 1.9 collective-permute-start
  20.1 9.6 %collective-permute-start.1 = (f32[4,1,8,512]{3,2,1,0:T(8,128)S(1)}, f32[4,1,8,512]{3,2,1,0:T(8,128)S(1)}, u32[]{:S(2)}, u32[]{:S(2)}) collective-permute-start(f32[4,1,8,512]{3,2,1,0:T(8,128)S(1)} %get-tuple-element.1532), channel_id=1, source_target_pairs={{1,0},{2,1},{3,2},{4,3},{5,4},{6,5},{7,6},{8,7},{9,8},{10,9},{11,1... | collective-permute-start | bytes 196616 | tf_op jit(solution)/shard_map/ppermute | solution.py:18
  33.0 1.3 while.162
  34.4 1.2 while.163
  35.8 1.3 while.164
  42.9 1.2 while.165
  52.7 121.5 %all-gather.7.cloned.1.call-done = f32[64,1,8,512]{3,2,1,0:T(8,128)} async-done(((f32[2,1,8,512]{3,2,1,0:T(8,128)}), f32[64,1,8,512]{3,2,1,0:T(8,128)}) %all-gather.7.cloned.1.call-update) | async-done | bytes 1048592 | tf_op jit(solution)/shard_map/all_gather | solution.py:149
  174.1 140.3 %all-gather.9.cloned.1.call-done = f32[64,1,8,512]{3,2,1,0:T(8,128)} async-done(((f32[2,1,8,512]{3,2,1,0:T(8,128)}), f32[64,1,8,512]{3,2,1,0:T(8,128)}) %all-gather.9.cloned.1.call-update) | async-done | bytes 1048592 | tf_op jit(solution)/shard_map/all_gather | solution.py:148
  314.8 1.1 broadcast.6182.clone.4
  316.0 47.3 %while.160 = (s32[]{:T(128)}, f32[2,8,512]{2,1,0:T(8,128)S(1)}, f32[2,8,512]{2,1,0:T(8,128)S(1)}, f32[32,2,8,512]{3,2,1,0:T(8,128)S(1)}, f32[32,2,8,512]{3,2,1,0...) while((s32[]{:T(128)}, f32[2,8,512]{2,1,0:T(8,128)S(1)}, ...), condition=%wide.region_1.2_spmd.clone, body=%wide.region_0.1_spmd.clone.sunk | while | flops 122883 | bytes 329351 | solution.py:70
  316.0 1.5 bitcast_dynamic-update-slice_fusion.16
  317.5 1.5 bitcast_dynamic-update-slice_fusion.16
  318.9 1.5 bitcast_dynamic-update-slice_fusion.16
  320.4 1.5 bitcast_dynamic-update-slice_fusion.16
  321.9 1.5 bitcast_dynamic-update-slice_fusion.16
  323.4 1.5 bitcast_dynamic-update-slice_fusion.16
  324.9 1.5 bitcast_dynamic-update-slice_fusion.16
  326.3 1.5 bitcast_dynamic-update-slice_fusion.16
  327.8 1.5 bitcast_dynamic-update-slice_fusion.16
  329.3 1.5 bitcast_dynamic-update-slice_fusion.16
  330.8 1.5 bitcast_dynamic-update-slice_fusion.16
  332.2 1.5 bitcast_dynamic-update-slice_fusion.16
  333.7 1.5 bitcast_dynamic-update-slice_fusion.16
  335.2 1.5 bitcast_dynamic-update-slice_fusion.16
  336.7 1.5 bitcast_dynamic-update-slice_fusion.16
  338.2 1.5 bitcast_dynamic-update-slice_fusion.16
  339.6 1.5 bitcast_dynamic-update-slice_fusion.16
  341.1 1.5 bitcast_dynamic-update-slice_fusion.16
  342.6 1.5 bitcast_dynamic-update-slice_fusion.16
  344.1 1.5 bitcast_dynamic-update-slice_fusion.16
  345.6 1.5 bitcast_dynamic-update-slice_fusion.16
  347.0 1.5 bitcast_dynamic-update-slice_fusion.16
  348.5 1.5 bitcast_dynamic-update-slice_fusion.16
  350.0 1.5 bitcast_dynamic-update-slice_fusion.16
  351.5 1.5 bitcast_dynamic-update-slice_fusion.16
  352.9 1.5 bitcast_dynamic-update-slice_fusion.16
  354.4 1.5 bitcast_dynamic-update-slice_fusion.16
  355.9 1.5 bitcast_dynamic-update-slice_fusion.16
  357.4 1.5 bitcast_dynamic-update-slice_fusion.16
  358.9 1.5 bitcast_dynamic-update-slice_fusion.16
  360.4 1.5 bitcast_dynamic-update-slice_fusion.16
  361.8 1.5 bitcast_dynamic-update-slice_fusion.16
  365.5 26.7 %while.161 = (s32[]{:T(128)}, f32[2,8,512]{2,1,0:T(8,128)S(1)}, f32[32,2,8,512]{3,2,1,0:T(8,128)S(1)}, f32[32,2,8,512]{3,2,1,0:T(8,128)S(1)}, f32[32,2,8,512]{3,...) while((s32[]{:T(128)}, f32[2,8,512]{2,1,0:T(8,128)S(1)}, ...), condition=%wide.region_3.4_spmd.clone, body=%wide.region_2.3_spmd.clone.sunk | while | flops 40964 | bytes 262279 | solution.py:79
  395.5 30.7 %all-gather.2 = f32[32,8,1,512]{3,1,2,0:T(8,128)S(1)} all-gather(f32[2,8,1,512]{3,1,2,0:T(8,128)S(1)} %copy.91), channel_id=4, replica_groups=mesh['wall'=16,'stream'=32] {'wall'}, dimensions={0}, use_global_device_ids=true | all-gather | bytes 557056 | tf_op jit(solution)/shard_map/all_gather | solution.py:175
  426.1 18.6 %all-gather.3 = f32[32,8,1,512]{3,1,2,0:T(8,128)S(1)} all-gather(f32[2,8,1,512]{3,1,2,0:T(8,128)S(1)} %copy.92), channel_id=5, replica_groups=mesh['wall'=16,'stream'=32] {'wall'}, dimensions={0}, use_global_device_ids=true | all-gather | bytes 557056 | tf_op jit(solution)/shard_map/all_gather | solution.py:174
  445.5 1.8 while.166
  (401 shorter events, 58.9 us)
Async XLA Ops:
  6.5 1.1 copy-start.1
  6.5 1.2 copy-start
  6.5 167.6 %all-gather.7.cloned.1.call-start = ((), (), s32[]{:S(2)}) async-start(), calls=%async_computation | async-start | bytes 1081344 | tf_op jit(solution)/shard_map/all_gather | solution.py:149
  8.0 32.7 %collective-permute-start.2 = (f32[4,8,1,512]{3,2,1,0:T(1,128)S(1)}, f32[4,8,1,512]{3,2,1,0:T(1,128)S(1)}, u32[]{:S(2)}, u32[]{:S(2)}) collective-permute-start(f32[4,8,1,512]{3,2,1,0:T(1,128)S(1)} %get-tuple-element.1533), channel_id=1, source_target_pairs={{0,32},{32,64},{64,96},{96,128},{128,160},{160,192},{192,224},{224... | collective-permute-start | bytes 196616 | tf_op jit(solution)/shard_map/ppermute | solution.py:17
  12.6 28.2 %collective-permute-start.3 = (f32[4,8,1,512]{3,2,1,0:T(1,128)S(1)}, f32[4,8,1,512]{3,2,1,0:T(1,128)S(1)}, u32[]{:S(2)}, u32[]{:S(2)}) collective-permute-start(f32[4,8,1,512]{3,2,1,0:T(1,128)S(1)} %get-tuple-element.1534), channel_id=1, source_target_pairs={{32,0},{64,32},{96,64},{128,96},{160,128},{192,160},{224,192},{256... | collective-permute-start | bytes 196616 | tf_op jit(solution)/shard_map/ppermute | solution.py:18
  18.2 22.8 %collective-permute-start = (f32[4,1,8,512]{3,2,1,0:T(8,128)S(1)}, f32[4,1,8,512]{3,2,1,0:T(8,128)S(1)}, u32[]{:S(2)}, u32[]{:S(2)}) collective-permute-start(f32[4,1,8,512]{3,2,1,0:T(8,128)S(1)} %get-tuple-element.1531), channel_id=1, source_target_pairs={{0,1},{1,2},{2,3},{3,4},{4,5},{5,6},{6,7},{7,8},{8,9},{9,10},{10,1... | collective-permute-start | bytes 196616 | tf_op jit(solution)/shard_map/ppermute | solution.py:17
  20.1 20.8 %collective-permute-start.1 = (f32[4,1,8,512]{3,2,1,0:T(8,128)S(1)}, f32[4,1,8,512]{3,2,1,0:T(8,128)S(1)}, u32[]{:S(2)}, u32[]{:S(2)}) collective-permute-start(f32[4,1,8,512]{3,2,1,0:T(8,128)S(1)} %get-tuple-element.1532), channel_id=1, source_target_pairs={{1,0},{2,1},{3,2},{4,3},{5,4},{6,5},{7,6},{8,7},{9,8},{10,9},{11,1... | collective-permute-start | bytes 196616 | tf_op jit(solution)/shard_map/ppermute | solution.py:18
  29.8 0.7 copy-start.34
  29.8 0.7 copy-start.35
  30.6 0.7 copy-start.13
  30.6 0.7 copy-start.33
  31.4 0.7 copy-start.18
  32.0 0.7 copy-start.25
  35.7 15.0 %copy-start.6 = (f32[32,2,1,1]{1,3,2,0:T(1,128)}, f32[32,2,1,1]{1,3,2,0:T(1,128)S(1)}, u32[]{:S(2)}) copy-start(f32[32,2,1,1]{1,3,2,0:T(1,128)S(1)} %get-tuple-element.879) | copy-start | bytes 772
  37.1 0.7 copy-start.12
  37.1 0.7 copy-start.32
  37.8 0.7 copy-start.17
  39.9 0.7 copy-start.16
  42.8 271.7 %all-gather.9.cloned.1.call-start = ((), (), s32[]{:S(2)}) async-start(), calls=%async_computation.1 | async-start | bytes 1081344 | tf_op jit(solution)/shard_map/all_gather | solution.py:148
  44.1 6.6 %copy-start.8 = (f32[32,2,1,1]{1,3,2,0:T(1,128)}, f32[32,2,1,1]{1,3,2,0:T(1,128)S(1)}, u32[]{:S(2)}) copy-start(f32[32,2,1,1]{1,3,2,0:T(1,128)S(1)} %get-tuple-element.885) | copy-start | bytes 772
  46.3 0.7 copy-start.24
  50.7 0.7 copy-start.31
  51.4 0.7 copy-start.30
  363.3 1.0 copy-start.2
  363.3 1.3 copy-start.3
  364.7 0.8 copy-start.5
  365.5 26.8 %copy-start.28 = (f32[2]{0:T(128)S(1)}, f32[2]{0:T(128)}, u32[]{:S(2)}) copy-start(f32[2]{0:T(128)} %negate_bitcast_fusion.1) | copy-start | bytes 28
  365.5 26.8 %copy-start.29 = (f32[2]{0:T(128)S(1)}, f32[2]{0:T(128)}, u32[]{:S(2)}) copy-start(f32[2]{0:T(128)} %subtract_bitcast_fusion) | copy-start | bytes 28
  392.2 0.7 copy-start.23
  392.2 0.7 copy-start.26
  392.2 0.7 copy-start.27
  392.9 0.7 copy-start.7
  392.9 0.7 copy-start.9
  392.9 0.7 copy-start.10
  392.9 0.8 copy-start.11
  394.1 0.6 copy-start.22
  394.1 0.7 copy-start.21
  444.9 0.6 copy-start.14
  444.9 0.7 copy-start.15
  447.4 0.8 copy-start.4
  449.0 0.6 copy-start.20
  449.0 0.7 copy-start.19
Sparse Core Ops, SparseCore 0:
  42.9 131.2 all-gather.6
  177.2 137.1 all-gather.8
where the time goes:
time: 462 us; the launch traced here: 457 us
  waiting for transfers between devices  262 us (57%)
  other arithmetic  86.6 us (19%)
  blocking collectives  49.2 us (11%)
  starting transfers between devices  21.7 us (5%)
  local copies, waits for them, and re-layouts  19 us (4%)
  between operations  14.3 us (3%)
    all_gather x1, waiting for transfers between devices, per_device(): lax.all_gather(blocked[:, 0][None], 'stream', axis=0, tiled=True)  140 us
    all_gather x1, waiting for transfers between devices, per_device(): lax.all_gather(blocked[:, width - 1][None], 'stream', axis=0, tiled=True)  121 us
    dynamic_update_slice x224, other arithmetic, sweep(): lax.scan(forward, (level_start, weight_start), (leading, trailing))  77.9 us
    all_gather x1, blocking collectives, per_device(): lax.all_gather(lower_end[None], 'wall', axis=0, tiled=True)  30.7 us
    all_gather x1, blocking collectives, per_device(): lax.all_gather(upper_end[None], 'wall', axis=0, tiled=True)  18.6 us
    ppermute x2, starting transfers between devices, padded(): after = lax.ppermute(leading, axis, down)  15.2 us
    unnamed x80, local copies, waits for them, and re-layouts  12.5 us
  transfers between devices with their start and end apart: 6, of which 2 were waited for; matrix products, arithmetic and copies ran while one was open for 3% of the time, Pallas kernels for 0%

commit v1 on v0

v1 whole, which is shorter than its diff:
```python
import functools

import jax
import jax.numpy as jnp
import numpy as np
from jax import lax
from jax.experimental import pallas as pl
from jax.experimental.pallas import tpu as pltpu
from jax.sharding import PartitionSpec as P

ADVECT_STEP = 0.2
DRIFT_RATES = (1.0, -0.5)
FLUX_SCALE = 0.25 * ADVECT_STEP
HIGHEST = lax.Precision.HIGHEST


def line_factors(rate):
    base = 1.0 + 2.0 * rate
    root = np.sqrt(1.0 + 4.0 * rate)
    return 2.0 * rate / (base + root), 1.0 / root


def cyclic_links(rate, width, blocks):
    decay, _ = line_factors(rate)
    step = decay**width
    table = np.zeros((blocks, 2, blocks, 2))
    for block in range(blocks):
        for other in range(blocks):
            table[block, 0, other, 0] = step ** ((block - 1 - other) % blocks)
            table[block, 1, other, 1] = step ** ((other - block - 1) % blocks)
    return table.reshape(2 * blocks, 2 * blocks) / (1.0 - step**blocks)


def bounded_links(rate, width, blocks):
    decay, _ = line_factors(rate)
    step = decay**width
    length = width * blocks
    table = np.zeros((blocks, 2, blocks, 2))
    below_wall = np.zeros((blocks, 2))
    above_wall = np.zeros((blocks, 2))
    for block in range(blocks):
        below_wall[block, 1] = decay ** (width * block + 1)
        above_wall[block, 0] = decay ** (length - width * block - width + 1)
    mirror = decay ** (length + 1)
    below_weight = -(below_wall - mirror * above_wall) / (1.0 - mirror**2)
    above_weight = -(above_wall - mirror * below_wall) / (1.0 - mirror**2)
    for block in range(blocks):
        for other in range(blocks):
            if other < block:
                table[block, 0, other, 0] = step ** (block - 1 - other)
            if other > block:
                table[block, 1, other, 1] = step ** (other - block - 1)
        table[block, 0] += decay ** (width * block) * below_weight
        table[block, 1] += decay ** (length - width * (block + 1)) * above_weight
    return table.reshape(2 * blocks, 2 * blocks)


def whole(memory=pltpu.VMEM):
    return pl.BlockSpec(memory_space=memory)


def call(kernel, outs, ins, scratch=()):
    return pl.pallas_call(
        kernel,
        out_shape=[jax.ShapeDtypeStruct(shape, jnp.float32) for shape in outs],
        in_specs=[whole()] * len(ins),
        out_specs=[whole()] * len(outs),
        scratch_shapes=list(scratch),
        compiler_params=pltpu.CompilerParams(vmem_limit_bytes=32 * 1024 * 1024),
    )(*ins)


def edge_kernel(conc, vel, volt, low_out, high_out, right_out):
    width = conc.shape[1]
    depth = conc.shape[2]
    for item in range(4):
        if item < 2:
            right_out[item] = conc[item, width - 1]
        elif item == 2:
            right_out[item] = vel[0, width - 1]
        else:
            right_out[item] = volt[width - 1]
        for x in range(width):
            if item < 2:
                layer = conc.at[item, x]
            elif item == 2:
                layer = vel.at[1, x]
            else:
                layer = volt.at[x]
            low_out[item, x : x + 1] = layer[0:1]
            high_out[item, x : x + 1] = layer[depth - 1 : depth]


def face(conc_low, conc_high, speed_low, speed_high, volt_low, volt_high, species):
    drift = speed_low + speed_high - (2.0 * DRIFT_RATES[species]) * (volt_high - volt_low)
    return (conc_low + conc_high) * drift


def predict_kernel(
    decays, conc, vel, volt, low_edge, high_edge, left_halo, below_halo, above_halo, pred, spill, ends
):
    width, depth, span = volt.shape
    row = lax.broadcasted_iota(jnp.int32, (depth, span), 0)
    bottom = [
        face(below_halo[s], low_edge[s], below_halo[2], low_edge[2], below_halo[3], low_edge[3], s)
        for s in range(2)
    ]
    top = [
        face(high_edge[s], above_halo[s], high_edge[2], above_halo[2], high_edge[3], above_halo[3], s)
        for s in range(2)
    ]
    half = span // 2
    left = [face(left_halo[s], conc[s, 0], left_halo[2], vel[0, 0], left_halo[3], volt[0], s) for s in range(2)]
    running = []
    for s in range(2):
        moved = -FLUX_SCALE * left[s]
        spill[s] = moved
        running.append(moved)
    for x in range(width):
        here = volt[x]
        volt_up = pltpu.roll(here, depth - 1, 0)
        volt_next = pltpu.roll(here, span - 1, 1)
        speed_up = pltpu.roll(vel[1, x], depth - 1, 0)
        speed_next = pltpu.roll(vel[2, x], span - 1, 1)
        for s in range(2):
            value = conc[s, x]
            wall = face(value, pltpu.roll(value, depth - 1, 0), vel[1, x], speed_up, here, volt_up, s)
            wall_low = jnp.where(row == 0, bottom[s][x : x + 1], pltpu.roll(wall, 1, 0))
            wall_high = jnp.where(row == depth - 1, top[s][x : x + 1], wall)
            side = face(value, pltpu.roll(value, span - 1, 1), vel[2, x], speed_next, here, volt_next, s)
            total = (wall_high - wall_low) + (side - pltpu.roll(side, 1, 1)) - left[s]
            if x + 1 < width:
                right = face(value, conc[s, x + 1], vel[0, x], vel[0, x + 1], here, volt[x + 1], s)
                total = total + right
                left[s] = right
            result = value - FLUX_SCALE * total
            pred[s, x] = result
            running[s] = result + decays[s] * running[s]
    for s in range(2):
        behind = pred[s, width - 1]
        for x in range(width - 2, -1, -1):
            behind = pred[s, x] + decays[s] * behind
        behind = behind + (1.0 / decays[s]) * spill[s]
        for z in range(depth):
            for part in range(2):
                peer = (s * depth + z) * 2 + part
                cut = slice(part * half, (part + 1) * half)
                ends[peer, 0:1] = running[s][z : z + 1, cut]
                ends[peer, 1:2] = behind[z : z + 1, cut]


def link_kernel(axis, share, ends, table, links, flat):
    blocks = ends.shape[0]
    for block in range(blocks):
        flat[2 * block : 2 * block + 2] = ends[block]
    species = lax.div(lax.axis_index(axis), share)
    solved = jnp.dot(table[species], flat[...], precision=HIGHEST, preferred_element_type=jnp.float32)
    for block in range(blocks):
        links[block] = solved[2 * block : 2 * block + 2]


def stream_kernel(decays, gains, wall_decays, wall_gains, pred, spill, links, base, ends, carry):
    _, width, depth, span = pred.shape
    half = span // 2
    for s in range(2):
        for z in range(depth):
            for part in range(2):
                peer = (s * depth + z) * 2 + part
                cut = slice(part * half, (part + 1) * half)
                carry[0, s, z : z + 1, cut] = links[peer, 0:1]
                carry[1, s, z : z + 1, cut] = links[peer, 1:2]
    row = lax.broadcasted_iota(jnp.int32, (depth, span), 0)
    for s in range(2):
        behind = carry[1, s]
        for x in range(width - 1, -1, -1):
            base[s, x] = decays[s] * behind
            behind = pred[s, x] + decays[s] * behind
        running = carry[0, s] + spill[s]
        for x in range(width):
            running = pred[s, x] + decays[s] * running
            value = (gains[s] * wall_gains[s]) * (running + base[s, x])
            forward = value
            back = value
            step = 1
            while step < depth:
                scale = wall_decays[s] ** step
                forward = forward + jnp.where(row >= step, scale * pltpu.roll(forward, step, 0), 0.0)
                back = back + jnp.where(row < depth - step, scale * pltpu.roll(back, depth - step, 0), 0.0)
                step *= 2
            base[s, x] = forward + back - value
            ends[s * width + x, 0:1] = forward[depth - 1 : depth]
            ends[s * width + x, 1:2] = back[0:1]


def wall_kernel(wall_decays, base, links, out):
    _, width, depth, span = base.shape
    row = lax.broadcasted_iota(jnp.int32, (depth, span), 0)
    for s in range(2):
        from_below = jnp.zeros((depth, span), jnp.float32)
        from_above = jnp.zeros((depth, span), jnp.float32)
        for z in range(depth):
            from_below = jnp.where(row == z, wall_decays[s] ** (z + 1), from_below)
            from_above = jnp.where(row == z, wall_decays[s] ** (depth - z), from_above)
        for x in range(width):
            peer = s * width + x
            out[s, x] = base[s, x] + from_below * links[peer, 0:1] + from_above * links[peer, 1:2]


def exchange(values, axis):
    return lax.all_to_all(values, axis, split_axis=0, concat_axis=0, tiled=True)


def per_device(concentration, velocity, potential):
    _, width, depth, span = concentration.shape
    stream = lax.axis_size("stream")
    wall = lax.axis_size("wall")
    stream_total = width * stream
    wall_total = depth * wall
    rates_x = (4.0 * width * width, float(stream_total * stream_total // 25))
    rates_z = (4.0 * depth * depth, float(wall_total * wall_total // 16))
    decays_x, gains_x = zip(*[tuple(float(v) for v in line_factors(rate)) for rate in rates_x])
    decays_z, gains_z = zip(*[tuple(float(v) for v in line_factors(rate)) for rate in rates_z])
    links_x = jnp.array(np.stack([cyclic_links(rate, width, stream) for rate in rates_x]), jnp.float32)
    links_z = jnp.array(np.stack([bounded_links(rate, depth, wall) for rate in rates_z]), jnp.float32)

    edges = (4, width, span)
    low_edge, high_edge, right_edge = call(
        edge_kernel, [edges, edges, (4, depth, span)], (concentration, velocity, potential)
    )
    ring = [(i, (i + 1) % stream) for i in range(stream)]
    rising = [(i, i + 1) for i in range(wall - 1)]
    falling = [(i + 1, i) for i in range(wall - 1)]
    left_halo = lax.ppermute(right_edge, "stream", ring)
    below_halo = lax.ppermute(high_edge, "wall", rising)
    above_halo = lax.ppermute(low_edge, "wall", falling)
    half = span // 2
    pred, spill, ends = call(
        functools.partial(predict_kernel, decays_x),
        [concentration.shape, (2, depth, span), (stream, 2, half)],
        (concentration, velocity, potential, low_edge, high_edge, left_halo, below_halo, above_halo),
    )
    ends = exchange(ends, "stream")
    (links,) = call(
        functools.partial(link_kernel, "stream", 2 * depth),
        [ends.shape],
        (ends, links_x),
        [pltpu.VMEM((2 * stream, half), jnp.float32)],
    )
    links = exchange(links, "stream")
    base, ends = call(
        functools.partial(stream_kernel, decays_x, gains_x, decays_z, gains_z),
        [concentration.shape, (wall, 2, span)],
        (pred, spill, links),
        [pltpu.VMEM((2, 2, depth, span), jnp.float32)],
    )
    ends = exchange(ends, "wall")
    (links,) = call(
        functools.partial(link_kernel, "wall", width),
        [ends.shape],
        (ends, links_z),
        [pltpu.VMEM((2 * wall, span), jnp.float32)],
    )
    links = exchange(links, "wall")
    (out,) = call(functools.partial(wall_kernel, decays_z), [concentration.shape], (base, links))
    return out


def solution(mesh):
    return jax.shard_map(
        per_device,
        mesh=mesh,
        in_specs=(
            P(None, "stream", "wall", None),
            P(None, "stream", "wall", None),
            P("stream", "wall", None),
        ),
        out_specs=P(None, "stream", "wall", None),
        check_vma=False,
    )
```

time: 462 us -> 89.6 us (0.19)
  waiting for transfers between devices: 262 us -> 3.41 us
  other arithmetic: 86.6 us -> 0 us
  blocking collectives: 49.2 us -> 68.1 us
  local copies, waits for them, and re-layouts: 19 us -> 2.86 us
  between operations: 14.3 us -> 0.08 us
  starting transfers between devices: 21.7 us -> 12.6 us
    all_gather x2 -> x0, waiting for transfers between devices: 262 us -> none  [the longest x1 140 us: per_device(): lax.all_gather(blocked[:, 0][None], 'stream', axis=0, tiled=True)]
    dynamic_update_slice x224 -> x0, other arithmetic: 77.9 us -> none  [sweep(): lax.scan(forward, (level_start, weight_start), (leading, trailing))]
    all_to_all x0 -> x4, blocking collectives: none -> 68.1 us  [exchange(): return lax.all_to_all(values, axis, split_axis=0, concat_axis=0, tiled=True)]
    all_gather x2 -> x0, blocking collectives: 49.2 us -> none  [the longest x1 30.7 us: per_device(): lax.all_gather(lower_end[None], 'wall', axis=0, tiled=True)]
    unnamed x80 -> x10, local copies, waits for them, and re-layouts: 12.5 us -> 2.86 us
    ppermute x4 -> x3, starting transfers between devices: 21.6 us -> 12.6 us  [the longest x1 5.48 us: per_device(): left_halo = lax.ppermute(right_edge, 'stream', ring)]
  transfers between devices with their start and end apart: 6 -> 3, of which waited for: 2 -> 1; matrix products, arithmetic and copies ran while one was open for 3% -> 0% of each run, Pallas kernels for 0% -> 0%
where the time goes in v1:
time: 89.6 us; the launch traced here: 89.2 us
  blocking collectives  68.1 us (76%)
  starting transfers between devices  12.6 us (14%)
  waiting for transfers between devices  3.41 us (4%)
  local copies, waits for them, and re-layouts  2.86 us (3%)
  Pallas kernels  2.13 us (2%)
    all_to_all x4, blocking collectives, exchange(): return lax.all_to_all(values, axis, split_axis=0, concat_axis=0, tiled=True)  68.1 us
    ppermute x1, starting transfers between devices, per_device(): left_halo = lax.ppermute(right_edge, 'stream', ring)  5.48 us
    ppermute x1, starting transfers between devices, per_device(): above_halo = lax.ppermute(low_edge, 'wall', falling)  5.23 us
    ppermute x1, waiting for transfers between devices, per_device(): left_halo = lax.ppermute(right_edge, 'stream', ring)  3.41 us
    unnamed x10, local copies, waits for them, and re-layouts  2.86 us
    pallas_call x6, Pallas kernels, call(): pl.pallas_call(kernel, out_shape=[jax.ShapeDtypeStruct(shape, jnp.float32...  2.13 us
    ppermute x1, starting transfers between devices, per_device(): below_halo = lax.ppermute(high_edge, 'wall', rising)  1.92 us
  transfers between devices with their start and end apart: 3, of which 1 were waited for; matrix products, arithmetic and copies ran while one was open for 0% of the time, Pallas kernels for 0%

profile of v1, /device:TPU:1, one launch (start us, length us, event | category | flops | bytes accessed | tf_op | source)
XLA Modules:
  0.0 89.2 jit_solution(16070090504854500721)
XLA Ops:
  0.0 0.0 copy-start
  0.0 1.0 %copy-done = f32[3,8,8,512]{3,2,1,0:T(8,128)S(1)} copy-done((f32[3,8,8,512]{3,2,1,0:T(8,128)S(1)}, f32[3,8,8,512]{3,2,1,0:T(8,128)}, u32[]{:S(2)}) %copy-start) | copy-done | bytes 393240
  1.0 0.0 copy-start.1
  1.0 0.9 %copy-done.1 = f32[2,8,8,512]{3,2,1,0:T(8,128)S(1)} copy-done((f32[2,8,8,512]{3,2,1,0:T(8,128)S(1)}, f32[2,8,8,512]{3,2,1,0:T(8,128)}, u32[]{:S(2)}) %copy-start.1) | copy-done | bytes 262168
  1.9 0.0 copy-start.2
  1.9 0.9 %copy-done.2 = f32[8,8,512]{2,1,0:T(8,128)S(1)} copy-done((f32[8,8,512]{2,1,0:T(8,128)S(1)}, f32[8,8,512]{2,1,0:T(8,128)}, u32[]{:S(2)}) %copy-start.2) | copy-done | bytes 131096
  2.9 5.5 %collective-permute-start = (f32[4,8,512]{2,1,0:T(8,128)S(1)}, f32[4,8,512]{2,1,0:T(8,128)S(1)}, u32[]{:S(2)}, u32[]{:S(2)}) collective-permute-start(f32[4,8,512]{2,1,0:T(8,128)S(1)} %get-tuple-element.15), channel_id=1, source_target_pairs={{0,1},{1,2},{2,3},{3,4},{4,5},{5,6},{6,7},{7,8},{8,9},{9,10},{10,1... | collective-permute-start | bytes 196616 | tf_op jit(solution)/shard_map/ppermute | solution.py:233
  8.4 5.2 %collective-permute-start.2 = (f32[4,8,512]{2,1,0:T(8,128)S(1)}, f32[4,8,512]{2,1,0:T(8,128)S(1)}, u32[]{:S(2)}, u32[]{:S(2)}) collective-permute-start(f32[4,8,512]{2,1,0:T(8,128)S(1)} %get-tuple-element.13.low_edge), channel_id=1, source_target_pairs={{32,0},{64,32},{96,64},{128,96},{160,128},{192,160},{224,192},{256... | collective-permute-start | bytes 196616 | tf_op jit(solution)/shard_map/ppermute | solution.py:235
  13.6 1.9 %collective-permute-start.1 = (f32[4,8,512]{2,1,0:T(8,128)S(1)}, f32[4,8,512]{2,1,0:T(8,128)S(1)}, u32[]{:S(2)}, u32[]{:S(2)}) collective-permute-start(f32[4,8,512]{2,1,0:T(8,128)S(1)} %get-tuple-element.14.high_edge), channel_id=1, source_target_pairs={{0,32},{32,64},{64,96},{96,128},{128,160},{160,192},{192,224},{224... | collective-permute-start | bytes 196616 | tf_op jit(solution)/shard_map/ppermute | solution.py:234
  15.5 3.4 %collective-permute-done.left_halo = f32[4,8,512]{2,1,0:T(8,128)S(1)} collective-permute-done((f32[4,8,512]{2,1,0:T(8,128)S(1)}, f32[4,8,512]{2,1,0:T(8,128)S(1)}, u32[]{:S(2)}, u32[]{:S(2)}) %collective-permute-start) | collective-permute-done | bytes 65568 | tf_op jit(solution)/shard_map/ppermute | solution.py:233
  19.0 0.0 collective-permute-done.2.above_halo
  19.0 0.0 collective-permute-done.1.below_halo
  19.0 0.6 shard_map.56
  19.5 0.0 copy-start.3
  19.5 27.4 %all_to_all.20.ends = f32[32,2,256]{2,1,0:T(2,128)S(1)} all-to-all(f32[32,2,256]{2,1,0:T(2,128)S(1)} %get-tuple-element.18), channel_id=1, replica_groups=mesh['wall'=16,'stream'=32] {'stream'}, dimensions={0} | all-to-all | bytes 131072 | tf_op jit(solution)/shard_map/all_to_all | solution.py:210
  46.9 0.0 copy-done.3
  46.9 0.2 shard_map.57
  47.2 17.2 %all_to_all.21.links = f32[32,2,256]{2,1,0:T(2,128)S(1)} all-to-all(f32[32,2,256]{2,1,0:T(2,128)S(1)} %shard_map.57), channel_id=1, replica_groups=mesh['wall'=16,'stream'=32] {'stream'}, dimensions={0} | all-to-all | bytes 131072 | tf_op jit(solution)/shard_map/all_to_all | solution.py:210
  64.3 0.4 shard_map.58
  64.7 0.0 copy-start.4
  64.7 14.8 %all_to_all.22.ends = f32[16,2,512]{2,1,0:T(2,128)S(1)} all-to-all(f32[16,2,512]{2,1,0:T(2,128)S(1)} %get-tuple-element.20), channel_id=1, replica_groups=mesh['wall'=16,'stream'=32] {'wall'}, dimensions={0} | all-to-all | bytes 131072 | tf_op jit(solution)/shard_map/all_to_all | solution.py:210
  79.5 0.0 copy-done.4
  79.5 0.2 shard_map.59
  79.7 8.7 %all_to_all.23.links = f32[16,2,512]{2,1,0:T(2,128)S(1)} all-to-all(f32[16,2,512]{2,1,0:T(2,128)S(1)} %shard_map.59), channel_id=1, replica_groups=mesh['wall'=16,'stream'=32] {'wall'}, dimensions={0} | all-to-all | bytes 131072 | tf_op jit(solution)/shard_map/all_to_all | solution.py:210
  88.4 0.7 shard_map.60
  (1 shorter events, 0.0 us)
Async XLA Ops:
  0.0 1.0 %copy-start = (f32[3,8,8,512]{3,2,1,0:T(8,128)S(1)}, f32[3,8,8,512]{3,2,1,0:T(8,128)}, u32[]{:S(2)}) copy-start(f32[3,8,8,512]{3,2,1,0:T(8,128)} %vel.3) | copy-start | bytes 1179652
  1.0 0.9 %copy-start.1 = (f32[2,8,8,512]{3,2,1,0:T(8,128)S(1)}, f32[2,8,8,512]{3,2,1,0:T(8,128)}, u32[]{:S(2)}) copy-start(f32[2,8,8,512]{3,2,1,0:T(8,128)} %conc.3) | copy-start | bytes 786436
  1.9 0.9 %copy-start.2 = (f32[8,8,512]{2,1,0:T(8,128)S(1)}, f32[8,8,512]{2,1,0:T(8,128)}, u32[]{:S(2)}) copy-start(f32[8,8,512]{2,1,0:T(8,128)} %volt.3) | copy-start | bytes 393220
  2.9 16.1 %collective-permute-start = (f32[4,8,512]{2,1,0:T(8,128)S(1)}, f32[4,8,512]{2,1,0:T(8,128)S(1)}, u32[]{:S(2)}, u32[]{:S(2)}) collective-permute-start(f32[4,8,512]{2,1,0:T(8,128)S(1)} %get-tuple-element.15), channel_id=1, source_target_pairs={{0,1},{1,2},{2,3},{3,4},{4,5},{5,6},{6,7},{7,8},{8,9},{9,10},{10,1... | collective-permute-start | bytes 196616 | tf_op jit(solution)/shard_map/ppermute | solution.py:233
  8.4 10.6 %collective-permute-start.2 = (f32[4,8,512]{2,1,0:T(8,128)S(1)}, f32[4,8,512]{2,1,0:T(8,128)S(1)}, u32[]{:S(2)}, u32[]{:S(2)}) collective-permute-start(f32[4,8,512]{2,1,0:T(8,128)S(1)} %get-tuple-element.13.low_edge), channel_id=1, source_target_pairs={{32,0},{64,32},{96,64},{128,96},{160,128},{192,160},{224,192},{256... | collective-permute-start | bytes 196616 | tf_op jit(solution)/shard_map/ppermute | solution.py:235
  13.6 5.3 %collective-permute-start.1 = (f32[4,8,512]{2,1,0:T(8,128)S(1)}, f32[4,8,512]{2,1,0:T(8,128)S(1)}, u32[]{:S(2)}, u32[]{:S(2)}) collective-permute-start(f32[4,8,512]{2,1,0:T(8,128)S(1)} %get-tuple-element.14.high_edge), channel_id=1, source_target_pairs={{0,32},{32,64},{64,96},{96,128},{128,160},{160,192},{192,224},{224... | collective-permute-start | bytes 196616 | tf_op jit(solution)/shard_map/ppermute | solution.py:234
  19.5 27.4 %copy-start.3 = (f32[2,64,64]{2,1,0:T(8,128)S(1)}, f32[2,64,64]{2,1,0:T(8,128)}, u32[]{:S(2)}) copy-start(f32[2,64,64]{2,1,0:T(8,128)} %constant.4.clone.table) | copy-start | bytes 98308
  64.7 14.8 %copy-start.4 = (f32[2,32,32]{2,1,0:T(8,128)S(1)}, f32[2,32,32]{2,1,0:T(8,128)}, u32[]{:S(2)}) copy-start(f32[2,32,32]{2,1,0:T(8,128)} %constant.5.clone.table) | copy-start | bytes 24580

commit v2 on v1

v2 whole, which is shorter than its diff:
```python
import functools

import jax
import jax.numpy as jnp
import numpy as np
from jax import lax
from jax.experimental import pallas as pl
from jax.experimental.pallas import tpu as pltpu
from jax.sharding import PartitionSpec as P

ADVECT_STEP = 0.2
DRIFT_RATES = (1.0, -0.5)
FLUX_SCALE = 0.25 * ADVECT_STEP
TEAM = 4
HALVES = 2


def line_factors(rate):
    base = 1.0 + 2.0 * rate
    root = np.sqrt(1.0 + 4.0 * rate)
    return float(2.0 * rate / (base + root)), float(1.0 / root)


def pick(index, values):
    chosen = jnp.float32(values[0])
    for place, value in enumerate(values):
        if place:
            chosen = jnp.where(index == place, jnp.float32(value), chosen)
    return chosen


def whole(memory=pltpu.VMEM):
    return pl.BlockSpec(memory_space=memory)


def call(kernel, outs, ins, scratch=(), source=pltpu.VMEM, room=32):
    return pl.pallas_call(
        kernel,
        out_shape=[jax.ShapeDtypeStruct(shape, jnp.float32) for shape in outs],
        in_specs=[whole(source)] * len(ins),
        out_specs=[whole()] * len(outs),
        scratch_shapes=list(scratch),
        compiler_params=pltpu.CompilerParams(vmem_limit_bytes=room * 1024 * 1024),
    )(*ins)


def edge_kernel(conc_in, vel_in, volt_in, low_out, high_out, right_out, conc, speed, volt, arrived):
    width, depth, _ = volt.shape
    copies = [
        pltpu.make_async_copy(source, target, arrived.at[place])
        for place, (source, target) in enumerate(
            (
                (conc_in, conc),
                (vel_in.at[1], speed),
                (volt_in, volt),
                (vel_in.at[0, width - 1], right_out.at[2]),
            )
        )
    ]
    for copy in copies:
        copy.start()
    for copy in copies:
        copy.wait()
    for item, layers in enumerate((conc.at[0], conc.at[1], speed, volt)):
        if item != 2:
            right_out[item] = layers[width - 1]
        for x in range(width):
            low_out[item, x : x + 1] = layers[x, 0:1]
            high_out[item, x : x + 1] = layers[x, depth - 1 : depth]


def face(conc_low, conc_high, speed_low, speed_high, volt_low, volt_high, species):
    drift = speed_low + speed_high - (2.0 * DRIFT_RATES[species]) * (volt_high - volt_low)
    return (conc_low + conc_high) * drift


def predict_kernel(
    decays, conc, vel, volt, low_edge, high_edge, left_halo, below_halo, above_halo, pred, spill, ends
):
    width, depth, span = volt.shape
    row = lax.broadcasted_iota(jnp.int32, (depth, span), 0)
    bottom = [
        face(below_halo[s], low_edge[s], below_halo[2], low_edge[2], below_halo[3], low_edge[3], s)
        for s in range(2)
    ]
    top = [
        face(high_edge[s], above_halo[s], high_edge[2], above_halo[2], high_edge[3], above_halo[3], s)
        for s in range(2)
    ]
    half = span // HALVES
    left = [face(left_halo[s], conc[s, 0], left_halo[2], vel[0, 0], left_halo[3], volt[0], s) for s in range(2)]
    running = []
    for s in range(2):
        moved = -FLUX_SCALE * left[s]
        spill[s] = moved
        running.append(moved)
    for x in range(width):
        here = volt[x]
        volt_up = pltpu.roll(here, depth - 1, 0)
        volt_next = pltpu.roll(here, span - 1, 1)
        speed_up = pltpu.roll(vel[1, x], depth - 1, 0)
        speed_next = pltpu.roll(vel[2, x], span - 1, 1)
        for s in range(2):
            value = conc[s, x]
            wall = face(value, pltpu.roll(value, depth - 1, 0), vel[1, x], speed_up, here, volt_up, s)
            wall_low = jnp.where(row == 0, bottom[s][x : x + 1], pltpu.roll(wall, 1, 0))
            wall_high = jnp.where(row == depth - 1, top[s][x : x + 1], wall)
            side = face(value, pltpu.roll(value, span - 1, 1), vel[2, x], speed_next, here, volt_next, s)
            total = (wall_high - wall_low) + (side - pltpu.roll(side, 1, 1)) - left[s]
            if x + 1 < width:
                right = face(value, conc[s, x + 1], vel[0, x], vel[0, x + 1], here, volt[x + 1], s)
                total = total + right
                left[s] = right
            result = value - FLUX_SCALE * total
            pred[s, x] = result
            running[s] = result + decays[s] * running[s]
    for s in range(2):
        behind = pred[s, width - 1]
        for x in range(width - 2, -1, -1):
            behind = pred[s, x] + decays[s] * behind
        behind = behind + (1.0 / decays[s]) * spill[s]
        for part in range(HALVES):
            cut = slice(part * half, (part + 1) * half)
            ends[s * HALVES + part, 0] = running[s][:, cut]
            ends[s * HALVES + part, 1] = behind[:, cut]


def decayed(parts, step):
    total = parts[0]
    for part in parts[1:]:
        total = step * total + part
    return total


def stream_sum_kernel(steps, ends, sums):
    step = pick(lax.div(lax.rem(lax.axis_index("stream"), TEAM), HALVES), steps)
    before = decayed([ends[m, 0] for m in range(TEAM)], step)
    after = decayed([ends[m, 1] for m in range(TEAM - 1, -1, -1)], step)
    for team in range(sums.shape[0]):
        sums[team, 0] = before
        sums[team, 1] = after


def stream_link_kernel(steps, ends, sums, links):
    position = lax.axis_index("stream")
    species = lax.div(lax.rem(position, TEAM), HALVES)
    team = lax.div(position, TEAM)
    teams = sums.shape[0]
    step = pick(species, steps)
    leap = pick(species, [value**TEAM for value in steps])
    closing = pick(species, [1.0 / (1.0 - value ** (TEAM * teams)) for value in steps])
    before = decayed([sums[lax.rem(team + k, teams), 0] for k in range(teams)], leap) * closing
    after = decayed([sums[lax.rem(team + teams - k, teams), 1] for k in range(teams)], leap) * closing
    for m in range(TEAM):
        links[m, 0] = before
        before = step * before + ends[m, 0]
    for m in range(TEAM - 1, -1, -1):
        links[m, 1] = after
        after = step * after + ends[m, 1]


def stream_kernel(decays, gains, wall_decays, wall_gains, pred, spill, links, base, ends):
    _, width, depth, span = pred.shape
    row = lax.broadcasted_iota(jnp.int32, (depth, span), 0)
    for s in range(2):
        entering = [
            jnp.concatenate([links[s * HALVES + part, side] for part in range(HALVES)], axis=1) for side in range(2)
        ]
        behind = entering[1]
        for x in range(width - 1, -1, -1):
            base[s, x] = decays[s] * behind
            behind = pred[s, x] + decays[s] * behind
        running = entering[0] + spill[s]
        for x in range(width):
            running = pred[s, x] + decays[s] * running
            value = (gains[s] * wall_gains[s]) * (running + base[s, x])
            forward = value
            back = value
            step = 1
            while step < depth:
                scale = wall_decays[s] ** step
                forward = forward + jnp.where(row >= step, scale * pltpu.roll(forward, step, 0), 0.0)
                back = back + jnp.where(row < depth - step, scale * pltpu.roll(back, depth - step, 0), 0.0)
                step *= 2
            base[s, x] = forward + back - value
            for m in range(TEAM):
                ends[m, 0, s, x : x + 1] = forward[depth - 1 : depth]
                ends[m, 1, s, x : x + 1] = back[0:1]


def wall_sum_kernel(steps, ends, sums):
    for s in range(2):
        before = decayed([ends[m, 0, s] for m in range(TEAM)], steps[s])
        after = decayed([ends[m, 1, s] for m in range(TEAM - 1, -1, -1)], steps[s])
        for team in range(sums.shape[0]):
            sums[team, 0, s] = before
            sums[team, 1, s] = after


def chosen_sum(parts, index, weights):
    total = None
    for place, part in enumerate(parts):
        term = pick(index, [row[place] for row in weights]) * part
        total = term if total is None else total + term
    return total


def wall_kernel(decays, base, ends, sums, out):
    _, width, depth, span = base.shape
    teams = sums.shape[0]
    position = lax.axis_index("wall")
    member = lax.rem(position, TEAM)
    team = lax.div(position, TEAM)
    row = lax.broadcasted_iota(jnp.int32, (depth, span), 0)
    for s in range(2):
        step = decays[s] ** depth
        leap = step**TEAM
        mirror = decays[s] ** (depth * TEAM * teams + 1)
        scale = -1.0 / (1.0 - mirror * mirror)
        below = [sums[t, 0, s] for t in range(teams)]
        above = [sums[t, 1, s] for t in range(teams)]
        top = decays[s] * decayed(below, leap)
        bottom = decays[s] * decayed(above[::-1], leap)
        from_bottom = scale * (bottom - mirror * top)
        from_top = scale * (top - mirror * bottom)
        before = chosen_sum(
            below + [from_bottom],
            team,
            [[leap ** (t - 1 - k) if k < t else 0.0 for k in range(teams)] + [leap**t] for t in range(teams)],
        )
        after = chosen_sum(
            above + [from_top],
            team,
            [[leap ** (k - t - 1) if k > t else 0.0 for k in range(teams)] + [leap ** (teams - 1 - t)] for t in range(teams)],
        )
        before = chosen_sum(
            [ends[m, 0, s] for m in range(TEAM)] + [before],
            member,
            [[step ** (m - 1 - k) if k < m else 0.0 for k in range(TEAM)] + [step**m] for m in range(TEAM)],
        )
        after = chosen_sum(
            [ends[m, 1, s] for m in range(TEAM)] + [after],
            member,
            [[step ** (k - m - 1) if k > m else 0.0 for k in range(TEAM)] + [step ** (TEAM - 1 - m)] for m in range(TEAM)],
        )
        rise = jnp.zeros((depth, span), jnp.float32)
        fall = jnp.zeros((depth, span), jnp.float32)
        for z in range(depth):
            rise = jnp.where(row == z, decays[s] ** (z + 1), rise)
            fall = jnp.where(row == z, decays[s] ** (depth - z), fall)
        for x in range(width):
            out[s, x] = base[s, x] + rise * before[x : x + 1] + fall * after[x : x + 1]


def exchange(values, axis, size, stride):
    peers = values.shape[0]
    groups = [
        [start + offset + stride * k for k in range(peers)]
        for start in range(0, size, stride * peers)
        for offset in range(stride)
    ]
    return lax.all_to_all(values, axis, split_axis=0, concat_axis=0, tiled=True, axis_index_groups=groups)


def per_device(concentration, velocity, potential):
    _, width, depth, span = concentration.shape
    stream = lax.axis_size("stream")
    wall = lax.axis_size("wall")
    stream_total = width * stream
    wall_total = depth * wall
    rates_x = (4.0 * width * width, float(stream_total * stream_total // 25))
    rates_z = (4.0 * depth * depth, float(wall_total * wall_total // 16))
    decays_x, gains_x = zip(*[line_factors(rate) for rate in rates_x])
    decays_z, gains_z = zip(*[line_factors(rate) for rate in rates_z])
    steps_x = [decay**width for decay in decays_x]
    steps_z = [decay**depth for decay in decays_z]

    edges = (4, width, span)
    low_edge, high_edge, right_edge = call(
        edge_kernel,
        [edges, edges, (4, depth, span)],
        (concentration, velocity, potential),
        [
            pltpu.VMEM(concentration.shape, jnp.float32),
            pltpu.VMEM(potential.shape, jnp.float32),
            pltpu.VMEM(potential.shape, jnp.float32),
            pltpu.SemaphoreType.DMA((4,)),
        ],
        pltpu.HBM,
        62,
    )
    ring = [(i, (i + 1) % stream) for i in range(stream)]
    rising = [(i, i + 1) for i in range(wall - 1)]
    falling = [(i + 1, i) for i in range(wall - 1)]
    left_halo = lax.ppermute(right_edge, "stream", ring)
    below_halo = lax.ppermute(high_edge, "wall", rising)
    above_halo = lax.ppermute(low_edge, "wall", falling)
    share = (2, depth, span // HALVES)
    pred, spill, ends = call(
        functools.partial(predict_kernel, decays_x),
        [concentration.shape, (2, depth, span), (TEAM,) + share],
        (concentration, velocity, potential, low_edge, high_edge, left_halo, below_halo, above_halo),
    )
    ends = exchange(ends, "stream", stream, 1)
    (sums,) = call(functools.partial(stream_sum_kernel, steps_x), [(stream // TEAM,) + share], (ends,))
    sums = exchange(sums, "stream", stream, TEAM)
    (links,) = call(functools.partial(stream_link_kernel, steps_x), [(TEAM,) + share], (ends, sums))
    links = exchange(links, "stream", stream, 1)
    line_ends = (2, 2, width, span)
    base, ends = call(
        functools.partial(stream_kernel, decays_x, gains_x, decays_z, gains_z),
        [concentration.shape, (TEAM,) + line_ends],
        (pred, spill, links),
    )
    ends = exchange(ends, "wall", wall, 1)
    (sums,) = call(functools.partial(wall_sum_kernel, steps_z), [(wall // TEAM,) + line_ends], (ends,))
    sums = exchange(sums, "wall", wall, TEAM)
    (out,) = call(functools.partial(wall_kernel, decays_z), [concentration.shape], (base, ends, sums))
    return out


def solution(mesh):
    return jax.shard_map(
        per_device,
        mesh=mesh,
        in_specs=(
            P(None, "stream", "wall", None),
            P(None, "stream", "wall", None),
            P("stream", "wall", None),
        ),
        out_specs=P(None, "stream", "wall", None),
        check_vma=False,
    )
```

time: 89.6 us -> 86.2 us (0.962)
  blocking collectives: 68.1 us -> 64.1 us
  Pallas kernels: 2.13 us -> 3.64 us
  local copies, waits for them, and re-layouts: 2.86 us -> 1.68 us
    all_to_all x4 -> x5, blocking collectives: 68.1 us -> 64.1 us  [exchange(): lax.all_to_all(values, axis, split_axis=0, concat_axis=0, tiled=True, axi...]
    pallas_call x6 -> x7, Pallas kernels: 2.13 us -> 3.64 us  [call(): pl.pallas_call(kernel, out_shape=[jax.ShapeDtypeStruct(shape, jnp.float32...]
    unnamed x10, local copies, waits for them, and re-layouts: 2.86 us -> 1.68 us
where the time goes in v2:
time: 86.2 us; the launch traced here: 85.7 us
  blocking collectives  64.1 us (74%)
  starting transfers between devices  12.6 us (15%)
  Pallas kernels  3.64 us (4%)
  waiting for transfers between devices  3.63 us (4%)
  local copies, waits for them, and re-layouts  1.68 us (2%)
    all_to_all x5, blocking collectives, exchange(): lax.all_to_all(values, axis, split_axis=0, concat_axis=0, tiled=True, axi...  64.1 us
    ppermute x1, starting transfers between devices, per_device(): left_halo = lax.ppermute(right_edge, 'stream', ring)  5.48 us
    ppermute x1, starting transfers between devices, per_device(): above_halo = lax.ppermute(low_edge, 'wall', falling)  5.22 us
    pallas_call x7, Pallas kernels, call(): pl.pallas_call(kernel, out_shape=[jax.ShapeDtypeStruct(shape, jnp.float32...  3.64 us
    ppermute x1, waiting for transfers between devices, per_device(): left_halo = lax.ppermute(right_edge, 'stream', ring)  3.62 us
    ppermute x1, starting transfers between devices, per_device(): below_halo = lax.ppermute(high_edge, 'wall', rising)  1.92 us
  transfers between devices with their start and end apart: 3, of which 1 were waited for; matrix products, arithmetic and copies ran while one was open for 0% of the time, Pallas kernels for 0%

profile of v2, /device:TPU:1, one launch (start us, length us, event | category | flops | bytes accessed | tf_op | source)
XLA Modules:
  0.0 85.7 jit_solution(2931192419888289913)
XLA Ops:
  0.0 0.0 copy-start.2
  0.0 0.0 copy-start
  0.0 0.0 copy-start.1
  0.0 1.9 %shard_map.37 = (f32[4,8,512]{2,1,0:T(8,128)}, f32[4,8,512]{2,1,0:T(8,128)}, f32[4,8,512]{2,1,0:T(8,128)}) custom-call(f32[2,8,8,512]{3,2,1,0:T(8,128)} %conc.1, f32[3,8,8,512]{3,2,1,0:T(8,128)} %vel.1, f32[8,8,512]{2,1,0:T(8,128)} %volt.1), custom_call_target="tpu_custom_call" | custom-call | tf_op jit(solution)/shard_map/pallas_call | solution.py:37
  1.9 5.5 %collective-permute-start = (f32[4,8,512]{2,1,0:T(8,128)}, f32[4,8,512]{2,1,0:T(8,128)S(1)}, u32[]{:S(2)}, u32[]{:S(2)}) collective-permute-start(f32[4,8,512]{2,1,0:T(8,128)} %get-tuple-element.15), channel_id=1, source_target_pairs={{0,1},{1,2},{2,3},{3,4},{4,5},{5,6},{6,7},{7,8},{8,9},{9,10},{10,1... | collective-permute-start | bytes 196616 | tf_op jit(solution)/shard_map/ppermute | solution.py:295
  7.4 5.2 %collective-permute-start.2 = (f32[4,8,512]{2,1,0:T(8,128)}, f32[4,8,512]{2,1,0:T(8,128)S(1)}, u32[]{:S(2)}, u32[]{:S(2)}) collective-permute-start(f32[4,8,512]{2,1,0:T(8,128)} %get-tuple-element.13.low_edge), channel_id=1, source_target_pairs={{32,0},{64,32},{96,64},{128,96},{160,128},{192,160},{224,192},{256... | collective-permute-start | bytes 196616 | tf_op jit(solution)/shard_map/ppermute | solution.py:297
  12.6 1.9 %collective-permute-start.1 = (f32[4,8,512]{2,1,0:T(8,128)}, f32[4,8,512]{2,1,0:T(8,128)S(1)}, u32[]{:S(2)}, u32[]{:S(2)}) collective-permute-start(f32[4,8,512]{2,1,0:T(8,128)} %get-tuple-element.14.high_edge), channel_id=1, source_target_pairs={{0,32},{32,64},{64,96},{96,128},{128,160},{160,192},{192,224},{224... | collective-permute-start | bytes 196616 | tf_op jit(solution)/shard_map/ppermute | solution.py:296
  14.5 3.6 %collective-permute-done.left_halo = f32[4,8,512]{2,1,0:T(8,128)S(1)} collective-permute-done((f32[4,8,512]{2,1,0:T(8,128)}, f32[4,8,512]{2,1,0:T(8,128)S(1)}, u32[]{:S(2)}, u32[]{:S(2)}) %collective-permute-start) | collective-permute-done | bytes 65568 | tf_op jit(solution)/shard_map/ppermute | solution.py:295
  18.1 0.0 collective-permute-done.2.above_halo
  18.1 0.0 collective-permute-done.1.below_halo
  18.1 0.0 copy-done.2
  18.2 0.0 copy-done
  18.2 0.0 copy-done.1
  18.2 0.0 copy-start.3
  18.2 0.8 copy-done.3
  19.0 0.0 copy-start.4
  19.0 0.8 copy-done.4
  19.9 0.5 shard_map.38
  20.4 7.6 %all_to_all.25.ends = f32[4,2,8,256]{3,2,1,0:T(8,128)S(1)} all-to-all(f32[4,2,8,256]{3,2,1,0:T(8,128)S(1)} %get-tuple-element.18), channel_id=1, replica_groups={{0,1,2,3},{4,5,6,7},{8,9,10,11},{12,13,14,15},{16,17,18,19},{20,21,22,2..., dimensions={0} | all-to-all | bytes 131072 | tf_op jit(solution)/shard_map/all_to_all | solution.py:262
  28.0 27.9 %all_to_all.26.sums = f32[8,2,8,256]{3,2,1,0:T(8,128)S(1)} all-to-all(f32[8,2,8,256]{3,2,1,0:T(8,128)S(1)} %shard_map.39), channel_id=1, replica_groups={{0,4,8,12,16,20,24,28},{1,5,9,13,17,21,25,29},{2,6,10,14,18,22,26,30},{..., dimensions={0} | all-to-all | bytes 262144 | tf_op jit(solution)/shard_map/all_to_all | solution.py:262
  55.9 7.6 %all_to_all.27.links = f32[4,2,8,256]{3,2,1,0:T(8,128)S(1)} all-to-all(f32[4,2,8,256]{3,2,1,0:T(8,128)S(1)} %shard_map.40), channel_id=1, replica_groups={{0,1,2,3},{4,5,6,7},{8,9,10,11},{12,13,14,15},{16,17,18,19},{20,21,22,2..., dimensions={0} | all-to-all | bytes 131072 | tf_op jit(solution)/shard_map/all_to_all | solution.py:262
  63.5 0.3 shard_map.41
  63.8 9.3 %all_to_all.28.ends = f32[4,2,2,8,512]{4,3,2,1,0:T(8,128)S(1)} all-to-all(f32[4,2,2,8,512]{4,3,2,1,0:T(8,128)S(1)} %get-tuple-element.20), channel_id=1, replica_groups={{0,32,64,96},{128,160,192,224},{256,288,320,352},{384,416,448,480},{1,3..., dimensions={0} | all-to-all | bytes 524288 | tf_op jit(solution)/shard_map/all_to_all | solution.py:262
  73.2 11.7 %all_to_all.29.sums = f32[4,2,2,8,512]{4,3,2,1,0:T(8,128)S(1)} all-to-all(f32[4,2,2,8,512]{4,3,2,1,0:T(8,128)S(1)} %shard_map.42), channel_id=1, replica_groups={{0,128,256,384},{32,160,288,416},{64,192,320,448},{96,224,352,480},{1,1..., dimensions={0} | all-to-all | bytes 524288 | tf_op jit(solution)/shard_map/all_to_all | solution.py:262
  84.9 0.8 shard_map.43
  (3 shorter events, 0.1 us)
Async XLA Ops:
  0.0 18.1 %copy-start.2 = (f32[8,8,512]{2,1,0:T(8,128)S(1)}, f32[8,8,512]{2,1,0:T(8,128)}, u32[]{:S(2)}) copy-start(f32[8,8,512]{2,1,0:T(8,128)} %volt.1) | copy-start | bytes 393220
  0.0 18.2 %copy-start = (f32[3,8,8,512]{3,2,1,0:T(8,128)S(1)}, f32[3,8,8,512]{3,2,1,0:T(8,128)}, u32[]{:S(2)}) copy-start(f32[3,8,8,512]{3,2,1,0:T(8,128)} %vel.1) | copy-start | bytes 1179652
  0.0 18.2 %copy-start.1 = (f32[2,8,8,512]{3,2,1,0:T(8,128)S(1)}, f32[2,8,8,512]{3,2,1,0:T(8,128)}, u32[]{:S(2)}) copy-start(f32[2,8,8,512]{3,2,1,0:T(8,128)} %conc.1) | copy-start | bytes 786436
  1.9 16.3 %collective-permute-start = (f32[4,8,512]{2,1,0:T(8,128)}, f32[4,8,512]{2,1,0:T(8,128)S(1)}, u32[]{:S(2)}, u32[]{:S(2)}) collective-permute-start(f32[4,8,512]{2,1,0:T(8,128)} %get-tuple-element.15), channel_id=1, source_target_pairs={{0,1},{1,2},{2,3},{3,4},{4,5},{5,6},{6,7},{7,8},{8,9},{9,10},{10,1... | collective-permute-start | bytes 196616 | tf_op jit(solution)/shard_map/ppermute | solution.py:295
  7.4 10.8 %collective-permute-start.2 = (f32[4,8,512]{2,1,0:T(8,128)}, f32[4,8,512]{2,1,0:T(8,128)S(1)}, u32[]{:S(2)}, u32[]{:S(2)}) collective-permute-start(f32[4,8,512]{2,1,0:T(8,128)} %get-tuple-element.13.low_edge), channel_id=1, source_target_pairs={{32,0},{64,32},{96,64},{128,96},{160,128},{192,160},{224,192},{256... | collective-permute-start | bytes 196616 | tf_op jit(solution)/shard_map/ppermute | solution.py:297
  12.6 5.6 %collective-permute-start.1 = (f32[4,8,512]{2,1,0:T(8,128)}, f32[4,8,512]{2,1,0:T(8,128)S(1)}, u32[]{:S(2)}, u32[]{:S(2)}) collective-permute-start(f32[4,8,512]{2,1,0:T(8,128)} %get-tuple-element.14.high_edge), channel_id=1, source_target_pairs={{0,32},{32,64},{64,96},{96,128},{128,160},{160,192},{192,224},{224... | collective-permute-start | bytes 196616 | tf_op jit(solution)/shard_map/ppermute | solution.py:296
  18.2 0.8 copy-start.3
  19.0 0.8 copy-start.4

commit v3 on v1

v3 whole, which is shorter than its diff:
```python
import functools

import jax
import jax.numpy as jnp
import numpy as np
from jax import lax
from jax.experimental import pallas as pl
from jax.experimental.pallas import tpu as pltpu
from jax.sharding import PartitionSpec as P

ADVECT_STEP = 0.2
DRIFT_RATES = (1.0, -0.5)
FLUX_SCALE = 0.25 * ADVECT_STEP
HIGHEST = lax.Precision.HIGHEST
TEAM = 4
LANES = 128


def line_factors(rate):
    base = 1.0 + 2.0 * rate
    root = np.sqrt(1.0 + 4.0 * rate)
    return float(2.0 * rate / (base + root)), float(1.0 / root)


def block_tables(decay, gain, cells):
    place = np.arange(cells)
    local = gain * decay ** np.abs(place[:, None] - place[None, :])
    collect = np.stack([decay ** (cells - 1 - place), decay**place], axis=1)
    spread = gain * np.stack([decay ** (place + 1), decay ** (cells - place)])
    return local, collect, spread


def wall_tables(rates, stream_rates, width, depth):
    layers = width + 1
    size = 2 * layers * depth
    cells = 2 * width * depth
    inject = np.zeros((2, LANES, 2, layers, depth))
    into_cells = inject[0].reshape(2, width, depth, 2, layers, depth)
    top = inject[1, : 2 * width].reshape(2, width, 2, layers, depth)
    bottom = inject[1, 2 * width : 4 * width].reshape(2, width, 2, layers, depth)
    before = inject[1, LANES // 2 : LANES // 2 + 2 * depth].reshape(2, depth, 2, layers, depth)
    near = np.zeros((2, layers, depth, 2, layers, depth))
    collect = np.zeros((2, layers, depth, 2, 2, LANES // 4))
    spread = np.zeros((2, 2, LANES // 4, 2, layers, depth))
    output = np.zeros((2, layers, depth, 2, LANES))
    out_cells = output[:, :, :, 0].reshape(2, layers, depth, 2, width, depth)
    out_sums = output[:, :, :, 1, : 4 * depth].reshape(2, layers, depth, 2, 2, depth)
    out_before = output[:, :, :, 1, 4 * depth : 6 * depth].reshape(2, layers, depth, 2, depth)
    for s in range(2):
        local, gather, hand = block_tables(*line_factors(rates[s]), depth)
        decay = line_factors(stream_rates[s])[0]
        for layer in range(layers):
            x = layer - 1
            near[s, layer, :, s, layer, :] = local
            collect[s, layer, :, :, s, layer] = gather
            spread[:, s, layer, s, layer, :] = hand
            for z in range(depth):
                if layer:
                    into_cells[s, x, z, s, layer, z] = 1.0
                    out_cells[s, layer, z, s, x, z] = 1.0
                else:
                    before[s, z, s, layer, z] = 1.0
                    out_before[s, layer, z, s, z] = 1.0
                out_sums[s, layer, z, 0, s, z] = decay ** (width - 1 - x)
                out_sums[s, layer, z, 1, s, z] = decay**x
            if layer:
                top[s, x, s, layer, depth - 1] = -FLUX_SCALE
                bottom[s, x, s, layer, 0] = FLUX_SCALE
    inject = inject.reshape(2 * LANES, size)
    near = near.reshape(size, size)
    output = output.reshape(size, 2 * LANES)
    gathered = inject @ collect.reshape(size, LANES)
    solved = inject @ near @ output
    handed = spread.reshape(LANES, size) @ output
    return gathered, np.concatenate([solved[:LANES], handed, solved[LANES:]])


def stream_tables(rates, width, depth):
    near = np.zeros((2, width, depth, 2, width, depth))
    spread = np.zeros((LANES, 2, width, depth))
    entering = spread[: 4 * depth].reshape(2, 2, depth, 2, width, depth)
    before = spread[4 * depth : 6 * depth].reshape(2, depth, 2, width, depth)
    for s in range(2):
        local, _, hand = block_tables(*line_factors(rates[s]), width)
        for z in range(depth):
            near[s, :, z, s, :, z] = local
            entering[:, s, z, s, :, z] = hand
            before[s, z, s, :, z] = hand[0]
    cells = 2 * width * depth
    return np.concatenate([near.reshape(cells, cells), spread.reshape(LANES, cells)])


def whole(memory=pltpu.VMEM):
    return pl.BlockSpec(memory_space=memory)


def call(kernel, outs, ins, scratch=(), memory=pltpu.VMEM, room=32):
    return pl.pallas_call(
        kernel,
        out_shape=[jax.ShapeDtypeStruct(shape, jnp.float32) for shape in outs],
        in_specs=[whole(memory)] * len(ins),
        out_specs=[whole(memory)] * len(outs),
        scratch_shapes=list(scratch),
        compiler_params=pltpu.CompilerParams(vmem_limit_bytes=room * 1024 * 1024),
    )(*ins)


def edge_kernel(conc, vel, volt, edge, arrived):
    last = volt.shape[0] - 1
    copies = [
        pltpu.make_async_copy(source, edge.at[place], arrived.at[place])
        for place, source in enumerate((conc.at[0, last], conc.at[1, last], vel.at[0, last], volt.at[last]))
    ]
    for copy in copies:
        copy.start()
    for copy in copies:
        copy.wait()


def face(conc_low, conc_high, speed_low, speed_high, volt_low, volt_high, species):
    drift = speed_low + speed_high - (2.0 * DRIFT_RATES[species]) * (volt_high - volt_low)
    return (conc_low + conc_high) * drift


def predict_kernel(conc, vel, volt, left_halo, shares, rows):
    width, depth, span = volt.shape
    row = lax.broadcasted_iota(jnp.int32, (depth, span), 0)
    rows[LANES:] = jnp.zeros((LANES, span), jnp.float32)
    left = [face(left_halo[s], conc[s, 0], left_halo[2], vel[0, 0], left_halo[3], volt[0], s) for s in range(2)]
    for s in range(2):
        start = LANES + LANES // 2 + s * depth
        rows[start : start + depth] = -FLUX_SCALE * left[s]
    for x in range(width):
        here = volt[x]
        rise = vel[1, x]
        volt_up = pltpu.roll(here, depth - 1, 0)
        volt_next = pltpu.roll(here, span - 1, 1)
        speed_up = pltpu.roll(rise, depth - 1, 0)
        speed_next = pltpu.roll(vel[2, x], span - 1, 1)
        for s in range(2):
            value = conc[s, x]
            wall = face(value, pltpu.roll(value, depth - 1, 0), rise, speed_up, here, volt_up, s)
            wall = jnp.where(row == depth - 1, 0.0, wall)
            side = face(value, pltpu.roll(value, span - 1, 1), vel[2, x], speed_next, here, volt_next, s)
            total = (wall - pltpu.roll(wall, 1, 0)) + (side - pltpu.roll(side, 1, 1)) - left[s]
            if x + 1 < width:
                left[s] = face(value, conc[s, x + 1], vel[0, x], vel[0, x + 1], here, volt[x + 1], s)
                total = total + left[s]
            place = s * width + x
            rows[place * depth : (place + 1) * depth] = value - FLUX_SCALE * total
            drift = (2.0 * DRIFT_RATES[s]) * here
            top = slice(depth - 1, depth)
            for part, edge in enumerate(
                (value[top], rise[top] + drift[top], value[0:1], rise[0:1] - drift[0:1])
            ):
                line = LANES + part * 2 * width + place
                rows[line : line + 1] = edge
    places = shares.shape[2]
    tiles = LANES // places
    for part in range(2):
        for chunk in range(span // LANES):
            turned = rows[part * LANES : (part + 1) * LANES, chunk * LANES : (chunk + 1) * LANES].T
            shares[chunk * tiles : (chunk + 1) * tiles, part] = turned.reshape(tiles, places, LANES)


def by_lane(values, lane, unit):
    return jnp.where(lax.rem(lax.div(lane, unit), 2) == 0, values[0], values[1])


def wall_kernel(decays, stream_steps, blocks, width, depth, parts, collect, solve, solved, ends, sums, carry, fluxes):
    members, _, places, _ = parts.shape
    flat = members * places
    lane = lax.broadcasted_iota(jnp.int32, (places, LANES), 1)
    faces = 2 * width
    for m in range(TEAM):
        below = jnp.zeros((places, LANES), jnp.float32)
        for b in range(blocks):
            if b == 0:
                meet = pltpu.roll(parts[m * blocks, 1], LANES - 2 * faces, 1)
                below = meet * pltpu.roll(meet, LANES - faces, 1)
            meet = parts[m * blocks + b, 1]
            if b + 1 < blocks:
                meet = meet + pltpu.roll(parts[m * blocks + b + 1, 1], LANES - 2 * faces, 1)
            above = meet * pltpu.roll(meet, LANES - faces, 1)
            fluxes[m * blocks + b] = jnp.where(
                lane < faces, above, jnp.where(lane < 2 * faces, pltpu.roll(below, faces, 1), parts[m * blocks + b, 1])
            )
            below = above
    value = parts[:, 0].reshape(flat, LANES)
    flux = fluxes[...].reshape(flat, LANES)
    carry[...] = jnp.dot(
        jnp.concatenate([value, flux], axis=1), collect[...], precision=HIGHEST, preferred_element_type=jnp.float32
    ).reshape(members, places, LANES)
    side = LANES // 2
    unit = LANES // 4
    entering = lane < side
    step = by_lane([decay**depth for decay in decays], lane, unit)
    mirrors = [decay ** (depth * blocks + 1) for decay in decays]
    mirror = by_lane(mirrors, lane, unit)
    scale = by_lane([-d / (1.0 - m * m) for d, m in zip(decays, mirrors)], lane, unit)
    weights = [
        jnp.where(
            entering,
            by_lane([decay ** (depth * b) for decay in decays], lane, unit),
            by_lane([decay ** (depth * (blocks - 1 - b)) for decay in decays], lane, unit),
        )
        for b in range(blocks)
    ]
    for m in range(TEAM):
        before = jnp.zeros((places, LANES), jnp.float32)
        after = jnp.zeros((places, LANES), jnp.float32)
        befores = []
        afters = [None] * blocks
        for b in range(blocks):
            befores.append(before)
            before = step * before + carry[m * blocks + b]
        for b in range(blocks - 1, -1, -1):
            afters[b] = after
            after = step * after + carry[m * blocks + b]
        total = jnp.where(entering, before, after)
        mirrored = scale * (pltpu.roll(total, side, 1) - mirror * total)
        for b in range(blocks):
            carry[m * blocks + b] = jnp.where(entering, befores[b], afters[b]) + weights[b] * mirrored
    full = jnp.concatenate([value, carry[...].reshape(flat, LANES), flux], axis=1)
    result = jnp.dot(full, solve[...], precision=HIGHEST, preferred_element_type=jnp.float32)
    solved[...] = result[:, :LANES].reshape(members, places, LANES)
    ends[...] = result[:, LANES:].reshape(members, places, LANES)
    step = by_lane(stream_steps, lane, depth)
    entering = lane < 2 * depth
    pack = LANES // (4 * depth)
    for group in range(blocks // pack):
        packed = None
        for part in range(pack):
            b = group * pack + part
            before = ends[b]
            after = ends[(TEAM - 1) * blocks + b]
            for m in range(1, TEAM):
                before = step * before + ends[m * blocks + b]
                after = step * after + ends[(TEAM - 1 - m) * blocks + b]
            both = jnp.where(entering, before, jnp.where(lane < 4 * depth, after, 0.0))
            packed = packed + pltpu.roll(both, part * 4 * depth, 1) if part else both
        for team in range(sums.shape[0]):
            sums[team, group] = packed


def stream_kernel(steps, blocks, depth, cells, ends, sums, solve, solved, carry):
    places = cells.shape[1]
    flat = cells.shape[0] * places
    teams, groups = sums.shape[0], sums.shape[1]
    pack = blocks // groups
    team = lax.div(lax.axis_index("stream"), TEAM)
    lane = lax.broadcasted_iota(jnp.int32, (places, LANES), 1)
    entering = lax.rem(lane, 4 * depth) < 2 * depth
    step = by_lane(steps, lane, depth)
    leap = by_lane([value**TEAM for value in steps], lane, depth)
    closing = by_lane([1.0 / (1.0 - value ** (TEAM * teams)) for value in steps], lane, depth)
    for group in range(groups):
        before = sums[team, group]
        after = before
        for k in range(1, teams):
            before = leap * before + sums[lax.rem(team + k, teams), group]
            after = leap * after + sums[lax.rem(team + teams - k, teams), group]
        both = closing * jnp.where(entering, before, after)
        for part in range(pack):
            b = group * pack + part
            before = pltpu.roll(both, LANES - part * 4 * depth, 1) if part else both
            after = before
            afters = [None] * TEAM
            for m in range(TEAM - 1, -1, -1):
                afters[m] = after
                after = step * after + ends[m * blocks + b]
            for m in range(TEAM):
                own = ends[m * blocks + b]
                carry[m * blocks + b] = jnp.where(lane < 4 * depth, jnp.where(entering, before, afters[m]), own)
                before = step * before + own
    full = jnp.concatenate([cells[...].reshape(flat, LANES), carry[...].reshape(flat, LANES)], axis=1)
    result = jnp.dot(full, solve[...], precision=HIGHEST, preferred_element_type=jnp.float32)
    solved[...] = result.reshape(cells.shape)


def place_kernel(shares, out):
    _, width, depth, span = out.shape
    tiles = LANES // shares.shape[1]
    for chunk in range(span // LANES):
        turned = shares[chunk * tiles : (chunk + 1) * tiles].reshape(LANES, LANES).T
        for s in range(2):
            for x in range(width):
                start = (s * width + x) * depth
                out[s, x, :, chunk * LANES : (chunk + 1) * LANES] = turned[start : start + depth]


def per_device(concentration, velocity, potential):
    _, width, depth, span = concentration.shape
    stream = lax.axis_size("stream")
    wall = lax.axis_size("wall")
    stream_total = width * stream
    wall_total = depth * wall
    rates_x = (4.0 * width * width, float(stream_total * stream_total // 25))
    rates_z = (4.0 * depth * depth, float(wall_total * wall_total // 16))
    steps_x = [line_factors(rate)[0] ** width for rate in rates_x]
    decays_z = [line_factors(rate)[0] for rate in rates_z]
    collect_z, solve_z = wall_tables(rates_z, rates_x, width, depth)
    solve_x = stream_tables(rates_x, width, depth)

    (edge,) = call(
        edge_kernel,
        [(4, depth, span)],
        (concentration, velocity, potential),
        [pltpu.SemaphoreType.DMA((4,))],
        pltpu.HBM,
        62,
    )
    left_halo = lax.ppermute(edge, "stream", [(i, (i + 1) % stream) for i in range(stream)])

    members = TEAM * wall
    teams = stream // TEAM
    plane = [[b * stream + t * TEAM + m for m in range(TEAM) for b in range(wall)] for t in range(teams)]
    ranks = [[t * TEAM + m for t in range(teams)] for m in range(TEAM)]
    swap = functools.partial(lax.all_to_all, split_axis=0, concat_axis=0, tiled=True)
    table = functools.partial(jnp.array, dtype=jnp.float32)
    places = span // members
    tile = (members, places, LANES)
    (shares,) = call(
        predict_kernel,
        [(members, 2, places, LANES)],
        (concentration, velocity, potential, left_halo),
        [pltpu.VMEM((2 * LANES, span), jnp.float32)],
    )
    parts = swap(shares, ("wall", "stream"), axis_index_groups=plane)
    pack = LANES // (4 * depth)
    cells, ends, sums = call(
        functools.partial(wall_kernel, decays_z, steps_x, wall, width, depth),
        [tile, tile, (teams, wall // pack, places, LANES)],
        (parts, table(collect_z), table(solve_z)),
        [pltpu.VMEM(tile, jnp.float32), pltpu.VMEM(tile, jnp.float32)],
    )
    sums = swap(sums, "stream", axis_index_groups=ranks)
    (cells,) = call(
        functools.partial(stream_kernel, steps_x, wall, depth),
        [tile],
        (cells, ends, sums, table(solve_x)),
        [pltpu.VMEM(tile, jnp.float32)],
    )
    shares = swap(cells, ("wall", "stream"), axis_index_groups=plane)
    (out,) = call(place_kernel, [concentration.shape], (shares,))
    return out


def solution(mesh):
    return jax.shard_map(
        per_device,
        mesh=mesh,
        in_specs=(
            P(None, "stream", "wall", None),
            P(None, "stream", "wall", None),
            P("stream", "wall", None),
        ),
        out_specs=P(None, "stream", "wall", None),
        check_vma=False,
    )
```

time: 89.6 us -> 83.9 us (0.936)
  blocking collectives: 68.1 us -> 58.8 us
  waiting for transfers between devices: 3.41 us -> 10.8 us
  starting transfers between devices: 12.6 us -> 5.48 us
  Pallas kernels: 2.13 us -> 8.5 us
  local copies, waits for them, and re-layouts: 2.86 us -> 0.03 us
    all_to_all x4 -> x3, blocking collectives: 68.1 us -> 58.8 us  [the longest x1 22.4 us: per_device(): sums = swap(sums, 'stream', axis_index_groups=ranks)]
    ppermute x3 -> x1, waiting for transfers between devices: 3.41 us -> 10.8 us  [per_device(): lax.ppermute(edge, 'stream', [(i, (i + 1) % stream) for i in range(stream)])]
    ppermute x3 -> x1, starting transfers between devices: 12.6 us -> 5.48 us  [per_device(): lax.ppermute(edge, 'stream', [(i, (i + 1) % stream) for i in range(stream)])]
    pallas_call x6 -> x5, Pallas kernels: 2.13 us -> 8.5 us  [call(): pl.pallas_call(kernel, out_shape=[jax.ShapeDtypeStruct(shape, jnp.float32...]
    unnamed x10 -> x12, local copies, waits for them, and re-layouts: 2.86 us -> 0.03 us
  transfers between devices with their start and end apart: 3 -> 1, of which waited for: 1 -> 1; matrix products, arithmetic and copies ran while one was open for 0% -> 0% of each run, Pallas kernels for 0% -> 0%
where the time goes in v3:
time: 83.9 us; the launch traced here: 83.7 us
  blocking collectives  58.8 us (70%)
  waiting for transfers between devices  10.8 us (13%)
  Pallas kernels  8.5 us (10%)
  starting transfers between devices  5.48 us (7%)
    all_to_all x1, blocking collectives, per_device(): sums = swap(sums, 'stream', axis_index_groups=ranks)  22.4 us
    all_to_all x1, blocking collectives, per_device(): parts = swap(shares, ('wall', 'stream'), axis_index_groups=plane)  18.7 us
    all_to_all x1, blocking collectives, per_device(): shares = swap(cells, ('wall', 'stream'), axis_index_groups=plane)  17.7 us
    ppermute x1, waiting for transfers between devices, per_device(): lax.ppermute(edge, 'stream', [(i, (i + 1) % stream) for i in range(stream)])  10.8 us
    pallas_call x5, Pallas kernels, call(): pl.pallas_call(kernel, out_shape=[jax.ShapeDtypeStruct(shape, jnp.float32...  8.5 us
    ppermute x1, starting transfers between devices, per_device(): lax.ppermute(edge, 'stream', [(i, (i + 1) % stream) for i in range(stream)])  5.48 us
  transfers between devices with their start and end apart: 1, of which 1 were waited for; matrix products, arithmetic and copies ran while one was open for 0% of the time, Pallas kernels for 0%

profile of v3, /device:TPU:1, one launch (start us, length us, event | category | flops | bytes accessed | tf_op | source)
XLA Modules:
  0.0 83.7 jit_solution(18420482429272865609)
XLA Ops:
  0.0 0.0 copy-start.2
  0.0 0.0 copy-start
  0.0 0.0 copy-start.1
  0.0 3.2 %shard_map.64 = f32[4,8,512]{2,1,0:T(8,128)} custom-call(f32[2,8,8,512]{3,2,1,0:T(8,128)} %conc.3, f32[3,8,8,512]{3,2,1,0:T(8,128)} %vel.3, f32[8,8,512]{2,1,0:T(8,128)} %volt.3), custom_call_target="tpu_custom_call" | custom-call | tf_op jit(solution)/shard_map/pallas_call | solution.py:98
  3.2 5.5 %collective-permute-start = (f32[4,8,512]{2,1,0:T(8,128)}, f32[4,8,512]{2,1,0:T(8,128)S(1)}, u32[]{:S(2)}, u32[]{:S(2)}) collective-permute-start(f32[4,8,512]{2,1,0:T(8,128)} %shard_map.64), channel_id=1, source_target_pairs={{0,1},{1,2},{2,3},{3,4},{4,5},{5,6},{6,7},{7,8},{8,9},{9,10},{10,1... | collective-permute-start | bytes 196616 | tf_op jit(solution)/shard_map/ppermute | solution.py:313
  8.7 10.8 %collective-permute-done.left_halo = f32[4,8,512]{2,1,0:T(8,128)S(1)} collective-permute-done((f32[4,8,512]{2,1,0:T(8,128)}, f32[4,8,512]{2,1,0:T(8,128)S(1)}, u32[]{:S(2)}, u32[]{:S(2)}) %collective-permute-start) | collective-permute-done | bytes 65568 | tf_op jit(solution)/shard_map/ppermute | solution.py:313
  19.5 0.0 copy-done.2
  19.5 0.0 copy-done
  19.5 0.0 copy-done.1
  19.5 1.2 %shard_map.65 = f32[64,2,8,128]{3,2,1,0:T(8,128)S(1)} custom-call(f32[2,8,8,512]{3,2,1,0:T(8,128)S(1)} %copy-done.1, f32[3,8,8,512]{3,2,1,0:T(8,128)S(1)} %copy-done, f32[8,8,512]{2,1,0:T(8,128)S(1)} %copy-done.2, f32[4,8,512]{2,1,0:T(8,128)S(1)} %collective-permute-done.left_halo), custom_call_target="tpu_custom_call" | custom-call | tf_op jit(solution)/shard_map/pallas_call | solution.py:98
  20.7 0.0 copy-start.3
  20.7 0.0 copy-start.5
  20.7 18.7 %all_to_all.15.parts = f32[64,2,8,128]{3,2,1,0:T(8,128)S(1)} all-to-all(f32[64,2,8,128]{3,2,1,0:T(8,128)S(1)} %shard_map.65), channel_id=1, replica_groups={{0,32,64,96,128,160,192,224,256,288,320,352,384,416,448,480,1,33,65,97,..., dimensions={0} | all-to-all | bytes 1048576 | tf_op jit(solution)/shard_map/all_to_all | solution.py:329
  39.4 0.0 copy-done.3
  39.4 0.0 copy-done.5
  39.4 2.7 %shard_map.66 = (f32[64,8,128]{2,1,0:T(8,128)S(1)}, f32[64,8,128]{2,1,0:T(8,128)S(1)}, f32[8,4,8,128]{3,2,1,0:T(8,128)S(1)}) custom-call(f32[64,2,8,128]{3,2,1,0:T(8,128)S(1)} %all_to_all.15.parts, f32[256,128]{1,0:T(8,128)S(1)} %copy-done.5, f32[384,256]{1,0:T(8,128)S(1)} %copy-done.3), custom_call_target="tpu_custom_call" | custom-call | tf_op jit(solution)/shard_map/pallas_call | solution.py:98
  42.1 0.0 copy-start.4
  42.1 22.4 %all_to_all.16.sums = f32[8,4,8,128]{3,2,1,0:T(8,128)S(1)} all-to-all(f32[8,4,8,128]{3,2,1,0:T(8,128)S(1)} %get-tuple-element.10), channel_id=1, replica_groups={{0,4,8,12,16,20,24,28},{1,5,9,13,17,21,25,29},{2,6,10,14,18,22,26,30},{..., dimensions={0} | all-to-all | bytes 262144 | tf_op jit(solution)/shard_map/all_to_all | solution.py:337
  64.5 0.0 copy-done.4
  64.5 0.7 shard_map.67
  65.2 17.7 %all_to_all.17.shares = f32[64,8,128]{2,1,0:T(8,128)S(1)} all-to-all(f32[64,8,128]{2,1,0:T(8,128)S(1)} %shard_map.67), channel_id=1, replica_groups={{0,32,64,96,128,160,192,224,256,288,320,352,384,416,448,480,1,33,65,97,..., dimensions={0} | all-to-all | bytes 524288 | tf_op jit(solution)/shard_map/all_to_all | solution.py:344
  82.8 0.8 shard_map.68
Async XLA Ops:
  0.0 19.5 %copy-start.2 = (f32[8,8,512]{2,1,0:T(8,128)S(1)}, f32[8,8,512]{2,1,0:T(8,128)}, u32[]{:S(2)}) copy-start(f32[8,8,512]{2,1,0:T(8,128)} %volt.3) | copy-start | bytes 393220
  0.0 19.5 %copy-start = (f32[3,8,8,512]{3,2,1,0:T(8,128)S(1)}, f32[3,8,8,512]{3,2,1,0:T(8,128)}, u32[]{:S(2)}) copy-start(f32[3,8,8,512]{3,2,1,0:T(8,128)} %vel.3) | copy-start | bytes 1179652
  0.0 19.5 %copy-start.1 = (f32[2,8,8,512]{3,2,1,0:T(8,128)S(1)}, f32[2,8,8,512]{3,2,1,0:T(8,128)}, u32[]{:S(2)}) copy-start(f32[2,8,8,512]{3,2,1,0:T(8,128)} %conc.3) | copy-start | bytes 786436
  3.2 16.3 %collective-permute-start = (f32[4,8,512]{2,1,0:T(8,128)}, f32[4,8,512]{2,1,0:T(8,128)S(1)}, u32[]{:S(2)}, u32[]{:S(2)}) collective-permute-start(f32[4,8,512]{2,1,0:T(8,128)} %shard_map.64), channel_id=1, source_target_pairs={{0,1},{1,2},{2,3},{3,4},{4,5},{5,6},{6,7},{7,8},{8,9},{9,10},{10,1... | collective-permute-start | bytes 196616 | tf_op jit(solution)/shard_map/ppermute | solution.py:313
  20.7 18.8 %copy-start.3 = (f32[384,256]{1,0:T(8,128)S(1)}, f32[384,256]{1,0:T(8,128)}, u32[]{:S(2)}) copy-start(f32[384,256]{1,0:T(8,128)} %constant.7.clone.solve) | copy-start | bytes 1179652
  20.7 18.8 %copy-start.5 = (f32[256,128]{1,0:T(8,128)S(1)}, f32[256,128]{1,0:T(8,128)}, u32[]{:S(2)}) copy-start(f32[256,128]{1,0:T(8,128)} %constant.6.clone.collect) | copy-start | bytes 393220
  42.1 22.4 %copy-start.4 = (f32[256,128]{1,0:T(8,128)S(1)}, f32[256,128]{1,0:T(8,128)}, u32[]{:S(2)}) copy-start(f32[256,128]{1,0:T(8,128)} %constant.8.clone.solve) | copy-start | bytes 393220

commit v4 on v3

v4 whole, which is shorter than its diff:
```python
import functools

import jax
import jax.numpy as jnp
import numpy as np
from jax import lax
from jax.experimental import pallas as pl
from jax.experimental.pallas import tpu as pltpu
from jax.sharding import PartitionSpec as P

ADVECT_STEP = 0.2
DRIFT_RATES = (1.0, -0.5)
FLUX_SCALE = 0.25 * ADVECT_STEP
TEAM = 4
HALVES = 2
LANES = 128


def line_factors(rate):
    base = 1.0 + 2.0 * rate
    root = np.sqrt(1.0 + 4.0 * rate)
    return float(2.0 * rate / (base + root)), float(1.0 / root)


def block_tables(decay, gain, cells):
    place = np.arange(cells)
    local = gain * decay ** np.abs(place[:, None] - place[None, :])
    collect = np.stack([decay ** (cells - 1 - place), decay**place], axis=1)
    spread = gain * np.stack([decay ** (place + 1), decay ** (cells - place)])
    return local, collect, spread


def collect_table(rates_x, rates_z, width, depth):
    table = np.zeros((4 * depth + 4 * width, 2, width, depth))
    stream_sums = table[: 4 * depth].reshape(2, 2, depth, 2, width, depth)
    wall_sums = table[4 * depth :].reshape(2, 2, width, 2, width, depth)
    for s in range(2):
        _, gather_x, _ = block_tables(*line_factors(rates_x[s]), width)
        _, gather_z, _ = block_tables(*line_factors(rates_z[s]), depth)
        for z in range(depth):
            stream_sums[:, s, z, s, :, z] = gather_x.T
        for x in range(width):
            wall_sums[:, s, x, s, x, :] = gather_z.T
    return table.reshape(-1, 2 * width * depth)


def wall_tables(rates_x, rates_z, width, depth):
    unit = LANES // 4
    collect = np.zeros((2, LANES, 2, 2, unit))
    solve = np.zeros((3, LANES, LANES))
    sums_in = collect[0, : 4 * depth].reshape(2, 2, depth, 2, 2, unit)
    ends_in = collect[0, 4 * depth : 4 * (depth + width)].reshape(2, 2, width, 2, 2, unit)
    flux_in = collect[1, : 4 * width].reshape(2, 2, width, 2, 2, unit)
    near = solve[0, : 4 * depth, : 4 * depth].reshape(2, 2, depth, 2, 2, depth)
    spread = solve[1, :, : 4 * depth].reshape(2, 2, unit, 2, 2, depth)
    moved = solve[1, :, 4 * depth : 4 * (depth + width)].reshape(2, 2, unit, 2, 2, width)
    flux_near = solve[2, : 4 * width, : 4 * depth].reshape(2, 2, width, 2, 2, depth)
    flux_moved = solve[2, : 4 * width, 4 * depth : 4 * (depth + width)].reshape(2, 2, width, 2, 2, width)
    for s in range(2):
        _, gather_x, _ = block_tables(*line_factors(rates_x[s]), width)
        local, gather_z, hand = block_tables(*line_factors(rates_z[s]), depth)
        decay = line_factors(rates_z[s])[0]
        for side in range(2):
            sums_in[side, s, :, :, s, width + side] = gather_z
            near[side, s, :, side, s, :] = local
            spread[:, s, width + side, side, s, :] = hand
            for x in range(width):
                ends_in[side, s, x, side, s, x] = 1.0
                moved[side, s, x, side, s, x] = 1.0
        for end, cell, size in ((0, depth - 1, -FLUX_SCALE), (1, 0, FLUX_SCALE)):
            for x in range(width):
                flux_in[end, s, x, :, s, x] = size * gather_z[cell]
                flux_moved[end, s, x, 1 - end, s, x] = size / decay
                for side in range(2):
                    flux_in[end, s, x, :, s, width + side] = size * gather_x[x, side] * gather_z[cell]
                    flux_near[end, s, x, side, s, :] = size * gather_x[x, side] * local[cell]
    return collect.reshape(2 * LANES, LANES), solve.reshape(3 * LANES, LANES)


def home_table(rates_x, rates_z, width, depth):
    cells = 2 * width * depth
    near = np.zeros((2, width, depth, 2, width, depth))
    stream_spread = np.zeros((2, width, depth, 2, 2, depth))
    wall_spread = np.zeros((2, width, depth, 2, 2, width))
    for s in range(2):
        local_x, _, hand_x = block_tables(*line_factors(rates_x[s]), width)
        local_z, _, hand_z = block_tables(*line_factors(rates_z[s]), depth)
        near[s, :, :, s, :, :] = np.einsum("xa,zb->xzab", local_x, local_z)
        stream_spread[s, :, :, :, s, :] = np.einsum("ex,zb->xzeb", hand_x, np.eye(depth))
        wall_spread[s, :, :, :, s, :] = np.einsum("xa,ez->xzea", local_x, hand_z)
    return np.concatenate([part.reshape(cells, -1) for part in (near, stream_spread, wall_spread)], axis=1)


def call(kernel, outs, ins, scratch=(), aliases=None):
    return pl.pallas_call(
        kernel,
        out_shape=[jax.ShapeDtypeStruct(shape, jnp.float32) for shape in outs],
        in_specs=[pl.BlockSpec(memory_space=pltpu.VMEM)] * len(ins),
        out_specs=[pl.BlockSpec(memory_space=pltpu.VMEM)] * len(outs),
        scratch_shapes=list(scratch),
        input_output_aliases=aliases or {},
        compiler_params=pltpu.CompilerParams(vmem_limit_bytes=32 * 1024 * 1024),
    )(*ins)


def drift(volt, species):
    return (2.0 * DRIFT_RATES[species]) * volt


def face(conc_low, conc_high, speed_low, speed_high, volt_low, volt_high, species):
    return (conc_low + conc_high) * (speed_low + speed_high - drift(volt_high - volt_low, species))


def last_layers(conc, vel, volt):
    return jnp.stack([conc[0, -1], conc[1, -1], vel[0, -1] + drift(volt[-1], 0), vel[0, -1] + drift(volt[-1], 1)])


def split(values):
    high = values.astype(jnp.bfloat16)
    return high, (values - high.astype(jnp.float32)).astype(jnp.bfloat16)


def product(left, right):
    left_high, left_low = split(left)
    right_high, right_low = split(right)
    dot = functools.partial(jnp.dot, preferred_element_type=jnp.float32)
    return dot(left_high, right_high) + (dot(left_low, right_high) + dot(left_high, right_low))


def predict_kernel(conc, vel, volt, collect, cells, rows):
    width, depth, span = volt.shape
    row = lax.broadcasted_iota(jnp.int32, (depth, span), 0)
    left = [None, None]
    sums = 4 * (width + depth)
    for x in range(width):
        here = volt[x]
        rise = vel[1, x]
        volt_up = pltpu.roll(here, depth - 1, 0)
        volt_next = pltpu.roll(here, span - 1, 1)
        speed_up = pltpu.roll(rise, depth - 1, 0)
        speed_next = pltpu.roll(vel[2, x], span - 1, 1)
        for s in range(2):
            value = conc[s, x]
            wall = face(value, pltpu.roll(value, depth - 1, 0), rise, speed_up, here, volt_up, s)
            wall = jnp.where(row == depth - 1, 0.0, wall)
            side = face(value, pltpu.roll(value, span - 1, 1), vel[2, x], speed_next, here, volt_next, s)
            total = (wall - pltpu.roll(wall, 1, 0)) + (side - pltpu.roll(side, 1, 1))
            if x:
                total = total - left[s]
            if x + 1 < width:
                left[s] = face(value, conc[s, x + 1], vel[0, x], vel[0, x + 1], here, volt[x + 1], s)
                total = total + left[s]
            place = s * width + x
            cells[place * depth : (place + 1) * depth] = value - FLUX_SCALE * total
            moved = drift(here, s)
            top = slice(depth - 1, depth)
            for part, edge in enumerate(
                (value[top], rise[top] + moved[top], value[0:1], rise[0:1] - moved[0:1])
            ):
                line = sums + part * 2 * width + place
                rows[line : line + 1] = edge
    rows[:sums] = product(collect[...], cells[...])


def enter_kernel(decays_x, decays_z, cells_in, rows_in, left_halo, conc, vel, volt, shares, cells, rows):
    width, depth, span = volt.shape
    row = lax.broadcasted_iota(jnp.int32, (depth, span), 0)
    for s in range(2):
        decay = decays_x[s]
        flux = (left_halo[s] + conc[s, 0]) * (left_halo[2 + s] + (vel[0, 0] - drift(volt[0], s)))
        taken = -FLUX_SCALE * flux
        gained = (decay - 1.0) * taken
        start = s * width * depth
        cells[start : start + depth] = cells_in[start : start + depth] + gained
        for side, scale in enumerate((decay ** (width - 1) * (decay - 1.0), 1.0 / decay - 1.0)):
            start = (side * 2 + s) * depth
            rows[start : start + depth] = rows_in[start : start + depth] + scale * taken
            weight = jnp.zeros((depth, span), jnp.float32)
            for z in range(depth):
                weight = jnp.where(row == z, decays_z[s] ** (z if side else depth - 1 - z), weight)
            line = 4 * depth + (side * 2 + s) * width
            rows[line : line + 1] = rows_in[line : line + 1] + jnp.sum(weight * gained, axis=0, keepdims=True)
    part = shares.shape[1] // HALVES
    tiles = LANES // part
    for chunk in range(span // LANES):
        turned = rows[:, chunk * LANES : (chunk + 1) * LANES].T
        half, start = divmod(chunk * tiles, shares.shape[0])
        for k in range(tiles):
            shares[start + k, half * part : (half + 1) * part] = turned[k * part : (k + 1) * part]


def by_lane(values, lane, unit):
    return jnp.where(lax.rem(lax.div(lane, unit), 2) == 0, values[0], values[1])


def wall_kernel(decays, stream_steps, blocks, width, depth, parts, collect, solve, ends, sums, carry, fluxes):
    members, places, _ = parts.shape
    flat = members * places
    lane = lax.broadcasted_iota(jnp.int32, (places, LANES), 1)
    faces = 2 * width
    first = LANES // 2
    for m in range(TEAM):
        line = m * blocks
        below = pltpu.roll(parts[line], LANES - first - 2 * faces, 1)
        below = below * pltpu.roll(below, LANES - faces, 1)
        for b in range(blocks):
            meet = pltpu.roll(parts[line + b], LANES - first, 1)
            if b + 1 < blocks:
                meet = meet + pltpu.roll(parts[line + b + 1], LANES - first - 2 * faces, 1)
            above = meet * pltpu.roll(meet, LANES - faces, 1)
            both = jnp.where(lane < faces, above, pltpu.roll(below, faces, 1))
            fluxes[line + b] = jnp.where(lane < 2 * faces, both, 0.0)
            below = above
    value = parts[...].reshape(flat, LANES)
    flux = fluxes[...].reshape(flat, LANES)
    carry[...] = product(jnp.concatenate([value, flux], axis=1), collect[...]).reshape(members, places, LANES)
    side = LANES // 2
    unit = LANES // 4
    entering = lane < side
    step = by_lane([decay**depth for decay in decays], lane, unit)
    mirrors = [decay ** (depth * blocks + 1) for decay in decays]
    mirror = by_lane(mirrors, lane, unit)
    scale = by_lane([-d / (1.0 - m * m) for d, m in zip(decays, mirrors)], lane, unit)
    weights = [
        jnp.where(
            entering,
            by_lane([decay ** (depth * b) for decay in decays], lane, unit),
            by_lane([decay ** (depth * (blocks - 1 - b)) for decay in decays], lane, unit),
        )
        for b in range(blocks)
    ]
    for m in range(TEAM):
        before = jnp.zeros((places, LANES), jnp.float32)
        after = jnp.zeros((places, LANES), jnp.float32)
        befores = []
        afters = [None] * blocks
        for b in range(blocks):
            befores.append(before)
            before = step * before + carry[m * blocks + b]
        for b in range(blocks - 1, -1, -1):
            afters[b] = after
            after = step * after + carry[m * blocks + b]
        total = jnp.where(entering, before, after)
        mirrored = scale * (pltpu.roll(total, side, 1) - mirror * total)
        for b in range(blocks):
            carry[m * blocks + b] = jnp.where(entering, befores[b], afters[b]) + weights[b] * mirrored
    full = jnp.concatenate([value, carry[...].reshape(flat, LANES), flux], axis=1)
    ends[...] = product(full, solve[...]).reshape(members, places, LANES)
    step = by_lane(stream_steps, lane, depth)
    entering = lane < 2 * depth
    pack = LANES // (4 * depth)
    for group in range(blocks // pack):
        packed = None
        for part in range(pack):
            b = group * pack + part
            before = ends[b]
            after = ends[(TEAM - 1) * blocks + b]
            for m in range(1, TEAM):
                before = step * before + ends[m * blocks + b]
                after = step * after + ends[(TEAM - 1 - m) * blocks + b]
            both = jnp.where(entering, before, jnp.where(lane < 4 * depth, after, 0.0))
            packed = packed + pltpu.roll(both, part * 4 * depth, 1) if part else both
        for team in range(sums.shape[0]):
            sums[team, group] = packed


def stream_kernel(steps, blocks, depth, ends, sums, links):
    places = ends.shape[1]
    teams, groups = sums.shape[0], sums.shape[1]
    pack = blocks // groups
    part = links.shape[1]
    team = lax.div(lax.axis_index("stream"), TEAM)
    lane = lax.broadcasted_iota(jnp.int32, (places, LANES), 1)
    entering = lax.rem(lane, 4 * depth) < 2 * depth
    step = by_lane(steps, lane, depth)
    leap = by_lane([value**TEAM for value in steps], lane, depth)
    closing = by_lane([1.0 / (1.0 - value ** (TEAM * teams)) for value in steps], lane, depth)
    for group in range(groups):
        before = sums[team, group]
        after = before
        for k in range(1, teams):
            before = leap * before + sums[lax.rem(team + k, teams), group]
            after = leap * after + sums[lax.rem(team + teams - k, teams), group]
        both = closing * jnp.where(entering, before, after)
        for slot in range(pack):
            b = group * pack + slot
            before = pltpu.roll(both, LANES - slot * 4 * depth, 1) if slot else both
            after = before
            afters = [None] * TEAM
            for m in range(TEAM - 1, -1, -1):
                afters[m] = after
                after = step * after + ends[m * blocks + b]
            for m in range(TEAM):
                own = ends[m * blocks + b]
                carry = jnp.where(lane < 4 * depth, jnp.where(entering, before, afters[m]), own)
                before = step * before + own
                halved = carry + pltpu.roll(pltpu.roll(carry, LANES // HALVES, 1), part, 0)
                links[m * blocks + b] = halved[:part]


def home_kernel(cells, links, table, out, rows, carry):
    _, width, depth, span = out.shape
    part = links.shape[1]
    lanes = LANES // HALVES
    for k in range(links.shape[0]):
        rows[k * part : (k + 1) * part] = links[k]
    for chunk in range(rows.shape[0] // LANES):
        turned = rows[chunk * LANES : (chunk + 1) * LANES].T
        for half in range(HALVES):
            start = half * (span // HALVES) + chunk * LANES
            carry[:, start : start + LANES] = turned[half * lanes : (half + 1) * lanes]
    result = product(table[...], jnp.concatenate([cells[...], carry[...]], axis=0))
    for s in range(2):
        for x in range(width):
            start = (s * width + x) * depth
            out[s, x] = result[start : start + depth]


def per_device(concentration, velocity, potential):
    _, width, depth, span = concentration.shape
    stream = lax.axis_size("stream")
    wall = lax.axis_size("wall")
    stream_total = width * stream
    wall_total = depth * wall
    rates_x = (4.0 * width * width, float(stream_total * stream_total // 25))
    rates_z = (4.0 * depth * depth, float(wall_total * wall_total // 16))
    decays_x = [line_factors(rate)[0] for rate in rates_x]
    decays_z = [line_factors(rate)[0] for rate in rates_z]
    steps_x = [decay**width for decay in decays_x]
    collect_z, solve_z = wall_tables(rates_x, rates_z, width, depth)
    collect = collect_table(rates_x, rates_z, width, depth)
    home = home_table(rates_x, rates_z, width, depth)

    edge = last_layers(concentration, velocity, potential)
    left_halo = lax.ppermute(edge, "stream", [(i, (i + 1) % stream) for i in range(stream)])

    members = TEAM * wall
    teams = stream // TEAM
    plane = [[b * stream + t * TEAM + m for m in range(TEAM) for b in range(wall)] for t in range(teams)]
    ranks = [[t * TEAM + m for t in range(teams)] for m in range(TEAM)]
    swap = functools.partial(lax.all_to_all, split_axis=0, concat_axis=0, tiled=True)
    table = functools.partial(jnp.array, dtype=jnp.float32)
    places = span // members
    tile = (members, places, LANES)
    flat = (2 * width * depth, span)
    cells, rows = call(
        predict_kernel, [flat, (LANES, span)], (concentration, velocity, potential, table(collect))
    )
    shares, cells, rows = call(
        functools.partial(enter_kernel, decays_x, decays_z),
        [tile, flat, (LANES, span)],
        (cells, rows, left_halo, concentration, velocity, potential),
        aliases={0: 1, 1: 2},
    )
    parts = swap(shares, ("wall", "stream"), axis_index_groups=plane)
    pack = LANES // (4 * depth)
    ends, sums = call(
        functools.partial(wall_kernel, decays_z, steps_x, wall, width, depth),
        [tile, (teams, wall // pack, places, LANES)],
        (parts, table(collect_z), table(solve_z)),
        [pltpu.VMEM(tile, jnp.float32), pltpu.VMEM(tile, jnp.float32)],
    )
    sums = swap(sums, "stream", axis_index_groups=ranks)
    (links,) = call(
        functools.partial(stream_kernel, steps_x, wall, depth),
        [(members, places // HALVES, LANES)],
        (ends, sums),
    )
    links = swap(links, ("wall", "stream"), axis_index_groups=plane)
    (out,) = call(
        home_kernel,
        [concentration.shape],
        (cells, links, table(home)),
        [pltpu.VMEM((span // HALVES, LANES), jnp.float32), pltpu.VMEM((LANES // HALVES, span), jnp.float32)],
    )
    return out


def solution(mesh):
    return jax.shard_map(
        per_device,
        mesh=mesh,
        in_specs=(
            P(None, "stream", "wall", None),
            P(None, "stream", "wall", None),
            P("stream", "wall", None),
        ),
        out_specs=P(None, "stream", "wall", None),
        check_vma=False,
    )
```

time: 83.9 us -> 76.1 us (0.907)
  Pallas kernels: 8.5 us -> 3.58 us
  blocking collectives: 58.8 us -> 55 us
  waiting for transfers between devices: 10.8 us -> 7.27 us
  local copies, waits for them, and re-layouts: 0.03 us -> 3.47 us
    pallas_call x5, Pallas kernels: 8.5 us -> 3.58 us  [call(): pl.pallas_call(kernel, out_shape=[jax.ShapeDtypeStruct(shape, jnp.float32...]
    ppermute x1, waiting for transfers between devices: 10.8 us -> 7.27 us  [per_device(): lax.ppermute(edge, 'stream', [(i, (i + 1) % stream) for i in range(stream)])]
    unnamed x12 -> x14, local copies, waits for them, and re-layouts: 0.03 us -> 2.68 us
    all_to_all x1, blocking collectives: 18.7 us -> 16.3 us  [per_device(): parts = swap(shares, ('wall', 'stream'), axis_index_groups=plane)]
    all_to_all x1, blocking collectives: 17.7 us -> 16.1 us  [per_device(): links = swap(links, ('wall', 'stream'), axis_index_groups=plane)]
  transfers between devices with their start and end apart: 1 -> 1, of which waited for: 1 -> 1; matrix products, arithmetic and copies ran while one was open for 0% -> 0% of each run, Pallas kernels for 0% -> 1%
where the time goes in v4:
time: 76.1 us; the launch traced here: 75.6 us
  blocking collectives  55 us (72%)
  waiting for transfers between devices  7.27 us (10%)
  starting transfers between devices  5.48 us (7%)
  Pallas kernels  3.58 us (5%)
  local copies, waits for them, and re-layouts  3.47 us (5%)
    all_to_all x1, blocking collectives, per_device(): sums = swap(sums, 'stream', axis_index_groups=ranks)  22.6 us
    all_to_all x1, blocking collectives, per_device(): parts = swap(shares, ('wall', 'stream'), axis_index_groups=plane)  16.3 us
    all_to_all x1, blocking collectives, per_device(): links = swap(links, ('wall', 'stream'), axis_index_groups=plane)  16.1 us
    ppermute x1, waiting for transfers between devices, per_device(): lax.ppermute(edge, 'stream', [(i, (i + 1) % stream) for i in range(stream)])  7.27 us
    ppermute x1, starting transfers between devices, per_device(): lax.ppermute(edge, 'stream', [(i, (i + 1) % stream) for i in range(stream)])  5.48 us
    pallas_call x5, Pallas kernels, call(): pl.pallas_call(kernel, out_shape=[jax.ShapeDtypeStruct(shape, jnp.float32...  3.58 us
    unnamed x14, local copies, waits for them, and re-layouts  2.68 us
  transfers between devices with their start and end apart: 1, of which 1 were waited for; matrix products, arithmetic and copies ran while one was open for 0% of the time, Pallas kernels for 1%

profile of v4, /device:TPU:1, one launch (start us, length us, event | category | flops | bytes accessed | tf_op | source)
XLA Modules:
  0.0 75.6 jit_solution(11925320483919833264)
XLA Ops:
  0.0 0.0 copy-start.1
  0.0 0.8 %slice_bitcast_fusion.1 = (f32[1,8,512]{2,1,0:T(8,128)S(1)}, f32[1,8,512]{2,1,0:T(8,128)S(1)}) fusion(f32[2,8,8,512]{3,2,1,0:T(8,128)} %conc.3), kind=kLoop, calls=%fused_computation.4 | loop fusion | bytes 65536 | tf_op jit(solution)/shard_map/stack;squeeze | solution.py:115
  0.8 0.7 bitcast_add_fusion.1
  1.5 5.5 %collective-permute-start = (f32[4,8,512]{2,1,0:T(8,128)S(1)}, f32[4,8,512]{2,1,0:T(8,128)S(1)}, u32[]{:S(2)}, u32[]{:S(2)}) collective-permute-start(f32[4,8,512]{2,1,0:T(8,128)S(1)} %pad_maximum_fusion), channel_id=1, source_target_pairs={{0,1},{1,2},{2,3},{3,4},{4,5},{5,6},{6,7},{7,8},{8,9},{9,10},{10,1... | collective-permute-start | bytes 196616 | tf_op jit(solution)/shard_map/ppermute | solution.py:335
  7.0 0.0 copy-done.1
  7.0 0.0 copy-start
  7.1 1.0 %copy-done = f32[3,8,8,512]{3,2,1,0:T(8,128)S(1)} copy-done((f32[3,8,8,512]{3,2,1,0:T(8,128)S(1)}, f32[3,8,8,512]{3,2,1,0:T(8,128)}, u32[]{:S(2)}) %copy-start) | copy-done | bytes 393240
  8.0 0.0 copy-start.2
  8.0 0.9 %copy-done.2 = f32[8,8,512]{2,1,0:T(8,128)S(1)} copy-done((f32[8,8,512]{2,1,0:T(8,128)S(1)}, f32[8,8,512]{2,1,0:T(8,128)}, u32[]{:S(2)}) %copy-start.2) | copy-done | bytes 131096
  8.9 0.0 copy-start.6
  9.0 0.8 copy-done.6
  9.7 0.6 shard_map.73
  10.3 7.3 %collective-permute-done.left_halo = f32[4,8,512]{2,1,0:T(8,128)S(1)} collective-permute-done((f32[4,8,512]{2,1,0:T(8,128)S(1)}, f32[4,8,512]{2,1,0:T(8,128)S(1)}, u32[]{:S(2)}, u32[]{:S(2)}) %collective-permute-start) | collective-permute-done | bytes 65568 | tf_op jit(solution)/shard_map/ppermute | solution.py:335
  17.6 0.2 shard_map.74
  17.8 0.0 copy-start.3
  17.8 0.0 copy-start.5
  17.8 16.3 %all_to_all.15.parts = f32[64,8,128]{2,1,0:T(8,128)S(1)} all-to-all(f32[64,8,128]{2,1,0:T(8,128)S(1)} %get-tuple-element.14), channel_id=1, replica_groups={{0,32,64,96,128,160,192,224,256,288,320,352,384,416,448,480,1,33,65,97,..., dimensions={0} | all-to-all | bytes 524288 | tf_op jit(solution)/shard_map/all_to_all | solution.py:355
  34.1 0.0 copy-done.3
  34.1 0.0 copy-done.5
  34.1 1.5 %shard_map.75 = (f32[64,8,128]{2,1,0:T(8,128)S(1)}, f32[8,4,8,128]{3,2,1,0:T(8,128)S(1)}) custom-call(f32[64,8,128]{2,1,0:T(8,128)S(1)} %all_to_all.15.parts, f32[256,128]{1,0:T(8,128)S(1)} %copy-done.5, f32[384,128]{1,0:T(8,128)S(1)} %copy-done.3), custom_call_target="tpu_custom_call" | custom-call | tf_op jit(solution)/shard_map/pallas_call | solution.py:95
  35.6 22.6 %all_to_all.16.sums = f32[8,4,8,128]{3,2,1,0:T(8,128)S(1)} all-to-all(f32[8,4,8,128]{3,2,1,0:T(8,128)S(1)} %get-tuple-element.16), channel_id=1, replica_groups={{0,4,8,12,16,20,24,28},{1,5,9,13,17,21,25,29},{2,6,10,14,18,22,26,30},{..., dimensions={0} | all-to-all | bytes 262144 | tf_op jit(solution)/shard_map/all_to_all | solution.py:363
  58.2 0.2 shard_map.76
  58.4 0.0 copy-start.4
  58.4 16.1 %all_to_all.17.links = f32[64,4,128]{2,1,0:T(4,128)S(1)} all-to-all(f32[64,4,128]{2,1,0:T(4,128)S(1)} %shard_map.76), channel_id=1, replica_groups={{0,32,64,96,128,160,192,224,256,288,320,352,384,416,448,480,1,33,65,97,..., dimensions={0} | all-to-all | bytes 262144 | tf_op jit(solution)/shard_map/all_to_all | solution.py:369
  74.5 0.0 copy-done.4
  74.5 1.0 %shard_map.77 = f32[2,8,8,512]{3,2,1,0:T(8,128)} custom-call(f32[128,512]{1,0:T(8,128)S(1)} %get-tuple-element.13.cells, f32[64,4,128]{2,1,0:T(4,128)S(1)} %all_to_all.17.links, f32[128,192]{1,0:T(8,128)S(1)} %copy-done.4), custom_call_target="tpu_custom_call" | custom-call | tf_op jit(solution)/shard_map/pallas_call | solution.py:95
  (1 shorter events, 0.0 us)
Async XLA Ops:
  0.0 7.0 %copy-start.1 = (f32[2,8,8,512]{3,2,1,0:T(8,128)S(1)}, f32[2,8,8,512]{3,2,1,0:T(8,128)}, u32[]{:S(2)}) copy-start(f32[2,8,8,512]{3,2,1,0:T(8,128)} %conc.3) | copy-start | bytes 786436
  1.5 16.1 %collective-permute-start = (f32[4,8,512]{2,1,0:T(8,128)S(1)}, f32[4,8,512]{2,1,0:T(8,128)S(1)}, u32[]{:S(2)}, u32[]{:S(2)}) collective-permute-start(f32[4,8,512]{2,1,0:T(8,128)S(1)} %pad_maximum_fusion), channel_id=1, source_target_pairs={{0,1},{1,2},{2,3},{3,4},{4,5},{5,6},{6,7},{7,8},{8,9},{9,10},{10,1... | collective-permute-start | bytes 196616 | tf_op jit(solution)/shard_map/ppermute | solution.py:335
  7.0 1.0 %copy-start = (f32[3,8,8,512]{3,2,1,0:T(8,128)S(1)}, f32[3,8,8,512]{3,2,1,0:T(8,128)}, u32[]{:S(2)}) copy-start(f32[3,8,8,512]{3,2,1,0:T(8,128)} %vel.3) | copy-start | bytes 1179652
  8.0 0.9 %copy-start.2 = (f32[8,8,512]{2,1,0:T(8,128)S(1)}, f32[8,8,512]{2,1,0:T(8,128)}, u32[]{:S(2)}) copy-start(f32[8,8,512]{2,1,0:T(8,128)} %volt.3) | copy-start | bytes 393220
  8.9 0.8 %copy-start.6 = (f32[64,128]{1,0:T(8,128)S(1)}, f32[64,128]{1,0:T(8,128)}, u32[]{:S(2)}) copy-start(f32[64,128]{1,0:T(8,128)} %constant.12.clone.collect) | copy-start | bytes 98308
  17.8 16.3 %copy-start.3 = (f32[384,128]{1,0:T(8,128)S(1)}, f32[384,128]{1,0:T(8,128)}, u32[]{:S(2)}) copy-start(f32[384,128]{1,0:T(8,128)} %constant.14.clone.solve) | copy-start | bytes 589828
  17.8 16.3 %copy-start.5 = (f32[256,128]{1,0:T(8,128)S(1)}, f32[256,128]{1,0:T(8,128)}, u32[]{:S(2)}) copy-start(f32[256,128]{1,0:T(8,128)} %constant.13.clone.collect) | copy-start | bytes 393220
  58.4 16.1 %copy-start.4 = (f32[128,192]{1,0:T(8,128)S(1)}, f32[128,192]{1,0:T(8,128)}, u32[]{:S(2)}) copy-start(f32[128,192]{1,0:T(8,128)} %constant.15.clone.table) | copy-start | bytes 294916

commit v5 on v4

--- a/solution.py
+++ b/solution.py
@@ -46,16 +46,17 @@
 
 def wall_tables(rates_x, rates_z, width, depth):
     unit = LANES // 4
-    collect = np.zeros((2, LANES, 2, 2, unit))
-    solve = np.zeros((3, LANES, LANES))
-    sums_in = collect[0, : 4 * depth].reshape(2, 2, depth, 2, 2, unit)
-    ends_in = collect[0, 4 * depth : 4 * (depth + width)].reshape(2, 2, width, 2, 2, unit)
-    flux_in = collect[1, : 4 * width].reshape(2, 2, width, 2, 2, unit)
+    sums = 4 * (depth + width)
+    collect = np.zeros((LANES, 2, 2, unit))
+    solve = np.zeros((2, LANES, LANES))
+    sums_in = collect[: 4 * depth].reshape(2, 2, depth, 2, 2, unit)
+    ends_in = collect[4 * depth : sums].reshape(2, 2, width, 2, 2, unit)
+    flux_in = collect[sums : sums + 4 * width].reshape(2, 2, width, 2, 2, unit)
     near = solve[0, : 4 * depth, : 4 * depth].reshape(2, 2, depth, 2, 2, depth)
     spread = solve[1, :, : 4 * depth].reshape(2, 2, unit, 2, 2, depth)
-    moved = solve[1, :, 4 * depth : 4 * (depth + width)].reshape(2, 2, unit, 2, 2, width)
-    flux_near = solve[2, : 4 * width, : 4 * depth].reshape(2, 2, width, 2, 2, depth)
-    flux_moved = solve[2, : 4 * width, 4 * depth : 4 * (depth + width)].reshape(2, 2, width, 2, 2, width)
+    moved = solve[1, :, 4 * depth : sums].reshape(2, 2, unit, 2, 2, width)
+    flux_near = solve[0, sums : sums + 4 * width, : 4 * depth].reshape(2, 2, width, 2, 2, depth)
+    flux_moved = solve[0, sums : sums + 4 * width, 4 * depth : sums].reshape(2, 2, width, 2, 2, width)
     for s in range(2):
         _, gather_x, _ = block_tables(*line_factors(rates_x[s]), width)
         local, gather_z, hand = block_tables(*line_factors(rates_z[s]), depth)
@@ -74,10 +75,10 @@
                 for side in range(2):
                     flux_in[end, s, x, :, s, width + side] = size * gather_x[x, side] * gather_z[cell]
                     flux_near[end, s, x, side, s, :] = size * gather_x[x, side] * local[cell]
-    return collect.reshape(2 * LANES, LANES), solve.reshape(3 * LANES, LANES)
-
-
-def home_table(rates_x, rates_z, width, depth):
+    return collect.reshape(LANES, LANES), solve.reshape(2 * LANES, LANES)
+
+
+def home_tables(rates_x, rates_z, width, depth):
     cells = 2 * width * depth
     near = np.zeros((2, width, depth, 2, width, depth))
     stream_spread = np.zeros((2, width, depth, 2, 2, depth))
@@ -88,18 +89,19 @@
         near[s, :, :, s, :, :] = np.einsum("xa,zb->xzab", local_x, local_z)
         stream_spread[s, :, :, :, s, :] = np.einsum("ex,zb->xzeb", hand_x, np.eye(depth))
         wall_spread[s, :, :, :, s, :] = np.einsum("xa,ez->xzea", local_x, hand_z)
-    return np.concatenate([part.reshape(cells, -1) for part in (near, stream_spread, wall_spread)], axis=1)
-
-
-def call(kernel, outs, ins, scratch=(), aliases=None):
+    parts = (near[:, :, :, :, 0], stream_spread, wall_spread)
+    return near.reshape(cells, cells), np.concatenate([part.reshape(cells, -1) for part in parts], axis=1)
+
+
+def call(kernel, outs, ins, scratch=(), aliases=None, source=pltpu.VMEM, target=pltpu.VMEM, room=32 * 1024):
     return pl.pallas_call(
         kernel,
         out_shape=[jax.ShapeDtypeStruct(shape, jnp.float32) for shape in outs],
-        in_specs=[pl.BlockSpec(memory_space=pltpu.VMEM)] * len(ins),
-        out_specs=[pl.BlockSpec(memory_space=pltpu.VMEM)] * len(outs),
+        in_specs=[pl.BlockSpec(memory_space=source)] * len(ins),
+        out_specs=[pl.BlockSpec(memory_space=target)] * len(outs),
         scratch_shapes=list(scratch),
         input_output_aliases=aliases or {},
-        compiler_params=pltpu.CompilerParams(vmem_limit_bytes=32 * 1024 * 1024),
+        compiler_params=pltpu.CompilerParams(vmem_limit_bytes=room * 1024),
     )(*ins)
 
 
@@ -111,8 +113,16 @@
     return (conc_low + conc_high) * (speed_low + speed_high - drift(volt_high - volt_low, species))
 
 
-def last_layers(conc, vel, volt):
-    return jnp.stack([conc[0, -1], conc[1, -1], vel[0, -1] + drift(volt[-1], 0), vel[0, -1] + drift(volt[-1], 1)])
+def border_kernel(conc, vel, volt, edge, arrived):
+    last = volt.shape[0] - 1
+    copies = [
+        pltpu.make_async_copy(source, edge.at[place], arrived.at[place])
+        for place, source in enumerate((conc.at[0, last], conc.at[1, last], vel.at[0, last], volt.at[last]))
+    ]
+    for copy in copies:
+        copy.start()
+    for copy in copies:
+        copy.wait()
 
 
 def split(values):
@@ -120,14 +130,32 @@
     return high, (values - high.astype(jnp.float32)).astype(jnp.bfloat16)
 
 
-def product(left, right):
-    left_high, left_low = split(left)
-    right_high, right_low = split(right)
+def product(values, table):
+    high, low = split(values)
+    table_high, table_low = split(table)
     dot = functools.partial(jnp.dot, preferred_element_type=jnp.float32)
-    return dot(left_high, right_high) + (dot(left_low, right_high) + dot(left_high, right_low))
-
-
-def predict_kernel(conc, vel, volt, collect, cells, rows):
+    wide = table.shape[1]
+    beside = jnp.concatenate([table_high, table_low], axis=1)
+    if values.shape[1] <= LANES:
+        under = jnp.concatenate([table_high, jnp.zeros_like(table_low)], axis=1)
+        both = dot(jnp.concatenate([high, low], axis=1), jnp.concatenate([beside, under], axis=0))
+        return both[:, :wide] + both[:, wide:]
+    both = dot(high, beside)
+    return both[:, :wide] + (both[:, wide:] + dot(low, table_high))
+
+
+def left_product(table, values):
+    high, low = split(values)
+    table_high, table_low = split(table)
+    dot = functools.partial(jnp.dot, preferred_element_type=jnp.float32)
+    tall = table.shape[0]
+    above = jnp.concatenate([table_high, table_low], axis=0)
+    under = jnp.concatenate([table_high, jnp.zeros_like(table_low)], axis=0)
+    both = dot(jnp.concatenate([above, under], axis=1), jnp.concatenate([high, low], axis=0))
+    return both[:tall] + both[tall:]
+
+
+def predict_kernel(conc, vel, volt, table, near, rows, cells):
     width, depth, span = volt.shape
     row = lax.broadcasted_iota(jnp.int32, (depth, span), 0)
     left = [None, None]
@@ -159,19 +187,20 @@
             ):
                 line = sums + part * 2 * width + place
                 rows[line : line + 1] = edge
-    rows[:sums] = product(collect[...], cells[...])
-
-
-def enter_kernel(decays_x, decays_z, cells_in, rows_in, left_halo, conc, vel, volt, shares, cells, rows):
+    solved = left_product(table[...], cells[...])
+    near[...] = solved[: cells.shape[0]]
+    rows[:sums] = solved[cells.shape[0] :]
+
+
+def enter_kernel(decays_x, decays_z, rows_in, left_halo, conc, vel, volt, shares, gains, rows):
     width, depth, span = volt.shape
     row = lax.broadcasted_iota(jnp.int32, (depth, span), 0)
     for s in range(2):
         decay = decays_x[s]
-        flux = (left_halo[s] + conc[s, 0]) * (left_halo[2 + s] + (vel[0, 0] - drift(volt[0], s)))
+        flux = face(left_halo[s], conc[s, 0], left_halo[2], vel[0, 0], left_halo[3], volt[0], s)
         taken = -FLUX_SCALE * flux
         gained = (decay - 1.0) * taken
-        start = s * width * depth
-        cells[start : start + depth] = cells_in[start : start + depth] + gained
+        gains[s * depth : (s + 1) * depth] = gained
         for side, scale in enumerate((decay ** (width - 1) * (decay - 1.0), 1.0 / decay - 1.0)):
             start = (side * 2 + s) * depth
             rows[start : start + depth] = rows_in[start : start + depth] + scale * taken
@@ -189,31 +218,34 @@
             shares[start + k, half * part : (half + 1) * part] = turned[k * part : (k + 1) * part]
 
 
+def member_shift(team, teams):
+    return lax.div(team, teams // 2) * (TEAM // 2)
+
+
 def by_lane(values, lane, unit):
-    return jnp.where(lax.rem(lax.div(lane, unit), 2) == 0, values[0], values[1])
-
-
-def wall_kernel(decays, stream_steps, blocks, width, depth, parts, collect, solve, ends, sums, carry, fluxes):
+    return jnp.where(lax.bitwise_and(lane, unit) == 0, values[0], values[1])
+
+
+def wall_kernel(decays, stream_steps, blocks, width, depth, parts, collect, solve, ends, sums, carry, lines):
     members, places, _ = parts.shape
     flat = members * places
     lane = lax.broadcasted_iota(jnp.int32, (places, LANES), 1)
     faces = 2 * width
     first = LANES // 2
     for m in range(TEAM):
-        line = m * blocks
-        below = pltpu.roll(parts[line], LANES - first - 2 * faces, 1)
+        below = pltpu.roll(parts[m * blocks], LANES - 2 * faces, 1)
         below = below * pltpu.roll(below, LANES - faces, 1)
         for b in range(blocks):
-            meet = pltpu.roll(parts[line + b], LANES - first, 1)
+            own = parts[m * blocks + b]
+            meet = own
             if b + 1 < blocks:
-                meet = meet + pltpu.roll(parts[line + b + 1], LANES - first - 2 * faces, 1)
+                meet = meet + pltpu.roll(parts[m * blocks + b + 1], LANES - 2 * faces, 1)
             above = meet * pltpu.roll(meet, LANES - faces, 1)
-            both = jnp.where(lane < faces, above, pltpu.roll(below, faces, 1))
-            fluxes[line + b] = jnp.where(lane < 2 * faces, both, 0.0)
+            both = jnp.where(lane < first + faces, above, pltpu.roll(below, faces, 1))
+            lines[m * blocks + b] = jnp.where(lane < first, own, both)
             below = above
-    value = parts[...].reshape(flat, LANES)
-    flux = fluxes[...].reshape(flat, LANES)
-    carry[...] = product(jnp.concatenate([value, flux], axis=1), collect[...]).reshape(members, places, LANES)
+    value = lines[...].reshape(flat, LANES)
+    carry[...] = product(value, collect[...]).reshape(members, places, LANES)
     side = LANES // 2
     unit = LANES // 4
     entering = lane < side
@@ -244,20 +276,23 @@
         mirrored = scale * (pltpu.roll(total, side, 1) - mirror * total)
         for b in range(blocks):
             carry[m * blocks + b] = jnp.where(entering, befores[b], afters[b]) + weights[b] * mirrored
-    full = jnp.concatenate([value, carry[...].reshape(flat, LANES), flux], axis=1)
+    full = jnp.concatenate([value, carry[...].reshape(flat, LANES)], axis=1)
     ends[...] = product(full, solve[...]).reshape(members, places, LANES)
     step = by_lane(stream_steps, lane, depth)
     entering = lane < 2 * depth
     pack = LANES // (4 * depth)
+    shift = member_shift(lax.div(lax.axis_index("stream"), TEAM), sums.shape[0])
+    first = [lax.rem(shift + m, TEAM) * blocks for m in range(TEAM)]
     for group in range(blocks // pack):
         packed = None
         for part in range(pack):
             b = group * pack + part
-            before = ends[b]
-            after = ends[(TEAM - 1) * blocks + b]
+            own = [ends[first[m] + b] for m in range(TEAM)]
+            before = own[0]
+            after = own[-1]
             for m in range(1, TEAM):
-                before = step * before + ends[m * blocks + b]
-                after = step * after + ends[(TEAM - 1 - m) * blocks + b]
+                before = step * before + own[m]
+                after = step * after + own[TEAM - 1 - m]
             both = jnp.where(entering, before, jnp.where(lane < 4 * depth, after, 0.0))
             packed = packed + pltpu.roll(both, part * 4 * depth, 1) if part else both
         for team in range(sums.shape[0]):
@@ -270,8 +305,10 @@
     pack = blocks // groups
     part = links.shape[1]
     team = lax.div(lax.axis_index("stream"), TEAM)
+    shift = member_shift(team, teams)
+    first = [lax.rem(shift + m, TEAM) * blocks for m in range(TEAM)]
     lane = lax.broadcasted_iota(jnp.int32, (places, LANES), 1)
-    entering = lax.rem(lane, 4 * depth) < 2 * depth
+    entering = lax.bitwise_and(lane, 2 * depth) == 0
     step = by_lane(steps, lane, depth)
     leap = by_lane([value**TEAM for value in steps], lane, depth)
     closing = by_lane([1.0 / (1.0 - value ** (TEAM * teams)) for value in steps], lane, depth)
@@ -289,16 +326,16 @@
             afters = [None] * TEAM
             for m in range(TEAM - 1, -1, -1):
                 afters[m] = after
-                after = step * after + ends[m * blocks + b]
+                after = step * after + ends[first[m] + b]
             for m in range(TEAM):
-                own = ends[m * blocks + b]
+                own = ends[first[m] + b]
                 carry = jnp.where(lane < 4 * depth, jnp.where(entering, before, afters[m]), own)
                 before = step * before + own
                 halved = carry + pltpu.roll(pltpu.roll(carry, LANES // HALVES, 1), part, 0)
-                links[m * blocks + b] = halved[:part]
-
-
-def home_kernel(cells, links, table, out, rows, carry):
+                links[first[m] + b] = halved[:part]
+
+
+def home_kernel(near, gains, links, table, out, rows, carry, result, sent):
     _, width, depth, span = out.shape
     part = links.shape[1]
     lanes = LANES // HALVES
@@ -309,11 +346,19 @@
         for half in range(HALVES):
             start = half * (span // HALVES) + chunk * LANES
             carry[:, start : start + LANES] = turned[half * lanes : (half + 1) * lanes]
-    result = product(table[...], jnp.concatenate([cells[...], carry[...]], axis=0))
-    for s in range(2):
-        for x in range(width):
-            start = (s * width + x) * depth
-            out[s, x] = result[start : start + depth]
+    copies = []
+    for half in range(HALVES):
+        cut = slice(half * (span // HALVES), (half + 1) * (span // HALVES))
+        added = left_product(table[...], jnp.concatenate([gains[:, cut], carry[:, cut]], axis=0))
+        solved = near[:, cut] + added
+        for s in range(2):
+            for x in range(width):
+                start = (s * width + x) * depth
+                result[half, s, x] = solved[start : start + depth]
+        copies.append(pltpu.make_async_copy(result.at[half], out.at[:, :, :, cut], sent.at[half]))
+        copies[-1].start()
+    for copy in copies:
+        copy.wait()
 
 
 def per_device(concentration, velocity, potential):
@@ -329,28 +374,39 @@
     steps_x = [decay**width for decay in decays_x]
     collect_z, solve_z = wall_tables(rates_x, rates_z, width, depth)
     collect = collect_table(rates_x, rates_z, width, depth)
-    home = home_table(rates_x, rates_z, width, depth)
-
-    edge = last_layers(concentration, velocity, potential)
+    near, home = home_tables(rates_x, rates_z, width, depth)
+
+    (edge,) = call(
+        border_kernel,
+        [(4, depth, span)],
+        (concentration, velocity, potential),
+        [pltpu.SemaphoreType.DMA((4,))],
+        source=pltpu.HBM,
+        room=53 * 1024 + 848,
+    )
     left_halo = lax.ppermute(edge, "stream", [(i, (i + 1) % stream) for i in range(stream)])
 
     members = TEAM * wall
     teams = stream // TEAM
-    plane = [[b * stream + t * TEAM + m for m in range(TEAM) for b in range(wall)] for t in range(teams)]
-    ranks = [[t * TEAM + m for t in range(teams)] for m in range(TEAM)]
+    holders = [[t * TEAM + (m + t // (teams // 2) * (TEAM // 2)) % TEAM for m in range(TEAM)] for t in range(teams)]
+    plane = [[b * stream + place for place in team for b in range(wall)] for team in holders]
+    ranks = [[team[m] for team in holders] for m in range(TEAM)]
     swap = functools.partial(lax.all_to_all, split_axis=0, concat_axis=0, tiled=True)
     table = functools.partial(jnp.array, dtype=jnp.float32)
     places = span // members
     tile = (members, places, LANES)
     flat = (2 * width * depth, span)
-    cells, rows = call(
-        predict_kernel, [flat, (LANES, span)], (concentration, velocity, potential, table(collect))
-    )
-    shares, cells, rows = call(
+    near, rows = call(
+        predict_kernel,
+        [flat, (LANES, span)],
+        (concentration, velocity, potential, table(np.concatenate([near, collect]))),
+        [pltpu.VMEM(flat, jnp.float32)],
+    )
+    shares, gains, rows = call(
         functools.partial(enter_kernel, decays_x, decays_z),
-        [tile, flat, (LANES, span)],
-        (cells, rows, left_halo, concentration, velocity, potential),
-        aliases={0: 1, 1: 2},
+        [tile, (2 * depth, span), (LANES, span)],
+        (rows, left_halo, concentration, velocity, potential),
+        aliases={0: 2},
     )
     parts = swap(shares, ("wall", "stream"), axis_index_groups=plane)
     pack = LANES // (4 * depth)
@@ -370,8 +426,14 @@
     (out,) = call(
         home_kernel,
         [concentration.shape],
-        (cells, links, table(home)),
-        [pltpu.VMEM((span // HALVES, LANES), jnp.float32), pltpu.VMEM((LANES // HALVES, span), jnp.float32)],
+        (near, gains, links, table(home)),
+        [
+            pltpu.VMEM((span // HALVES, LANES), jnp.float32),
+            pltpu.VMEM((LANES // HALVES, span), jnp.float32),
+            pltpu.VMEM((HALVES, 2, width, depth, span // HALVES), jnp.float32),
+            pltpu.SemaphoreType.DMA((HALVES,)),
+        ],
+        target=pltpu.HBM,
     )
     return out
 

time: 76.1 us -> 74 us (0.972)
  local copies, waits for them, and re-layouts: 3.47 us -> 0.92 us
  waiting for transfers between devices: 7.27 us -> 8.97 us
  blocking collectives: 55 us -> 54.2 us
    all_to_all x1, blocking collectives: 16.1 us -> 13.7 us  [per_device(): links = swap(links, ('wall', 'stream'), axis_index_groups=plane)]
    unnamed x14, local copies, waits for them, and re-layouts: 2.68 us -> 0.92 us
    ppermute x1, waiting for transfers between devices: 7.27 us -> 8.97 us  [per_device(): lax.ppermute(edge, 'stream', [(i, (i + 1) % stream) for i in range(stream)])]
    all_to_all x1, blocking collectives: 22.6 us -> 24.2 us  [per_device(): sums = swap(sums, 'stream', axis_index_groups=ranks)]
    another operation x1 -> x0, local copies, waits for them, and re-layouts: 0.79 us -> none  [last_layers(): jnp.stack([conc[0, -1], conc[1, -1], vel[0, -1] + drift(volt[-1], 0), vel...]
    pallas_call x5 -> x6, Pallas kernels: 3.58 us -> 3.94 us  [call(): pl.pallas_call(kernel, out_shape=[jax.ShapeDtypeStruct(shape, jnp.float32...]
where the time goes in v5:
time: 74 us; the launch traced here: 73.6 us
  blocking collectives  54.2 us (73%)
  waiting for transfers between devices  8.97 us (12%)
  starting transfers between devices  5.48 us (7%)
  Pallas kernels  3.94 us (5%)
  local copies, waits for them, and re-layouts  0.92 us (1%)
    all_to_all x1, blocking collectives, per_device(): sums = swap(sums, 'stream', axis_index_groups=ranks)  24.2 us
    all_to_all x1, blocking collectives, per_device(): parts = swap(shares, ('wall', 'stream'), axis_index_groups=plane)  16.3 us
    all_to_all x1, blocking collectives, per_device(): links = swap(links, ('wall', 'stream'), axis_index_groups=plane)  13.7 us
    ppermute x1, waiting for transfers between devices, per_device(): lax.ppermute(edge, 'stream', [(i, (i + 1) % stream) for i in range(stream)])  8.97 us
    ppermute x1, starting transfers between devices, per_device(): lax.ppermute(edge, 'stream', [(i, (i + 1) % stream) for i in range(stream)])  5.48 us
    pallas_call x6, Pallas kernels, call(): pl.pallas_call(kernel, out_shape=[jax.ShapeDtypeStruct(shape, jnp.float32...  3.94 us
  transfers between devices with their start and end apart: 1, of which 1 were waited for; matrix products, arithmetic and copies ran while one was open for 0% of the time, Pallas kernels for 1%

profile of v5, /device:TPU:1, one launch (start us, length us, event | category | flops | bytes accessed | tf_op | source)
XLA Modules:
  0.0 73.6 jit_solution(17568637270318134981)
XLA Ops:
  0.0 0.0 copy-start.2
  0.0 0.0 copy-start
  0.0 0.0 copy-start.1
  0.0 0.9 %shard_map.74 = f32[4,8,512]{2,1,0:T(8,128)S(1)} custom-call(f32[2,8,8,512]{3,2,1,0:T(8,128)} %conc.5, f32[3,8,8,512]{3,2,1,0:T(8,128)} %vel.5, f32[8,8,512]{2,1,0:T(8,128)} %volt.5), custom_call_target="tpu_custom_call" | custom-call | tf_op jit(solution)/shard_map/pallas_call | solution.py:97
  0.9 5.5 %collective-permute-start = (f32[4,8,512]{2,1,0:T(8,128)S(1)}, f32[4,8,512]{2,1,0:T(8,128)S(1)}, u32[]{:S(2)}, u32[]{:S(2)}) collective-permute-start(f32[4,8,512]{2,1,0:T(8,128)S(1)} %shard_map.74), channel_id=1, source_target_pairs={{0,1},{1,2},{2,3},{3,4},{4,5},{5,6},{6,7},{7,8},{8,9},{9,10},{10,1... | collective-permute-start | bytes 196616 | tf_op jit(solution)/shard_map/ppermute | solution.py:387
  6.4 0.0 copy-done.2
  6.4 0.0 copy-done
  6.4 0.0 copy-done.1
  6.4 0.0 copy-start.4
  6.4 0.9 %copy-done.4 = f32[192,128]{1,0:T(8,128)S(1)} copy-done((f32[192,128]{1,0:T(8,128)S(1)}, f32[192,128]{1,0:T(8,128)}, u32[]{:S(2)}) %copy-start.4) | copy-done | bytes 98328
  7.3 0.7 shard_map.73
  8.0 9.0 %collective-permute-done.left_halo = f32[4,8,512]{2,1,0:T(8,128)S(1)} collective-permute-done((f32[4,8,512]{2,1,0:T(8,128)S(1)}, f32[4,8,512]{2,1,0:T(8,128)S(1)}, u32[]{:S(2)}, u32[]{:S(2)}) %collective-permute-start) | collective-permute-done | bytes 65568 | tf_op jit(solution)/shard_map/ppermute | solution.py:387
  17.0 0.2 shard_map.75
  17.1 0.0 copy-start.3
  17.1 0.0 copy-start.6
  17.2 16.3 %all_to_all.15.parts = f32[64,8,128]{2,1,0:T(8,128)S(1)} all-to-all(f32[64,8,128]{2,1,0:T(8,128)S(1)} %get-tuple-element.14), channel_id=1, replica_groups={{0,32,64,96,128,160,192,224,256,288,320,352,384,416,448,480,1,33,65,97,..., dimensions={0} | all-to-all | bytes 524288 | tf_op jit(solution)/shard_map/all_to_all | solution.py:411
  33.4 0.0 copy-done.3
  33.4 0.0 copy-done.6
  33.4 1.0 %shard_map.76 = (f32[64,8,128]{2,1,0:T(8,128)S(1)}, f32[8,4,8,128]{3,2,1,0:T(8,128)S(1)}) custom-call(f32[64,8,128]{2,1,0:T(8,128)S(1)} %all_to_all.15.parts, f32[128,128]{1,0:T(8,128)S(1)} %copy-done.6, f32[256,128]{1,0:T(8,128)S(1)} %copy-done.3), custom_call_target="tpu_custom_call" | custom-call | tf_op jit(solution)/shard_map/pallas_call | solution.py:97
  34.4 24.2 %all_to_all.16.sums = f32[8,4,8,128]{3,2,1,0:T(8,128)S(1)} all-to-all(f32[8,4,8,128]{3,2,1,0:T(8,128)S(1)} %get-tuple-element.16), channel_id=1, replica_groups={{0,4,8,12,18,22,26,30},{1,5,9,13,19,23,27,31},{2,6,10,14,16,20,24,28},{..., dimensions={0} | all-to-all | bytes 262144 | tf_op jit(solution)/shard_map/all_to_all | solution.py:419
  58.6 0.2 shard_map.77
  58.9 0.0 copy-start.5
  58.9 13.7 %all_to_all.17.links = f32[64,4,128]{2,1,0:T(4,128)S(1)} all-to-all(f32[64,4,128]{2,1,0:T(4,128)S(1)} %shard_map.77), channel_id=1, replica_groups={{0,32,64,96,128,160,192,224,256,288,320,352,384,416,448,480,1,33,65,97,..., dimensions={0} | all-to-all | bytes 262144 | tf_op jit(solution)/shard_map/all_to_all | solution.py:425
  72.6 0.0 copy-done.5
  72.6 1.0 %shard_map.78 = f32[2,8,8,512]{3,2,1,0:T(8,128)} custom-call(f32[128,512]{1,0:T(8,128)S(1)} %get-tuple-element.11.near, f32[16,512]{1,0:T(8,128)S(1)} %get-tuple-element.13.gains, f32[64,4,128]{2,1,0:T(4,128)S(1)} %all_to_all.17.links, f32[128,80]{1,0:T(8,128)S(1)} %copy-done.5), custom_call_target="tpu_custom_call" | custom-call | tf_op jit(solution)/shard_map/pallas_call | solution.py:97
Async XLA Ops:
  0.0 6.4 %copy-start.2 = (f32[8,8,512]{2,1,0:T(8,128)S(1)}, f32[8,8,512]{2,1,0:T(8,128)}, u32[]{:S(2)}) copy-start(f32[8,8,512]{2,1,0:T(8,128)} %volt.5) | copy-start | bytes 393220
  0.0 6.4 %copy-start = (f32[3,8,8,512]{3,2,1,0:T(8,128)S(1)}, f32[3,8,8,512]{3,2,1,0:T(8,128)}, u32[]{:S(2)}) copy-start(f32[3,8,8,512]{3,2,1,0:T(8,128)} %vel.5) | copy-start | bytes 1179652
  0.0 6.4 %copy-start.1 = (f32[2,8,8,512]{3,2,1,0:T(8,128)S(1)}, f32[2,8,8,512]{3,2,1,0:T(8,128)}, u32[]{:S(2)}) copy-start(f32[2,8,8,512]{3,2,1,0:T(8,128)} %conc.5) | copy-start | bytes 786436
  0.9 16.1 %collective-permute-start = (f32[4,8,512]{2,1,0:T(8,128)S(1)}, f32[4,8,512]{2,1,0:T(8,128)S(1)}, u32[]{:S(2)}, u32[]{:S(2)}) collective-permute-start(f32[4,8,512]{2,1,0:T(8,128)S(1)} %shard_map.74), channel_id=1, source_target_pairs={{0,1},{1,2},{2,3},{3,4},{4,5},{5,6},{6,7},{7,8},{8,9},{9,10},{10,1... | collective-permute-start | bytes 196616 | tf_op jit(solution)/shard_map/ppermute | solution.py:387
  6.4 0.9 %copy-start.4 = (f32[192,128]{1,0:T(8,128)S(1)}, f32[192,128]{1,0:T(8,128)}, u32[]{:S(2)}) copy-start(f32[192,128]{1,0:T(8,128)} %constant.8.clone.table) | copy-start | bytes 294916
  17.1 16.3 %copy-start.3 = (f32[256,128]{1,0:T(8,128)S(1)}, f32[256,128]{1,0:T(8,128)}, u32[]{:S(2)}) copy-start(f32[256,128]{1,0:T(8,128)} %constant.10.clone.solve) | copy-start | bytes 393220
  17.1 16.3 %copy-start.6 = (f32[128,128]{1,0:T(8,128)S(1)}, f32[128,128]{1,0:T(8,128)}, u32[]{:S(2)}) copy-start(f32[128,128]{1,0:T(8,128)} %constant.9.clone.collect) | copy-start | bytes 196612
  58.9 13.7 %copy-start.5 = (f32[128,80]{1,0:T(8,128)S(1)}, f32[128,80]{1,0:T(8,128)}, u32[]{:S(2)}) copy-start(f32[128,80]{1,0:T(8,128)} %constant.11.clone.table) | copy-start | bytes 122884

commit v6 on v5

--- a/solution.py
+++ b/solution.py
@@ -14,6 +14,7 @@
 TEAM = 4
 HALVES = 2
 LANES = 128
+SPREAD = 39
 
 
 def line_factors(rate):
@@ -222,6 +223,15 @@
     return lax.div(team, teams // 2) * (TEAM // 2)
 
 
+def list_place(member, block, blocks):
+    total = TEAM * blocks
+    return (member * blocks + block) * pow(SPREAD, -1, total) % total
+
+
+def shifted_place(member, block, blocks, shift):
+    return lax.rem(list_place(member, block, blocks) + shift * blocks, TEAM * blocks)
+
+
 def by_lane(values, lane, unit):
     return jnp.where(lax.bitwise_and(lane, unit) == 0, values[0], values[1])
 
@@ -233,16 +243,16 @@
     faces = 2 * width
     first = LANES // 2
     for m in range(TEAM):
-        below = pltpu.roll(parts[m * blocks], LANES - 2 * faces, 1)
+        below = pltpu.roll(parts[list_place(m, 0, blocks)], LANES - 2 * faces, 1)
         below = below * pltpu.roll(below, LANES - faces, 1)
         for b in range(blocks):
-            own = parts[m * blocks + b]
+            own = parts[list_place(m, b, blocks)]
             meet = own
             if b + 1 < blocks:
-                meet = meet + pltpu.roll(parts[m * blocks + b + 1], LANES - 2 * faces, 1)
+                meet = meet + pltpu.roll(parts[list_place(m, b + 1, blocks)], LANES - 2 * faces, 1)
             above = meet * pltpu.roll(meet, LANES - faces, 1)
             both = jnp.where(lane < first + faces, above, pltpu.roll(below, faces, 1))
-            lines[m * blocks + b] = jnp.where(lane < first, own, both)
+            lines[list_place(m, b, blocks)] = jnp.where(lane < first, own, both)
             below = above
     value = lines[...].reshape(flat, LANES)
     carry[...] = product(value, collect[...]).reshape(members, places, LANES)
@@ -268,26 +278,25 @@
         afters = [None] * blocks
         for b in range(blocks):
             befores.append(before)
-            before = step * before + carry[m * blocks + b]
+            before = step * before + carry[list_place(m, b, blocks)]
         for b in range(blocks - 1, -1, -1):
             afters[b] = after
-            after = step * after + carry[m * blocks + b]
+            after = step * after + carry[list_place(m, b, blocks)]
         total = jnp.where(entering, before, after)
         mirrored = scale * (pltpu.roll(total, side, 1) - mirror * total)
         for b in range(blocks):
-            carry[m * blocks + b] = jnp.where(entering, befores[b], afters[b]) + weights[b] * mirrored
+            carry[list_place(m, b, blocks)] = jnp.where(entering, befores[b], afters[b]) + weights[b] * mirrored
     full = jnp.concatenate([value, carry[...].reshape(flat, LANES)], axis=1)
     ends[...] = product(full, solve[...]).reshape(members, places, LANES)
     step = by_lane(stream_steps, lane, depth)
     entering = lane < 2 * depth
     pack = LANES // (4 * depth)
     shift = member_shift(lax.div(lax.axis_index("stream"), TEAM), sums.shape[0])
-    first = [lax.rem(shift + m, TEAM) * blocks for m in range(TEAM)]
     for group in range(blocks // pack):
         packed = None
         for part in range(pack):
             b = group * pack + part
-            own = [ends[first[m] + b] for m in range(TEAM)]
+            own = [ends[shifted_place(m, b, blocks, shift)] for m in range(TEAM)]
             before = own[0]
             after = own[-1]
             for m in range(1, TEAM):
@@ -306,7 +315,6 @@
     part = links.shape[1]
     team = lax.div(lax.axis_index("stream"), TEAM)
     shift = member_shift(team, teams)
-    first = [lax.rem(shift + m, TEAM) * blocks for m in range(TEAM)]
     lane = lax.broadcasted_iota(jnp.int32, (places, LANES), 1)
     entering = lax.bitwise_and(lane, 2 * depth) == 0
     step = by_lane(steps, lane, depth)
@@ -326,13 +334,13 @@
             afters = [None] * TEAM
             for m in range(TEAM - 1, -1, -1):
                 afters[m] = after
-                after = step * after + ends[first[m] + b]
+                after = step * after + ends[shifted_place(m, b, blocks, shift)]
             for m in range(TEAM):
-                own = ends[first[m] + b]
+                own = ends[shifted_place(m, b, blocks, shift)]
                 carry = jnp.where(lane < 4 * depth, jnp.where(entering, before, afters[m]), own)
                 before = step * before + own
                 halved = carry + pltpu.roll(pltpu.roll(carry, LANES // HALVES, 1), part, 0)
-                links[first[m] + b] = halved[:part]
+                links[shifted_place(m, b, blocks, shift)] = halved[:part]
 
 
 def home_kernel(near, gains, links, table, out, rows, carry, result, sent):
@@ -389,7 +397,8 @@
     members = TEAM * wall
     teams = stream // TEAM
     holders = [[t * TEAM + (m + t // (teams // 2) * (TEAM // 2)) % TEAM for m in range(TEAM)] for t in range(teams)]
-    plane = [[b * stream + place for place in team for b in range(wall)] for team in holders]
+    listed = [[b * stream + place for place in team for b in range(wall)] for team in holders]
+    plane = [[team[k * SPREAD % members] for k in range(members)] for team in listed]
     ranks = [[team[m] for team in holders] for m in range(TEAM)]
     swap = functools.partial(lax.all_to_all, split_axis=0, concat_axis=0, tiled=True)
     table = functools.partial(jnp.array, dtype=jnp.float32)

time: 74 us -> 73.4 us (level)
    all_to_all x1, blocking collectives: 24.2 us -> 22.1 us  [per_device(): sums = swap(sums, 'stream', axis_index_groups=ranks)]
    all_to_all x1, blocking collectives: 13.7 us -> 15.6 us  [per_device(): links = swap(links, ('wall', 'stream'), axis_index_groups=plane)]
where the time goes in v6:
time: 73.4 us; the launch traced here: 73.1 us
  blocking collectives  53.7 us (73%)
  waiting for transfers between devices  8.97 us (12%)
  starting transfers between devices  5.48 us (7%)
  Pallas kernels  3.98 us (5%)
  local copies, waits for them, and re-layouts  0.92 us (1%)
    all_to_all x1, blocking collectives, per_device(): sums = swap(sums, 'stream', axis_index_groups=ranks)  22.1 us
    all_to_all x1, blocking collectives, per_device(): parts = swap(shares, ('wall', 'stream'), axis_index_groups=plane)  16 us
    all_to_all x1, blocking collectives, per_device(): links = swap(links, ('wall', 'stream'), axis_index_groups=plane)  15.6 us
    ppermute x1, waiting for transfers between devices, per_device(): lax.ppermute(edge, 'stream', [(i, (i + 1) % stream) for i in range(stream)])  8.97 us
    ppermute x1, starting transfers between devices, per_device(): lax.ppermute(edge, 'stream', [(i, (i + 1) % stream) for i in range(stream)])  5.48 us
    pallas_call x6, Pallas kernels, call(): pl.pallas_call(kernel, out_shape=[jax.ShapeDtypeStruct(shape, jnp.float32...  3.98 us
  transfers between devices with their start and end apart: 1, of which 1 were waited for; matrix products, arithmetic and copies ran while one was open for 0% of the time, Pallas kernels for 1%

profile of v6, /device:TPU:1, one launch (start us, length us, event | category | flops | bytes accessed | tf_op | source)
XLA Modules:
  0.0 73.1 jit_solution(6808081754688374579)
XLA Ops:
  0.0 0.0 copy-start.2
  0.0 0.0 copy-start
  0.0 0.0 copy-start.1
  0.0 0.9 %shard_map.74 = f32[4,8,512]{2,1,0:T(8,128)S(1)} custom-call(f32[2,8,8,512]{3,2,1,0:T(8,128)} %conc.5, f32[3,8,8,512]{3,2,1,0:T(8,128)} %vel.5, f32[8,8,512]{2,1,0:T(8,128)} %volt.5), custom_call_target="tpu_custom_call" | custom-call | tf_op jit(solution)/shard_map/pallas_call | solution.py:98
  0.9 5.5 %collective-permute-start = (f32[4,8,512]{2,1,0:T(8,128)S(1)}, f32[4,8,512]{2,1,0:T(8,128)S(1)}, u32[]{:S(2)}, u32[]{:S(2)}) collective-permute-start(f32[4,8,512]{2,1,0:T(8,128)S(1)} %shard_map.74), channel_id=1, source_target_pairs={{0,1},{1,2},{2,3},{3,4},{4,5},{5,6},{6,7},{7,8},{8,9},{9,10},{10,1... | collective-permute-start | bytes 196616 | tf_op jit(solution)/shard_map/ppermute | solution.py:395
  6.4 0.0 copy-done.2
  6.4 0.0 copy-done
  6.4 0.0 copy-done.1
  6.4 0.0 copy-start.4
  6.4 0.9 %copy-done.4 = f32[192,128]{1,0:T(8,128)S(1)} copy-done((f32[192,128]{1,0:T(8,128)S(1)}, f32[192,128]{1,0:T(8,128)}, u32[]{:S(2)}) %copy-start.4) | copy-done | bytes 98328
  7.3 0.7 shard_map.73
  8.0 9.0 %collective-permute-done.left_halo = f32[4,8,512]{2,1,0:T(8,128)S(1)} collective-permute-done((f32[4,8,512]{2,1,0:T(8,128)S(1)}, f32[4,8,512]{2,1,0:T(8,128)S(1)}, u32[]{:S(2)}, u32[]{:S(2)}) %collective-permute-start) | collective-permute-done | bytes 65568 | tf_op jit(solution)/shard_map/ppermute | solution.py:395
  17.0 0.2 shard_map.75
  17.1 0.0 copy-start.3
  17.1 0.0 copy-start.6
  17.2 16.0 %all_to_all.15.parts = f32[64,8,128]{2,1,0:T(8,128)S(1)} all-to-all(f32[64,8,128]{2,1,0:T(8,128)S(1)} %get-tuple-element.14), channel_id=1, replica_groups={{0,226,448,163,385,96,322,33,259,481,192,418,129,355,66,288,3,225,451,1..., dimensions={0} | all-to-all | bytes 524288 | tf_op jit(solution)/shard_map/all_to_all | solution.py:420
  33.2 0.0 copy-done.3
  33.2 0.0 copy-done.6
  33.2 1.0 %shard_map.76 = (f32[64,8,128]{2,1,0:T(8,128)S(1)}, f32[8,4,8,128]{3,2,1,0:T(8,128)S(1)}) custom-call(f32[64,8,128]{2,1,0:T(8,128)S(1)} %all_to_all.15.parts, f32[128,128]{1,0:T(8,128)S(1)} %copy-done.6, f32[256,128]{1,0:T(8,128)S(1)} %copy-done.3), custom_call_target="tpu_custom_call" | custom-call | tf_op jit(solution)/shard_map/pallas_call | solution.py:98
  34.1 22.1 %all_to_all.16.sums = f32[8,4,8,128]{3,2,1,0:T(8,128)S(1)} all-to-all(f32[8,4,8,128]{3,2,1,0:T(8,128)S(1)} %get-tuple-element.16), channel_id=1, replica_groups={{0,4,8,12,18,22,26,30},{1,5,9,13,19,23,27,31},{2,6,10,14,16,20,24,28},{..., dimensions={0} | all-to-all | bytes 262144 | tf_op jit(solution)/shard_map/all_to_all | solution.py:428
  56.2 0.3 shard_map.77
  56.5 0.0 copy-start.5
  56.5 15.6 %all_to_all.17.links = f32[64,4,128]{2,1,0:T(4,128)S(1)} all-to-all(f32[64,4,128]{2,1,0:T(4,128)S(1)} %shard_map.77), channel_id=1, replica_groups={{0,226,448,163,385,96,322,33,259,481,192,418,129,355,66,288,3,225,451,1..., dimensions={0} | all-to-all | bytes 262144 | tf_op jit(solution)/shard_map/all_to_all | solution.py:434
  72.1 0.0 copy-done.5
  72.1 1.0 %shard_map.78 = f32[2,8,8,512]{3,2,1,0:T(8,128)} custom-call(f32[128,512]{1,0:T(8,128)S(1)} %get-tuple-element.11.near, f32[16,512]{1,0:T(8,128)S(1)} %get-tuple-element.13.gains, f32[64,4,128]{2,1,0:T(4,128)S(1)} %all_to_all.17.links, f32[128,80]{1,0:T(8,128)S(1)} %copy-done.5), custom_call_target="tpu_custom_call" | custom-call | tf_op jit(solution)/shard_map/pallas_call | solution.py:98
Async XLA Ops:
  0.0 6.4 %copy-start.2 = (f32[8,8,512]{2,1,0:T(8,128)S(1)}, f32[8,8,512]{2,1,0:T(8,128)}, u32[]{:S(2)}) copy-start(f32[8,8,512]{2,1,0:T(8,128)} %volt.5) | copy-start | bytes 393220
  0.0 6.4 %copy-start = (f32[3,8,8,512]{3,2,1,0:T(8,128)S(1)}, f32[3,8,8,512]{3,2,1,0:T(8,128)}, u32[]{:S(2)}) copy-start(f32[3,8,8,512]{3,2,1,0:T(8,128)} %vel.5) | copy-start | bytes 1179652
  0.0 6.4 %copy-start.1 = (f32[2,8,8,512]{3,2,1,0:T(8,128)S(1)}, f32[2,8,8,512]{3,2,1,0:T(8,128)}, u32[]{:S(2)}) copy-start(f32[2,8,8,512]{3,2,1,0:T(8,128)} %conc.5) | copy-start | bytes 786436
  0.9 16.1 %collective-permute-start = (f32[4,8,512]{2,1,0:T(8,128)S(1)}, f32[4,8,512]{2,1,0:T(8,128)S(1)}, u32[]{:S(2)}, u32[]{:S(2)}) collective-permute-start(f32[4,8,512]{2,1,0:T(8,128)S(1)} %shard_map.74), channel_id=1, source_target_pairs={{0,1},{1,2},{2,3},{3,4},{4,5},{5,6},{6,7},{7,8},{8,9},{9,10},{10,1... | collective-permute-start | bytes 196616 | tf_op jit(solution)/shard_map/ppermute | solution.py:395
  6.4 0.9 %copy-start.4 = (f32[192,128]{1,0:T(8,128)S(1)}, f32[192,128]{1,0:T(8,128)}, u32[]{:S(2)}) copy-start(f32[192,128]{1,0:T(8,128)} %constant.8.clone.table) | copy-start | bytes 294916
  17.1 16.1 %copy-start.3 = (f32[256,128]{1,0:T(8,128)S(1)}, f32[256,128]{1,0:T(8,128)}, u32[]{:S(2)}) copy-start(f32[256,128]{1,0:T(8,128)} %constant.10.clone.solve) | copy-start | bytes 393220
  17.1 16.0 %copy-start.6 = (f32[128,128]{1,0:T(8,128)S(1)}, f32[128,128]{1,0:T(8,128)}, u32[]{:S(2)}) copy-start(f32[128,128]{1,0:T(8,128)} %constant.9.clone.collect) | copy-start | bytes 196612
  56.5 15.6 %copy-start.5 = (f32[128,80]{1,0:T(8,128)S(1)}, f32[128,80]{1,0:T(8,128)}, u32[]{:S(2)}) copy-start(f32[128,80]{1,0:T(8,128)} %constant.11.clone.table) | copy-start | bytes 122884

commit v7 on v6

--- a/solution.py
+++ b/solution.py
@@ -90,8 +90,11 @@
         near[s, :, :, s, :, :] = np.einsum("xa,zb->xzab", local_x, local_z)
         stream_spread[s, :, :, :, s, :] = np.einsum("ex,zb->xzeb", hand_x, np.eye(depth))
         wall_spread[s, :, :, :, s, :] = np.einsum("xa,ez->xzea", local_x, hand_z)
-    parts = (near[:, :, :, :, 0], stream_spread, wall_spread)
-    return near.reshape(cells, cells), np.concatenate([part.reshape(cells, -1) for part in parts], axis=1)
+    ends = []
+    for x in (0, width - 1):
+        parts = (near[:, :, :, :, x], stream_spread, wall_spread)
+        ends.append(np.concatenate([part.reshape(cells, -1) for part in parts], axis=1))
+    return near.reshape(cells, cells), np.stack(ends)
 
 
 def call(kernel, outs, ins, scratch=(), aliases=None, source=pltpu.VMEM, target=pltpu.VMEM, room=32 * 1024):
@@ -114,8 +117,12 @@
     return (conc_low + conc_high) * (speed_low + speed_high - drift(volt_high - volt_low, species))
 
 
+def mirrored():
+    return lax.rem(lax.axis_index("wall"), 2)
+
+
 def border_kernel(conc, vel, volt, edge, arrived):
-    last = volt.shape[0] - 1
+    last = (volt.shape[0] - 1) * (1 - mirrored())
     copies = [
         pltpu.make_async_copy(source, edge.at[place], arrived.at[place])
         for place, source in enumerate((conc.at[0, last], conc.at[1, last], vel.at[0, last], volt.at[last]))
@@ -193,23 +200,32 @@
     rows[:sums] = solved[cells.shape[0] :]
 
 
-def enter_kernel(decays_x, decays_z, rows_in, left_halo, conc, vel, volt, shares, gains, rows):
+def enter_kernel(decays_x, decays_z, rows_in, halo, conc, vel, volt, shares, gains, rows):
     width, depth, span = volt.shape
     row = lax.broadcasted_iota(jnp.int32, (depth, span), 0)
+    odd = mirrored()
+    even = 1 - odd
+    place = odd * (width - 1)
+    sign = (even - odd).astype(jnp.float32)
     for s in range(2):
         decay = decays_x[s]
-        flux = face(left_halo[s], conc[s, 0], left_halo[2], vel[0, 0], left_halo[3], volt[0], s)
-        taken = -FLUX_SCALE * flux
+        fall = sign * drift(volt[place] - halo[3], s)
+        flux = (conc[s, place] + halo[s]) * (vel[0, place] + halo[2] - fall)
+        taken = (-FLUX_SCALE * sign) * flux
         gained = (decay - 1.0) * taken
         gains[s * depth : (s + 1) * depth] = gained
-        for side, scale in enumerate((decay ** (width - 1) * (decay - 1.0), 1.0 / decay - 1.0)):
+        scales = (decay ** (width - 1) * (decay - 1.0), 1.0 / decay - 1.0)
+        for side in range(2):
+            scale = jnp.where(odd == side, jnp.float32(scales[0]), jnp.float32(scales[1]))
             start = (side * 2 + s) * depth
             rows[start : start + depth] = rows_in[start : start + depth] + scale * taken
             weight = jnp.zeros((depth, span), jnp.float32)
             for z in range(depth):
                 weight = jnp.where(row == z, decays_z[s] ** (z if side else depth - 1 - z), weight)
-            line = 4 * depth + (side * 2 + s) * width
-            rows[line : line + 1] = rows_in[line : line + 1] + jnp.sum(weight * gained, axis=0, keepdims=True)
+            total = jnp.sum(weight * gained, axis=0, keepdims=True)
+            for x, here in ((0, even), (width - 1, odd)):
+                line = 4 * depth + (side * 2 + s) * width + x
+                rows[line : line + 1] = rows_in[line : line + 1] + here.astype(jnp.float32) * total
     part = shares.shape[1] // HALVES
     tiles = LANES // part
     for chunk in range(span // LANES):
@@ -357,7 +373,7 @@
     copies = []
     for half in range(HALVES):
         cut = slice(half * (span // HALVES), (half + 1) * (span // HALVES))
-        added = left_product(table[...], jnp.concatenate([gains[:, cut], carry[:, cut]], axis=0))
+        added = left_product(table[mirrored()], jnp.concatenate([gains[:, cut], carry[:, cut]], axis=0))
         solved = near[:, cut] + added
         for s in range(2):
             for x in range(width):
@@ -392,7 +408,10 @@
         source=pltpu.HBM,
         room=53 * 1024 + 848,
     )
-    left_halo = lax.ppermute(edge, "stream", [(i, (i + 1) % stream) for i in range(stream)])
+    pairs = [
+        (row * stream + i, row * stream + (i + (-1 if row % 2 else 1)) % stream) for row in range(wall) for i in range(stream)
+    ]
+    halo = lax.ppermute(edge, ("wall", "stream"), pairs)
 
     members = TEAM * wall
     teams = stream // TEAM
@@ -414,7 +433,7 @@
     shares, gains, rows = call(
         functools.partial(enter_kernel, decays_x, decays_z),
         [tile, (2 * depth, span), (LANES, span)],
-        (rows, left_halo, concentration, velocity, potential),
+        (rows, halo, concentration, velocity, potential),
         aliases={0: 2},
     )
     parts = swap(shares, ("wall", "stream"), axis_index_groups=plane)

time: 73.4 us -> 73.5 us (level)
  waiting for transfers between devices: 8.97 us -> 0.01 us
  starting transfers between devices: 5.48 us -> 14.4 us
    ppermute x1, waiting for transfers between devices: 8.97 us -> 0.01 us  [per_device(): halo = lax.ppermute(edge, ('wall', 'stream'), pairs)]
    ppermute x1, starting transfers between devices: 5.48 us -> 14.4 us  [per_device(): halo = lax.ppermute(edge, ('wall', 'stream'), pairs)]
  transfers between devices with their start and end apart: 1 -> 1, of which waited for: 1 -> 0; matrix products, arithmetic and copies ran while one was open for 0% -> 0% of each run, Pallas kernels for 1% -> 1%
where the time goes in v7:
time: 73.5 us; the launch traced here: 73.2 us
  blocking collectives  53.7 us (73%)
  starting transfers between devices  14.4 us (20%)
  Pallas kernels  4.01 us (5%)
  local copies, waits for them, and re-layouts  0.92 us (1%)
    all_to_all x1, blocking collectives, per_device(): sums = swap(sums, 'stream', axis_index_groups=ranks)  22.1 us
    all_to_all x1, blocking collectives, per_device(): parts = swap(shares, ('wall', 'stream'), axis_index_groups=plane)  16.1 us
    all_to_all x1, blocking collectives, per_device(): links = swap(links, ('wall', 'stream'), axis_index_groups=plane)  15.6 us
    ppermute x1, starting transfers between devices, per_device(): halo = lax.ppermute(edge, ('wall', 'stream'), pairs)  14.4 us
    pallas_call x6, Pallas kernels, call(): pl.pallas_call(kernel, out_shape=[jax.ShapeDtypeStruct(shape, jnp.float32...  4.01 us
  transfers between devices with their start and end apart: 1, of which 0 were waited for; matrix products, arithmetic and copies ran while one was open for 0% of the time, Pallas kernels for 1%

profile of v7, /device:TPU:1, one launch (start us, length us, event | category | flops | bytes accessed | tf_op | source)
XLA Modules:
  0.0 73.2 jit_solution(2480134564672963517)
XLA Ops:
  0.0 0.0 copy-start.2
  0.0 0.0 copy-start
  0.0 0.0 copy-start.1
  0.0 0.9 %shard_map.74 = f32[4,8,512]{2,1,0:T(8,128)S(1)} custom-call(f32[2,8,8,512]{3,2,1,0:T(8,128)} %conc.5, f32[3,8,8,512]{3,2,1,0:T(8,128)} %vel.5, f32[8,8,512]{2,1,0:T(8,128)} %volt.5), custom_call_target="tpu_custom_call" | custom-call | tf_op jit(solution)/shard_map/pallas_call | solution.py:101
  0.9 14.4 %collective-permute-start = (f32[4,8,512]{2,1,0:T(8,128)S(1)}, f32[4,8,512]{2,1,0:T(8,128)S(1)}, u32[]{:S(2)}, u32[]{:S(2)}) collective-permute-start(f32[4,8,512]{2,1,0:T(8,128)S(1)} %shard_map.74), channel_id=1, source_target_pairs={{0,1},{1,2},{2,3},{3,4},{4,5},{5,6},{6,7},{7,8},{8,9},{9,10},{10,1... | collective-permute-start | bytes 196616 | tf_op jit(solution)/shard_map/ppermute | solution.py:414
  15.3 0.0 copy-done.2
  15.3 0.0 copy-done
  15.3 0.0 copy-done.1
  15.4 0.0 copy-start.5
  15.4 0.9 %copy-done.5 = f32[192,128]{1,0:T(8,128)S(1)} copy-done((f32[192,128]{1,0:T(8,128)S(1)}, f32[192,128]{1,0:T(8,128)}, u32[]{:S(2)}) %copy-start.5) | copy-done | bytes 98328
  16.2 0.7 shard_map.73
  16.9 0.0 collective-permute-done.halo
  16.9 0.2 shard_map.75
  17.1 0.0 copy-start.4
  17.1 0.0 copy-start.6
  17.2 16.1 %all_to_all.15.parts = f32[64,8,128]{2,1,0:T(8,128)S(1)} all-to-all(f32[64,8,128]{2,1,0:T(8,128)S(1)} %get-tuple-element.14), channel_id=1, replica_groups={{0,226,448,163,385,96,322,33,259,481,192,418,129,355,66,288,3,225,451,1..., dimensions={0} | all-to-all | bytes 524288 | tf_op jit(solution)/shard_map/all_to_all | solution.py:439
  33.2 0.0 copy-done.4
  33.2 0.0 copy-done.6
  33.2 1.0 %shard_map.76 = (f32[64,8,128]{2,1,0:T(8,128)S(1)}, f32[8,4,8,128]{3,2,1,0:T(8,128)S(1)}) custom-call(f32[64,8,128]{2,1,0:T(8,128)S(1)} %all_to_all.15.parts, f32[128,128]{1,0:T(8,128)S(1)} %copy-done.6, f32[256,128]{1,0:T(8,128)S(1)} %copy-done.4), custom_call_target="tpu_custom_call" | custom-call | tf_op jit(solution)/shard_map/pallas_call | solution.py:101
  34.2 22.1 %all_to_all.16.sums = f32[8,4,8,128]{3,2,1,0:T(8,128)S(1)} all-to-all(f32[8,4,8,128]{3,2,1,0:T(8,128)S(1)} %get-tuple-element.16), channel_id=1, replica_groups={{0,4,8,12,18,22,26,30},{1,5,9,13,19,23,27,31},{2,6,10,14,16,20,24,28},{..., dimensions={0} | all-to-all | bytes 262144 | tf_op jit(solution)/shard_map/all_to_all | solution.py:447
  56.2 0.3 shard_map.77
  56.5 0.0 copy-start.3
  56.5 15.6 %all_to_all.17.links = f32[64,4,128]{2,1,0:T(4,128)S(1)} all-to-all(f32[64,4,128]{2,1,0:T(4,128)S(1)} %shard_map.77), channel_id=1, replica_groups={{0,226,448,163,385,96,322,33,259,481,192,418,129,355,66,288,3,225,451,1..., dimensions={0} | all-to-all | bytes 262144 | tf_op jit(solution)/shard_map/all_to_all | solution.py:453
  72.1 0.0 copy-done.3
  72.1 1.0 %shard_map.78 = f32[2,8,8,512]{3,2,1,0:T(8,128)} custom-call(f32[128,512]{1,0:T(8,128)S(1)} %get-tuple-element.11.near, f32[16,512]{1,0:T(8,128)S(1)} %get-tuple-element.13.gains, f32[64,4,128]{2,1,0:T(4,128)S(1)} %all_to_all.17.links, f32[2,128,80]{2,1,0:T(8,128)S(1)} %copy-done.3), custom_call_target="tpu_custom_call" | custom-call | tf_op jit(solution)/shard_map/pallas_call | solution.py:101
Async XLA Ops:
  0.0 15.3 %copy-start.2 = (f32[8,8,512]{2,1,0:T(8,128)S(1)}, f32[8,8,512]{2,1,0:T(8,128)}, u32[]{:S(2)}) copy-start(f32[8,8,512]{2,1,0:T(8,128)} %volt.5) | copy-start | bytes 393220
  0.0 15.3 %copy-start = (f32[3,8,8,512]{3,2,1,0:T(8,128)S(1)}, f32[3,8,8,512]{3,2,1,0:T(8,128)}, u32[]{:S(2)}) copy-start(f32[3,8,8,512]{3,2,1,0:T(8,128)} %vel.5) | copy-start | bytes 1179652
  0.0 15.3 %copy-start.1 = (f32[2,8,8,512]{3,2,1,0:T(8,128)S(1)}, f32[2,8,8,512]{3,2,1,0:T(8,128)}, u32[]{:S(2)}) copy-start(f32[2,8,8,512]{3,2,1,0:T(8,128)} %conc.5) | copy-start | bytes 786436
  0.9 16.0 %collective-permute-start = (f32[4,8,512]{2,1,0:T(8,128)S(1)}, f32[4,8,512]{2,1,0:T(8,128)S(1)}, u32[]{:S(2)}, u32[]{:S(2)}) collective-permute-start(f32[4,8,512]{2,1,0:T(8,128)S(1)} %shard_map.74), channel_id=1, source_target_pairs={{0,1},{1,2},{2,3},{3,4},{4,5},{5,6},{6,7},{7,8},{8,9},{9,10},{10,1... | collective-permute-start | bytes 196616 | tf_op jit(solution)/shard_map/ppermute | solution.py:414
  15.4 0.9 %copy-start.5 = (f32[192,128]{1,0:T(8,128)S(1)}, f32[192,128]{1,0:T(8,128)}, u32[]{:S(2)}) copy-start(f32[192,128]{1,0:T(8,128)} %constant.8.clone.table) | copy-start | bytes 294916
  17.1 16.1 %copy-start.4 = (f32[256,128]{1,0:T(8,128)S(1)}, f32[256,128]{1,0:T(8,128)}, u32[]{:S(2)}) copy-start(f32[256,128]{1,0:T(8,128)} %constant.10.clone.solve) | copy-start | bytes 393220
  17.1 16.1 %copy-start.6 = (f32[128,128]{1,0:T(8,128)S(1)}, f32[128,128]{1,0:T(8,128)}, u32[]{:S(2)}) copy-start(f32[128,128]{1,0:T(8,128)} %constant.9.clone.collect) | copy-start | bytes 196612
  56.5 15.6 %copy-start.3 = (f32[2,128,80]{2,1,0:T(8,128)S(1)}, f32[2,128,80]{2,1,0:T(8,128)}, u32[]{:S(2)}) copy-start(f32[2,128,80]{2,1,0:T(8,128)} %constant.11.clone.table) | copy-start | bytes 245764

commit v8 on v6

--- a/solution.py
+++ b/solution.py
@@ -287,22 +287,28 @@
         for b in range(blocks):
             carry[list_place(m, b, blocks)] = jnp.where(entering, befores[b], afters[b]) + weights[b] * mirrored
     full = jnp.concatenate([value, carry[...].reshape(flat, LANES)], axis=1)
-    ends[...] = product(full, solve[...]).reshape(members, places, LANES)
+    result = product(full, solve[...])
+    ends[...] = result.reshape(members, places, LANES)
     step = by_lane(stream_steps, lane, depth)
     entering = lane < 2 * depth
     pack = LANES // (4 * depth)
     shift = member_shift(lax.div(lax.axis_index("stream"), TEAM), sums.shape[0])
+    weights = []
+    for m in range(TEAM):
+        options = [by_lane([value**k for value in stream_steps], lane, depth) for k in range(TEAM)]
+        plain = jnp.where(entering, options[TEAM - 1 - m], options[m])
+        turned = (m + TEAM // 2) % TEAM
+        weights.append(jnp.where(shift == 0, plain, jnp.where(entering, options[TEAM - 1 - turned], options[turned])))
     for group in range(blocks // pack):
         packed = None
         for part in range(pack):
             b = group * pack + part
-            own = [ends[shifted_place(m, b, blocks, shift)] for m in range(TEAM)]
-            before = own[0]
-            after = own[-1]
-            for m in range(1, TEAM):
-                before = step * before + own[m]
-                after = step * after + own[TEAM - 1 - m]
-            both = jnp.where(entering, before, jnp.where(lane < 4 * depth, after, 0.0))
+            both = None
+            for m in range(TEAM):
+                place = list_place(m, b, blocks) * places
+                term = weights[m] * result[place : place + places]
+                both = term if both is None else both + term
+            both = jnp.where(lane < 4 * depth, both, 0.0)
             packed = packed + pltpu.roll(both, part * 4 * depth, 1) if part else both
         for team in range(sums.shape[0]):
             sums[team, group] = packed
@@ -343,28 +349,29 @@
                 links[shifted_place(m, b, blocks, shift)] = halved[:part]
 
 
-def home_kernel(near, gains, links, table, out, rows, carry, result, sent):
+def home_kernel(near, gains, links, table, out, rows, solved, sent):
     _, width, depth, span = out.shape
     part = links.shape[1]
     lanes = LANES // HALVES
-    for k in range(links.shape[0]):
-        rows[k * part : (k + 1) * part] = links[k]
-    for chunk in range(rows.shape[0] // LANES):
-        turned = rows[chunk * LANES : (chunk + 1) * LANES].T
-        for half in range(HALVES):
-            start = half * (span // HALVES) + chunk * LANES
-            carry[:, start : start + LANES] = turned[half * lanes : (half + 1) * lanes]
+    tiles = LANES // part
     copies = []
-    for half in range(HALVES):
-        cut = slice(half * (span // HALVES), (half + 1) * (span // HALVES))
-        added = left_product(table[...], jnp.concatenate([gains[:, cut], carry[:, cut]], axis=0))
-        solved = near[:, cut] + added
-        for s in range(2):
-            for x in range(width):
-                start = (s * width + x) * depth
-                result[half, s, x] = solved[start : start + depth]
-        copies.append(pltpu.make_async_copy(result.at[half], out.at[:, :, :, cut], sent.at[half]))
-        copies[-1].start()
+    for chunk in range(links.shape[0] // tiles):
+        for k in range(tiles):
+            rows[k * part : (k + 1) * part] = links[chunk * tiles + k]
+        turned = rows[...].T
+        cuts = [slice(half * (span // HALVES) + chunk * LANES, half * (span // HALVES) + (chunk + 1) * LANES) for half in range(HALVES)]
+        carry = jnp.concatenate([turned[half * lanes : (half + 1) * lanes] for half in range(HALVES)], axis=1)
+        gained = jnp.concatenate([gains[:, cut] for cut in cuts], axis=1)
+        added = left_product(table[...], jnp.concatenate([gained, carry], axis=0))
+        for half, cut in enumerate(cuts):
+            place = chunk * HALVES + half
+            total = near[:, cut] + added[:, half * LANES : (half + 1) * LANES]
+            for s in range(2):
+                for x in range(width):
+                    start = (s * width + x) * depth
+                    solved[place, s, x] = total[start : start + depth]
+            copies.append(pltpu.make_async_copy(solved.at[place], out.at[:, :, :, cut], sent.at[place]))
+            copies[-1].start()
     for copy in copies:
         copy.wait()
 
@@ -437,10 +444,9 @@
         [concentration.shape],
         (near, gains, links, table(home)),
         [
-            pltpu.VMEM((span // HALVES, LANES), jnp.float32),
-            pltpu.VMEM((LANES // HALVES, span), jnp.float32),
-            pltpu.VMEM((HALVES, 2, width, depth, span // HALVES), jnp.float32),
-            pltpu.SemaphoreType.DMA((HALVES,)),
+            pltpu.VMEM((LANES, LANES), jnp.float32),
+            pltpu.VMEM((span // LANES, 2, width, depth, LANES), jnp.float32),
+            pltpu.SemaphoreType.DMA((span // LANES,)),
         ],
         target=pltpu.HBM,
     )

time: 73.4 us -> 73.4 us (level)
  no operation moved by 1% of the time
where the time goes in v8:
time: 73.4 us; the launch traced here: 73.1 us
  blocking collectives  53.7 us (73%)
  waiting for transfers between devices  8.97 us (12%)
  starting transfers between devices  5.48 us (7%)
  Pallas kernels  3.93 us (5%)
  local copies, waits for them, and re-layouts  0.92 us (1%)
    all_to_all x1, blocking collectives, per_device(): sums = swap(sums, 'stream', axis_index_groups=ranks)  22.1 us
    all_to_all x1, blocking collectives, per_device(): parts = swap(shares, ('wall', 'stream'), axis_index_groups=plane)  16 us
    all_to_all x1, blocking collectives, per_device(): links = swap(links, ('wall', 'stream'), axis_index_groups=plane)  15.6 us
    ppermute x1, waiting for transfers between devices, per_device(): lax.ppermute(edge, 'stream', [(i, (i + 1) % stream) for i in range(stream)])  8.97 us
    ppermute x1, starting transfers between devices, per_device(): lax.ppermute(edge, 'stream', [(i, (i + 1) % stream) for i in range(stream)])  5.48 us
    pallas_call x6, Pallas kernels, call(): pl.pallas_call(kernel, out_shape=[jax.ShapeDtypeStruct(shape, jnp.float32...  3.93 us
  transfers between devices with their start and end apart: 1, of which 1 were waited for; matrix products, arithmetic and copies ran while one was open for 0% of the time, Pallas kernels for 1%

profile of v8, /device:TPU:1, one launch (start us, length us, event | category | flops | bytes accessed | tf_op | source)
XLA Modules:
  0.0 73.1 jit_solution(13778936804063059358)
XLA Ops:
  0.0 0.0 copy-start.2
  0.0 0.0 copy-start
  0.0 0.0 copy-start.1
  0.0 0.9 %shard_map.74 = f32[4,8,512]{2,1,0:T(8,128)S(1)} custom-call(f32[2,8,8,512]{3,2,1,0:T(8,128)} %conc.5, f32[3,8,8,512]{3,2,1,0:T(8,128)} %vel.5, f32[8,8,512]{2,1,0:T(8,128)} %volt.5), custom_call_target="tpu_custom_call" | custom-call | tf_op jit(solution)/shard_map/pallas_call | solution.py:98
  0.9 5.5 %collective-permute-start = (f32[4,8,512]{2,1,0:T(8,128)S(1)}, f32[4,8,512]{2,1,0:T(8,128)S(1)}, u32[]{:S(2)}, u32[]{:S(2)}) collective-permute-start(f32[4,8,512]{2,1,0:T(8,128)S(1)} %shard_map.74), channel_id=1, source_target_pairs={{0,1},{1,2},{2,3},{3,4},{4,5},{5,6},{6,7},{7,8},{8,9},{9,10},{10,1... | collective-permute-start | bytes 196616 | tf_op jit(solution)/shard_map/ppermute | solution.py:402
  6.4 0.0 copy-done.2
  6.4 0.0 copy-done
  6.4 0.0 copy-done.1
  6.4 0.0 copy-start.4
  6.4 0.9 %copy-done.4 = f32[192,128]{1,0:T(8,128)S(1)} copy-done((f32[192,128]{1,0:T(8,128)S(1)}, f32[192,128]{1,0:T(8,128)}, u32[]{:S(2)}) %copy-start.4) | copy-done | bytes 98328
  7.3 0.7 shard_map.73
  8.0 9.0 %collective-permute-done.left_halo = f32[4,8,512]{2,1,0:T(8,128)S(1)} collective-permute-done((f32[4,8,512]{2,1,0:T(8,128)S(1)}, f32[4,8,512]{2,1,0:T(8,128)S(1)}, u32[]{:S(2)}, u32[]{:S(2)}) %collective-permute-start) | collective-permute-done | bytes 65568 | tf_op jit(solution)/shard_map/ppermute | solution.py:402
  17.0 0.2 shard_map.75
  17.1 0.0 copy-start.3
  17.1 0.0 copy-start.6
  17.2 16.0 %all_to_all.15.parts = f32[64,8,128]{2,1,0:T(8,128)S(1)} all-to-all(f32[64,8,128]{2,1,0:T(8,128)S(1)} %get-tuple-element.14), channel_id=1, replica_groups={{0,226,448,163,385,96,322,33,259,481,192,418,129,355,66,288,3,225,451,1..., dimensions={0} | all-to-all | bytes 524288 | tf_op jit(solution)/shard_map/all_to_all | solution.py:427
  33.2 0.0 copy-done.3
  33.2 0.0 copy-done.6
  33.2 0.9 %shard_map.76 = (f32[64,8,128]{2,1,0:T(8,128)S(1)}, f32[8,4,8,128]{3,2,1,0:T(8,128)S(1)}) custom-call(f32[64,8,128]{2,1,0:T(8,128)S(1)} %all_to_all.15.parts, f32[128,128]{1,0:T(8,128)S(1)} %copy-done.6, f32[256,128]{1,0:T(8,128)S(1)} %copy-done.3), custom_call_target="tpu_custom_call" | custom-call | tf_op jit(solution)/shard_map/pallas_call | solution.py:98
  34.1 22.1 %all_to_all.16.sums = f32[8,4,8,128]{3,2,1,0:T(8,128)S(1)} all-to-all(f32[8,4,8,128]{3,2,1,0:T(8,128)S(1)} %get-tuple-element.16), channel_id=1, replica_groups={{0,4,8,12,18,22,26,30},{1,5,9,13,19,23,27,31},{2,6,10,14,16,20,24,28},{..., dimensions={0} | all-to-all | bytes 262144 | tf_op jit(solution)/shard_map/all_to_all | solution.py:435
  56.2 0.3 shard_map.77
  56.4 0.0 copy-start.5
  56.4 15.6 %all_to_all.17.links = f32[64,4,128]{2,1,0:T(4,128)S(1)} all-to-all(f32[64,4,128]{2,1,0:T(4,128)S(1)} %shard_map.77), channel_id=1, replica_groups={{0,226,448,163,385,96,322,33,259,481,192,418,129,355,66,288,3,225,451,1..., dimensions={0} | all-to-all | bytes 262144 | tf_op jit(solution)/shard_map/all_to_all | solution.py:441
  72.0 0.0 copy-done.5
  72.0 1.1 %shard_map.78 = f32[2,8,8,512]{3,2,1,0:T(8,128)} custom-call(f32[128,512]{1,0:T(8,128)S(1)} %get-tuple-element.11.near, f32[16,512]{1,0:T(8,128)S(1)} %get-tuple-element.13.gains, f32[64,4,128]{2,1,0:T(4,128)S(1)} %all_to_all.17.links, f32[128,80]{1,0:T(8,128)S(1)} %copy-done.5), custom_call_target="tpu_custom_call" | custom-call | tf_op jit(solution)/shard_map/pallas_call | solution.py:98
Async XLA Ops:
  0.0 6.4 %copy-start.2 = (f32[8,8,512]{2,1,0:T(8,128)S(1)}, f32[8,8,512]{2,1,0:T(8,128)}, u32[]{:S(2)}) copy-start(f32[8,8,512]{2,1,0:T(8,128)} %volt.5) | copy-start | bytes 393220
  0.0 6.4 %copy-start = (f32[3,8,8,512]{3,2,1,0:T(8,128)S(1)}, f32[3,8,8,512]{3,2,1,0:T(8,128)}, u32[]{:S(2)}) copy-start(f32[3,8,8,512]{3,2,1,0:T(8,128)} %vel.5) | copy-start | bytes 1179652
  0.0 6.4 %copy-start.1 = (f32[2,8,8,512]{3,2,1,0:T(8,128)S(1)}, f32[2,8,8,512]{3,2,1,0:T(8,128)}, u32[]{:S(2)}) copy-start(f32[2,8,8,512]{3,2,1,0:T(8,128)} %conc.5) | copy-start | bytes 786436
  0.9 16.1 %collective-permute-start = (f32[4,8,512]{2,1,0:T(8,128)S(1)}, f32[4,8,512]{2,1,0:T(8,128)S(1)}, u32[]{:S(2)}, u32[]{:S(2)}) collective-permute-start(f32[4,8,512]{2,1,0:T(8,128)S(1)} %shard_map.74), channel_id=1, source_target_pairs={{0,1},{1,2},{2,3},{3,4},{4,5},{5,6},{6,7},{7,8},{8,9},{9,10},{10,1... | collective-permute-start | bytes 196616 | tf_op jit(solution)/shard_map/ppermute | solution.py:402
  6.4 0.9 %copy-start.4 = (f32[192,128]{1,0:T(8,128)S(1)}, f32[192,128]{1,0:T(8,128)}, u32[]{:S(2)}) copy-start(f32[192,128]{1,0:T(8,128)} %constant.8.clone.table) | copy-start | bytes 294916
  17.1 16.1 %copy-start.3 = (f32[256,128]{1,0:T(8,128)S(1)}, f32[256,128]{1,0:T(8,128)}, u32[]{:S(2)}) copy-start(f32[256,128]{1,0:T(8,128)} %constant.10.clone.solve) | copy-start | bytes 393220
  17.1 16.0 %copy-start.6 = (f32[128,128]{1,0:T(8,128)S(1)}, f32[128,128]{1,0:T(8,128)}, u32[]{:S(2)}) copy-start(f32[128,128]{1,0:T(8,128)} %constant.9.clone.collect) | copy-start | bytes 196612
  56.4 15.6 %copy-start.5 = (f32[128,80]{1,0:T(8,128)S(1)}, f32[128,80]{1,0:T(8,128)}, u32[]{:S(2)}) copy-start(f32[128,80]{1,0:T(8,128)} %constant.11.clone.table) | copy-start | bytes 122884

commit v9 on v8

--- a/solution.py
+++ b/solution.py
@@ -236,12 +236,12 @@
     return jnp.where(lax.bitwise_and(lane, unit) == 0, values[0], values[1])
 
 
-def wall_kernel(decays, stream_steps, blocks, width, depth, parts, collect, solve, ends, sums, carry, lines):
+def wall_kernel(decays, stream_steps, blocks, width, depth, parts, collect, solve, ends, sums):
     members, places, _ = parts.shape
-    flat = members * places
     lane = lax.broadcasted_iota(jnp.int32, (places, LANES), 1)
     faces = 2 * width
     first = LANES // 2
+    lines = [None] * members
     for m in range(TEAM):
         below = pltpu.roll(parts[list_place(m, 0, blocks)], LANES - 2 * faces, 1)
         below = below * pltpu.roll(below, LANES - faces, 1)
@@ -254,8 +254,9 @@
             both = jnp.where(lane < first + faces, above, pltpu.roll(below, faces, 1))
             lines[list_place(m, b, blocks)] = jnp.where(lane < first, own, both)
             below = above
-    value = lines[...].reshape(flat, LANES)
-    carry[...] = product(value, collect[...]).reshape(members, places, LANES)
+    value = jnp.concatenate(lines, axis=0)
+    gathered = product(value, collect[...])
+    carry = [gathered[k * places : (k + 1) * places] for k in range(members)]
     side = LANES // 2
     unit = LANES // 4
     entering = lane < side
@@ -286,7 +287,7 @@
         mirrored = scale * (pltpu.roll(total, side, 1) - mirror * total)
         for b in range(blocks):
             carry[list_place(m, b, blocks)] = jnp.where(entering, befores[b], afters[b]) + weights[b] * mirrored
-    full = jnp.concatenate([value, carry[...].reshape(flat, LANES)], axis=1)
+    full = jnp.concatenate([value, jnp.concatenate(carry, axis=0)], axis=1)
     result = product(full, solve[...])
     ends[...] = result.reshape(members, places, LANES)
     step = by_lane(stream_steps, lane, depth)
@@ -430,7 +431,6 @@
         functools.partial(wall_kernel, decays_z, steps_x, wall, width, depth),
         [tile, (teams, wall // pack, places, LANES)],
         (parts, table(collect_z), table(solve_z)),
-        [pltpu.VMEM(tile, jnp.float32), pltpu.VMEM(tile, jnp.float32)],
     )
     sums = swap(sums, "stream", axis_index_groups=ranks)
     (links,) = call(

time: 73.4 us -> 73.4 us (level)
  no operation moved by 1% of the time
where the time goes in v9:
time: 73.4 us; the launch traced here: 73.1 us
  blocking collectives  53.7 us (73%)
  waiting for transfers between devices  8.97 us (12%)
  starting transfers between devices  5.48 us (7%)
  Pallas kernels  3.93 us (5%)
  local copies, waits for them, and re-layouts  0.92 us (1%)
    all_to_all x1, blocking collectives, per_device(): sums = swap(sums, 'stream', axis_index_groups=ranks)  22.1 us
    all_to_all x1, blocking collectives, per_device(): parts = swap(shares, ('wall', 'stream'), axis_index_groups=plane)  16 us
    all_to_all x1, blocking collectives, per_device(): links = swap(links, ('wall', 'stream'), axis_index_groups=plane)  15.6 us
    ppermute x1, waiting for transfers between devices, per_device(): lax.ppermute(edge, 'stream', [(i, (i + 1) % stream) for i in range(stream)])  8.97 us
    ppermute x1, starting transfers between devices, per_device(): lax.ppermute(edge, 'stream', [(i, (i + 1) % stream) for i in range(stream)])  5.48 us
    pallas_call x6, Pallas kernels, call(): pl.pallas_call(kernel, out_shape=[jax.ShapeDtypeStruct(shape, jnp.float32...  3.93 us
  transfers between devices with their start and end apart: 1, of which 1 were waited for; matrix products, arithmetic and copies ran while one was open for 0% of the time, Pallas kernels for 1%

profile of v9, /device:TPU:1, one launch (start us, length us, event | category | flops | bytes accessed | tf_op | source)
XLA Modules:
  0.0 73.1 jit_solution(12244101729585643082)
XLA Ops:
  0.0 0.0 copy-start.2
  0.0 0.0 copy-start
  0.0 0.0 copy-start.1
  0.0 0.9 %shard_map.74 = f32[4,8,512]{2,1,0:T(8,128)S(1)} custom-call(f32[2,8,8,512]{3,2,1,0:T(8,128)} %conc.5, f32[3,8,8,512]{3,2,1,0:T(8,128)} %vel.5, f32[8,8,512]{2,1,0:T(8,128)} %volt.5), custom_call_target="tpu_custom_call" | custom-call | tf_op jit(solution)/shard_map/pallas_call | solution.py:98
  0.9 5.5 %collective-permute-start = (f32[4,8,512]{2,1,0:T(8,128)S(1)}, f32[4,8,512]{2,1,0:T(8,128)S(1)}, u32[]{:S(2)}, u32[]{:S(2)}) collective-permute-start(f32[4,8,512]{2,1,0:T(8,128)S(1)} %shard_map.74), channel_id=1, source_target_pairs={{0,1},{1,2},{2,3},{3,4},{4,5},{5,6},{6,7},{7,8},{8,9},{9,10},{10,1... | collective-permute-start | bytes 196616 | tf_op jit(solution)/shard_map/ppermute | solution.py:403
  6.4 0.0 copy-done.2
  6.4 0.0 copy-done
  6.4 0.0 copy-done.1
  6.4 0.0 copy-start.4
  6.4 0.9 %copy-done.4 = f32[192,128]{1,0:T(8,128)S(1)} copy-done((f32[192,128]{1,0:T(8,128)S(1)}, f32[192,128]{1,0:T(8,128)}, u32[]{:S(2)}) %copy-start.4) | copy-done | bytes 98328
  7.3 0.7 shard_map.73
  8.0 9.0 %collective-permute-done.left_halo = f32[4,8,512]{2,1,0:T(8,128)S(1)} collective-permute-done((f32[4,8,512]{2,1,0:T(8,128)S(1)}, f32[4,8,512]{2,1,0:T(8,128)S(1)}, u32[]{:S(2)}, u32[]{:S(2)}) %collective-permute-start) | collective-permute-done | bytes 65568 | tf_op jit(solution)/shard_map/ppermute | solution.py:403
  17.0 0.2 shard_map.75
  17.1 0.0 copy-start.3
  17.1 0.0 copy-start.6
  17.2 16.0 %all_to_all.15.parts = f32[64,8,128]{2,1,0:T(8,128)S(1)} all-to-all(f32[64,8,128]{2,1,0:T(8,128)S(1)} %get-tuple-element.14), channel_id=1, replica_groups={{0,226,448,163,385,96,322,33,259,481,192,418,129,355,66,288,3,225,451,1..., dimensions={0} | all-to-all | bytes 524288 | tf_op jit(solution)/shard_map/all_to_all | solution.py:428
  33.2 0.0 copy-done.3
  33.2 0.0 copy-done.6
  33.2 0.9 %shard_map.76 = (f32[64,8,128]{2,1,0:T(8,128)S(1)}, f32[8,4,8,128]{3,2,1,0:T(8,128)S(1)}) custom-call(f32[64,8,128]{2,1,0:T(8,128)S(1)} %all_to_all.15.parts, f32[128,128]{1,0:T(8,128)S(1)} %copy-done.6, f32[256,128]{1,0:T(8,128)S(1)} %copy-done.3), custom_call_target="tpu_custom_call" | custom-call | tf_op jit(solution)/shard_map/pallas_call | solution.py:98
  34.1 22.1 %all_to_all.16.sums = f32[8,4,8,128]{3,2,1,0:T(8,128)S(1)} all-to-all(f32[8,4,8,128]{3,2,1,0:T(8,128)S(1)} %get-tuple-element.16), channel_id=1, replica_groups={{0,4,8,12,18,22,26,30},{1,5,9,13,19,23,27,31},{2,6,10,14,16,20,24,28},{..., dimensions={0} | all-to-all | bytes 262144 | tf_op jit(solution)/shard_map/all_to_all | solution.py:435
  56.2 0.3 shard_map.77
  56.4 0.0 copy-start.5
  56.4 15.6 %all_to_all.17.links = f32[64,4,128]{2,1,0:T(4,128)S(1)} all-to-all(f32[64,4,128]{2,1,0:T(4,128)S(1)} %shard_map.77), channel_id=1, replica_groups={{0,226,448,163,385,96,322,33,259,481,192,418,129,355,66,288,3,225,451,1..., dimensions={0} | all-to-all | bytes 262144 | tf_op jit(solution)/shard_map/all_to_all | solution.py:441
  72.0 0.0 copy-done.5
  72.0 1.1 %shard_map.78 = f32[2,8,8,512]{3,2,1,0:T(8,128)} custom-call(f32[128,512]{1,0:T(8,128)S(1)} %get-tuple-element.11.near, f32[16,512]{1,0:T(8,128)S(1)} %get-tuple-element.13.gains, f32[64,4,128]{2,1,0:T(4,128)S(1)} %all_to_all.17.links, f32[128,80]{1,0:T(8,128)S(1)} %copy-done.5), custom_call_target="tpu_custom_call" | custom-call | tf_op jit(solution)/shard_map/pallas_call | solution.py:98
Async XLA Ops:
  0.0 6.4 %copy-start.2 = (f32[8,8,512]{2,1,0:T(8,128)S(1)}, f32[8,8,512]{2,1,0:T(8,128)}, u32[]{:S(2)}) copy-start(f32[8,8,512]{2,1,0:T(8,128)} %volt.5) | copy-start | bytes 393220
  0.0 6.4 %copy-start = (f32[3,8,8,512]{3,2,1,0:T(8,128)S(1)}, f32[3,8,8,512]{3,2,1,0:T(8,128)}, u32[]{:S(2)}) copy-start(f32[3,8,8,512]{3,2,1,0:T(8,128)} %vel.5) | copy-start | bytes 1179652
  0.0 6.4 %copy-start.1 = (f32[2,8,8,512]{3,2,1,0:T(8,128)S(1)}, f32[2,8,8,512]{3,2,1,0:T(8,128)}, u32[]{:S(2)}) copy-start(f32[2,8,8,512]{3,2,1,0:T(8,128)} %conc.5) | copy-start | bytes 786436
  0.9 16.1 %collective-permute-start = (f32[4,8,512]{2,1,0:T(8,128)S(1)}, f32[4,8,512]{2,1,0:T(8,128)S(1)}, u32[]{:S(2)}, u32[]{:S(2)}) collective-permute-start(f32[4,8,512]{2,1,0:T(8,128)S(1)} %shard_map.74), channel_id=1, source_target_pairs={{0,1},{1,2},{2,3},{3,4},{4,5},{5,6},{6,7},{7,8},{8,9},{9,10},{10,1... | collective-permute-start | bytes 196616 | tf_op jit(solution)/shard_map/ppermute | solution.py:403
  6.4 0.9 %copy-start.4 = (f32[192,128]{1,0:T(8,128)S(1)}, f32[192,128]{1,0:T(8,128)}, u32[]{:S(2)}) copy-start(f32[192,128]{1,0:T(8,128)} %constant.8.clone.table) | copy-start | bytes 294916
  17.1 16.1 %copy-start.3 = (f32[256,128]{1,0:T(8,128)S(1)}, f32[256,128]{1,0:T(8,128)}, u32[]{:S(2)}) copy-start(f32[256,128]{1,0:T(8,128)} %constant.10.clone.solve) | copy-start | bytes 393220
  17.1 16.0 %copy-start.6 = (f32[128,128]{1,0:T(8,128)S(1)}, f32[128,128]{1,0:T(8,128)}, u32[]{:S(2)}) copy-start(f32[128,128]{1,0:T(8,128)} %constant.9.clone.collect) | copy-start | bytes 196612
  56.4 15.6 %copy-start.5 = (f32[128,80]{1,0:T(8,128)S(1)}, f32[128,80]{1,0:T(8,128)}, u32[]{:S(2)}) copy-start(f32[128,80]{1,0:T(8,128)} %constant.11.clone.table) | copy-start | bytes 122884

commit v10 on v8

--- a/solution.py
+++ b/solution.py
@@ -349,16 +349,12 @@
                 links[shifted_place(m, b, blocks, shift)] = halved[:part]
 
 
-def home_kernel(near, gains, links, table, out, rows, solved, sent):
+def home_kernel(near, gains, links, table, out, solved, sent):
     _, width, depth, span = out.shape
-    part = links.shape[1]
     lanes = LANES // HALVES
-    tiles = LANES // part
     copies = []
-    for chunk in range(links.shape[0] // tiles):
-        for k in range(tiles):
-            rows[k * part : (k + 1) * part] = links[chunk * tiles + k]
-        turned = rows[...].T
+    for chunk in range(links.shape[0] // LANES):
+        turned = links[chunk * LANES : (chunk + 1) * LANES].T
         cuts = [slice(half * (span // HALVES) + chunk * LANES, half * (span // HALVES) + (chunk + 1) * LANES) for half in range(HALVES)]
         carry = jnp.concatenate([turned[half * lanes : (half + 1) * lanes] for half in range(HALVES)], axis=1)
         gained = jnp.concatenate([gains[:, cut] for cut in cuts], axis=1)
@@ -442,9 +438,8 @@
     (out,) = call(
         home_kernel,
         [concentration.shape],
-        (near, gains, links, table(home)),
+        (near, gains, links.reshape(-1, LANES), table(home)),
         [
-            pltpu.VMEM((LANES, LANES), jnp.float32),
             pltpu.VMEM((span // LANES, 2, width, depth, LANES), jnp.float32),
             pltpu.SemaphoreType.DMA((span // LANES,)),
         ],

time: 73.4 us -> 73.4 us (level)
  no operation moved by 1% of the time
where the time goes in v10:
time: 73.4 us; the launch traced here: 73.1 us
  blocking collectives  53.7 us (73%)
  waiting for transfers between devices  8.97 us (12%)
  starting transfers between devices  5.48 us (7%)
  Pallas kernels  3.92 us (5%)
  local copies, waits for them, and re-layouts  0.92 us (1%)
    all_to_all x1, blocking collectives, per_device(): sums = swap(sums, 'stream', axis_index_groups=ranks)  22.1 us
    all_to_all x1, blocking collectives, per_device(): parts = swap(shares, ('wall', 'stream'), axis_index_groups=plane)  16 us
    all_to_all x1, blocking collectives, per_device(): links = swap(links, ('wall', 'stream'), axis_index_groups=plane)  15.6 us
    ppermute x1, waiting for transfers between devices, per_device(): lax.ppermute(edge, 'stream', [(i, (i + 1) % stream) for i in range(stream)])  8.97 us
    ppermute x1, starting transfers between devices, per_device(): lax.ppermute(edge, 'stream', [(i, (i + 1) % stream) for i in range(stream)])  5.48 us
    pallas_call x6, Pallas kernels, call(): pl.pallas_call(kernel, out_shape=[jax.ShapeDtypeStruct(shape, jnp.float32...  3.92 us
  transfers between devices with their start and end apart: 1, of which 1 were waited for; matrix products, arithmetic and copies ran while one was open for 0% of the time, Pallas kernels for 1%

profile of v10, /device:TPU:1, one launch (start us, length us, event | category | flops | bytes accessed | tf_op | source)
XLA Modules:
  0.0 73.1 jit_solution(13799200699823094679)
XLA Ops:
  0.0 0.0 copy-start.2
  0.0 0.0 copy-start
  0.0 0.0 copy-start.1
  0.0 0.9 %shard_map.74 = f32[4,8,512]{2,1,0:T(8,128)S(1)} custom-call(f32[2,8,8,512]{3,2,1,0:T(8,128)} %conc.5, f32[3,8,8,512]{3,2,1,0:T(8,128)} %vel.5, f32[8,8,512]{2,1,0:T(8,128)} %volt.5), custom_call_target="tpu_custom_call" | custom-call | tf_op jit(solution)/shard_map/pallas_call | solution.py:98
  0.9 5.5 %collective-permute-start = (f32[4,8,512]{2,1,0:T(8,128)S(1)}, f32[4,8,512]{2,1,0:T(8,128)S(1)}, u32[]{:S(2)}, u32[]{:S(2)}) collective-permute-start(f32[4,8,512]{2,1,0:T(8,128)S(1)} %shard_map.74), channel_id=1, source_target_pairs={{0,1},{1,2},{2,3},{3,4},{4,5},{5,6},{6,7},{7,8},{8,9},{9,10},{10,1... | collective-permute-start | bytes 196616 | tf_op jit(solution)/shard_map/ppermute | solution.py:398
  6.4 0.0 copy-done.2
  6.4 0.0 copy-done
  6.4 0.0 copy-done.1
  6.4 0.0 copy-start.4
  6.4 0.9 %copy-done.4 = f32[192,128]{1,0:T(8,128)S(1)} copy-done((f32[192,128]{1,0:T(8,128)S(1)}, f32[192,128]{1,0:T(8,128)}, u32[]{:S(2)}) %copy-start.4) | copy-done | bytes 98328
  7.3 0.7 shard_map.73
  8.0 9.0 %collective-permute-done.left_halo = f32[4,8,512]{2,1,0:T(8,128)S(1)} collective-permute-done((f32[4,8,512]{2,1,0:T(8,128)S(1)}, f32[4,8,512]{2,1,0:T(8,128)S(1)}, u32[]{:S(2)}, u32[]{:S(2)}) %collective-permute-start) | collective-permute-done | bytes 65568 | tf_op jit(solution)/shard_map/ppermute | solution.py:398
  17.0 0.2 shard_map.75
  17.1 0.0 copy-start.3
  17.1 0.0 copy-start.6
  17.2 16.0 %all_to_all.15.parts = f32[64,8,128]{2,1,0:T(8,128)S(1)} all-to-all(f32[64,8,128]{2,1,0:T(8,128)S(1)} %get-tuple-element.14), channel_id=1, replica_groups={{0,226,448,163,385,96,322,33,259,481,192,418,129,355,66,288,3,225,451,1..., dimensions={0} | all-to-all | bytes 524288 | tf_op jit(solution)/shard_map/all_to_all | solution.py:423
  33.2 0.0 copy-done.3
  33.2 0.0 copy-done.6
  33.2 0.9 %shard_map.76 = (f32[64,8,128]{2,1,0:T(8,128)S(1)}, f32[8,4,8,128]{3,2,1,0:T(8,128)S(1)}) custom-call(f32[64,8,128]{2,1,0:T(8,128)S(1)} %all_to_all.15.parts, f32[128,128]{1,0:T(8,128)S(1)} %copy-done.6, f32[256,128]{1,0:T(8,128)S(1)} %copy-done.3), custom_call_target="tpu_custom_call" | custom-call | tf_op jit(solution)/shard_map/pallas_call | solution.py:98
  34.1 22.1 %all_to_all.16.sums = f32[8,4,8,128]{3,2,1,0:T(8,128)S(1)} all-to-all(f32[8,4,8,128]{3,2,1,0:T(8,128)S(1)} %get-tuple-element.16), channel_id=1, replica_groups={{0,4,8,12,18,22,26,30},{1,5,9,13,19,23,27,31},{2,6,10,14,16,20,24,28},{..., dimensions={0} | all-to-all | bytes 262144 | tf_op jit(solution)/shard_map/all_to_all | solution.py:431
  56.2 0.3 shard_map.77
  56.4 0.0 copy-start.5
  56.4 15.6 %all_to_all.17 = f32[64,4,128]{2,1,0:T(4,128)S(1)} all-to-all(f32[64,4,128]{2,1,0:T(4,128)S(1)} %shard_map.77), channel_id=1, replica_groups={{0,226,448,163,385,96,322,33,259,481,192,418,129,355,66,288,3,225,451,1..., dimensions={0} | all-to-all | bytes 262144 | tf_op jit(solution)/shard_map/all_to_all | solution.py:437
  72.0 0.0 copy-done.5
  72.0 1.0 %shard_map.78 = f32[2,8,8,512]{3,2,1,0:T(8,128)} custom-call(f32[128,512]{1,0:T(8,128)S(1)} %get-tuple-element.11.near, f32[16,512]{1,0:T(8,128)S(1)} %get-tuple-element.13.gains, f32[256,128]{1,0:T(8,128)S(1)} %bitcast.1, f32[128,80]{1,0:T(8,128)S(1)} %copy-done.5), custom_call_target="tpu_custom_call" | custom-call | tf_op jit(solution)/shard_map/pallas_call | solution.py:98
Async XLA Ops:
  0.0 6.4 %copy-start.2 = (f32[8,8,512]{2,1,0:T(8,128)S(1)}, f32[8,8,512]{2,1,0:T(8,128)}, u32[]{:S(2)}) copy-start(f32[8,8,512]{2,1,0:T(8,128)} %volt.5) | copy-start | bytes 393220
  0.0 6.4 %copy-start = (f32[3,8,8,512]{3,2,1,0:T(8,128)S(1)}, f32[3,8,8,512]{3,2,1,0:T(8,128)}, u32[]{:S(2)}) copy-start(f32[3,8,8,512]{3,2,1,0:T(8,128)} %vel.5) | copy-start | bytes 1179652
  0.0 6.4 %copy-start.1 = (f32[2,8,8,512]{3,2,1,0:T(8,128)S(1)}, f32[2,8,8,512]{3,2,1,0:T(8,128)}, u32[]{:S(2)}) copy-start(f32[2,8,8,512]{3,2,1,0:T(8,128)} %conc.5) | copy-start | bytes 786436
  0.9 16.1 %collective-permute-start = (f32[4,8,512]{2,1,0:T(8,128)S(1)}, f32[4,8,512]{2,1,0:T(8,128)S(1)}, u32[]{:S(2)}, u32[]{:S(2)}) collective-permute-start(f32[4,8,512]{2,1,0:T(8,128)S(1)} %shard_map.74), channel_id=1, source_target_pairs={{0,1},{1,2},{2,3},{3,4},{4,5},{5,6},{6,7},{7,8},{8,9},{9,10},{10,1... | collective-permute-start | bytes 196616 | tf_op jit(solution)/shard_map/ppermute | solution.py:398
  6.4 0.9 %copy-start.4 = (f32[192,128]{1,0:T(8,128)S(1)}, f32[192,128]{1,0:T(8,128)}, u32[]{:S(2)}) copy-start(f32[192,128]{1,0:T(8,128)} %constant.8.clone.table) | copy-start | bytes 294916
  17.1 16.1 %copy-start.3 = (f32[256,128]{1,0:T(8,128)S(1)}, f32[256,128]{1,0:T(8,128)}, u32[]{:S(2)}) copy-start(f32[256,128]{1,0:T(8,128)} %constant.10.clone.solve) | copy-start | bytes 393220
  17.1 16.0 %copy-start.6 = (f32[128,128]{1,0:T(8,128)S(1)}, f32[128,128]{1,0:T(8,128)}, u32[]{:S(2)}) copy-start(f32[128,128]{1,0:T(8,128)} %constant.9.clone.collect) | copy-start | bytes 196612
  56.4 15.6 %copy-start.5 = (f32[128,80]{1,0:T(8,128)S(1)}, f32[128,80]{1,0:T(8,128)}, u32[]{:S(2)}) copy-start(f32[128,80]{1,0:T(8,128)} %constant.11.clone.table) | copy-start | bytes 122884

commit v11 on v10

--- a/solution.py
+++ b/solution.py
@@ -229,7 +229,7 @@
 
 
 def shifted_place(member, block, blocks, shift):
-    return lax.rem(list_place(member, block, blocks) + shift * blocks, TEAM * blocks)
+    return lax.bitwise_and(list_place(member, block, blocks) + shift * blocks, TEAM * blocks - 1)
 
 
 def by_lane(values, lane, unit):

time: 73.4 us -> 73.4 us (level)
  no operation moved by 1% of the time
where the time goes in v11:
time: 73.4 us; the launch traced here: 73 us
  blocking collectives  53.7 us (73%)
  waiting for transfers between devices  8.97 us (12%)
  starting transfers between devices  5.48 us (7%)
  Pallas kernels  3.88 us (5%)
  local copies, waits for them, and re-layouts  0.92 us (1%)
    all_to_all x1, blocking collectives, per_device(): sums = swap(sums, 'stream', axis_index_groups=ranks)  22.1 us
    all_to_all x1, blocking collectives, per_device(): parts = swap(shares, ('wall', 'stream'), axis_index_groups=plane)  16 us
    all_to_all x1, blocking collectives, per_device(): links = swap(links, ('wall', 'stream'), axis_index_groups=plane)  15.6 us
    ppermute x1, waiting for transfers between devices, per_device(): lax.ppermute(edge, 'stream', [(i, (i + 1) % stream) for i in range(stream)])  8.97 us
    ppermute x1, starting transfers between devices, per_device(): lax.ppermute(edge, 'stream', [(i, (i + 1) % stream) for i in range(stream)])  5.48 us
    pallas_call x6, Pallas kernels, call(): pl.pallas_call(kernel, out_shape=[jax.ShapeDtypeStruct(shape, jnp.float32...  3.88 us
  transfers between devices with their start and end apart: 1, of which 1 were waited for; matrix products, arithmetic and copies ran while one was open for 0% of the time, Pallas kernels for 1%

profile of v11, /device:TPU:1, one launch (start us, length us, event | category | flops | bytes accessed | tf_op | source)
XLA Modules:
  0.0 73.0 jit_solution(17726390951637645616)
XLA Ops:
  0.0 0.0 copy-start.2
  0.0 0.0 copy-start
  0.0 0.0 copy-start.1
  0.0 0.9 %shard_map.74 = f32[4,8,512]{2,1,0:T(8,128)S(1)} custom-call(f32[2,8,8,512]{3,2,1,0:T(8,128)} %conc.5, f32[3,8,8,512]{3,2,1,0:T(8,128)} %vel.5, f32[8,8,512]{2,1,0:T(8,128)} %volt.5), custom_call_target="tpu_custom_call" | custom-call | tf_op jit(solution)/shard_map/pallas_call | solution.py:98
  0.9 5.5 %collective-permute-start = (f32[4,8,512]{2,1,0:T(8,128)S(1)}, f32[4,8,512]{2,1,0:T(8,128)S(1)}, u32[]{:S(2)}, u32[]{:S(2)}) collective-permute-start(f32[4,8,512]{2,1,0:T(8,128)S(1)} %shard_map.74), channel_id=1, source_target_pairs={{0,1},{1,2},{2,3},{3,4},{4,5},{5,6},{6,7},{7,8},{8,9},{9,10},{10,1... | collective-permute-start | bytes 196616 | tf_op jit(solution)/shard_map/ppermute | solution.py:398
  6.4 0.0 copy-done.2
  6.4 0.0 copy-done
  6.4 0.0 copy-done.1
  6.4 0.0 copy-start.4
  6.4 0.9 %copy-done.4 = f32[192,128]{1,0:T(8,128)S(1)} copy-done((f32[192,128]{1,0:T(8,128)S(1)}, f32[192,128]{1,0:T(8,128)}, u32[]{:S(2)}) %copy-start.4) | copy-done | bytes 98328
  7.3 0.7 shard_map.73
  8.0 9.0 %collective-permute-done.left_halo = f32[4,8,512]{2,1,0:T(8,128)S(1)} collective-permute-done((f32[4,8,512]{2,1,0:T(8,128)S(1)}, f32[4,8,512]{2,1,0:T(8,128)S(1)}, u32[]{:S(2)}, u32[]{:S(2)}) %collective-permute-start) | collective-permute-done | bytes 65568 | tf_op jit(solution)/shard_map/ppermute | solution.py:398
  17.0 0.2 shard_map.75
  17.1 0.0 copy-start.3
  17.1 0.0 copy-start.6
  17.2 16.0 %all_to_all.15.parts = f32[64,8,128]{2,1,0:T(8,128)S(1)} all-to-all(f32[64,8,128]{2,1,0:T(8,128)S(1)} %get-tuple-element.14), channel_id=1, replica_groups={{0,226,448,163,385,96,322,33,259,481,192,418,129,355,66,288,3,225,451,1..., dimensions={0} | all-to-all | bytes 524288 | tf_op jit(solution)/shard_map/all_to_all | solution.py:423
  33.2 0.0 copy-done.3
  33.2 0.0 copy-done.6
  33.2 0.9 %shard_map.76 = (f32[64,8,128]{2,1,0:T(8,128)S(1)}, f32[8,4,8,128]{3,2,1,0:T(8,128)S(1)}) custom-call(f32[64,8,128]{2,1,0:T(8,128)S(1)} %all_to_all.15.parts, f32[128,128]{1,0:T(8,128)S(1)} %copy-done.6, f32[256,128]{1,0:T(8,128)S(1)} %copy-done.3), custom_call_target="tpu_custom_call" | custom-call | tf_op jit(solution)/shard_map/pallas_call | solution.py:98
  34.1 22.1 %all_to_all.16.sums = f32[8,4,8,128]{3,2,1,0:T(8,128)S(1)} all-to-all(f32[8,4,8,128]{3,2,1,0:T(8,128)S(1)} %get-tuple-element.16), channel_id=1, replica_groups={{0,4,8,12,18,22,26,30},{1,5,9,13,19,23,27,31},{2,6,10,14,16,20,24,28},{..., dimensions={0} | all-to-all | bytes 262144 | tf_op jit(solution)/shard_map/all_to_all | solution.py:431
  56.2 0.2 shard_map.77
  56.4 0.0 copy-start.5
  56.4 15.6 %all_to_all.17 = f32[64,4,128]{2,1,0:T(4,128)S(1)} all-to-all(f32[64,4,128]{2,1,0:T(4,128)S(1)} %shard_map.77), channel_id=1, replica_groups={{0,226,448,163,385,96,322,33,259,481,192,418,129,355,66,288,3,225,451,1..., dimensions={0} | all-to-all | bytes 262144 | tf_op jit(solution)/shard_map/all_to_all | solution.py:437
  72.0 0.0 copy-done.5
  72.0 1.0 %shard_map.78 = f32[2,8,8,512]{3,2,1,0:T(8,128)} custom-call(f32[128,512]{1,0:T(8,128)S(1)} %get-tuple-element.11.near, f32[16,512]{1,0:T(8,128)S(1)} %get-tuple-element.13.gains, f32[256,128]{1,0:T(8,128)S(1)} %bitcast.1, f32[128,80]{1,0:T(8,128)S(1)} %copy-done.5), custom_call_target="tpu_custom_call" | custom-call | tf_op jit(solution)/shard_map/pallas_call | solution.py:98
Async XLA Ops:
  0.0 6.4 %copy-start.2 = (f32[8,8,512]{2,1,0:T(8,128)S(1)}, f32[8,8,512]{2,1,0:T(8,128)}, u32[]{:S(2)}) copy-start(f32[8,8,512]{2,1,0:T(8,128)} %volt.5) | copy-start | bytes 393220
  0.0 6.4 %copy-start = (f32[3,8,8,512]{3,2,1,0:T(8,128)S(1)}, f32[3,8,8,512]{3,2,1,0:T(8,128)}, u32[]{:S(2)}) copy-start(f32[3,8,8,512]{3,2,1,0:T(8,128)} %vel.5) | copy-start | bytes 1179652
  0.0 6.4 %copy-start.1 = (f32[2,8,8,512]{3,2,1,0:T(8,128)S(1)}, f32[2,8,8,512]{3,2,1,0:T(8,128)}, u32[]{:S(2)}) copy-start(f32[2,8,8,512]{3,2,1,0:T(8,128)} %conc.5) | copy-start | bytes 786436
  0.9 16.1 %collective-permute-start = (f32[4,8,512]{2,1,0:T(8,128)S(1)}, f32[4,8,512]{2,1,0:T(8,128)S(1)}, u32[]{:S(2)}, u32[]{:S(2)}) collective-permute-start(f32[4,8,512]{2,1,0:T(8,128)S(1)} %shard_map.74), channel_id=1, source_target_pairs={{0,1},{1,2},{2,3},{3,4},{4,5},{5,6},{6,7},{7,8},{8,9},{9,10},{10,1... | collective-permute-start | bytes 196616 | tf_op jit(solution)/shard_map/ppermute | solution.py:398
  6.4 0.9 %copy-start.4 = (f32[192,128]{1,0:T(8,128)S(1)}, f32[192,128]{1,0:T(8,128)}, u32[]{:S(2)}) copy-start(f32[192,128]{1,0:T(8,128)} %constant.8.clone.table) | copy-start | bytes 294916
  17.1 16.1 %copy-start.3 = (f32[256,128]{1,0:T(8,128)S(1)}, f32[256,128]{1,0:T(8,128)}, u32[]{:S(2)}) copy-start(f32[256,128]{1,0:T(8,128)} %constant.10.clone.solve) | copy-start | bytes 393220
  17.1 16.0 %copy-start.6 = (f32[128,128]{1,0:T(8,128)S(1)}, f32[128,128]{1,0:T(8,128)}, u32[]{:S(2)}) copy-start(f32[128,128]{1,0:T(8,128)} %constant.9.clone.collect) | copy-start | bytes 196612
  56.4 15.6 %copy-start.5 = (f32[128,80]{1,0:T(8,128)S(1)}, f32[128,80]{1,0:T(8,128)}, u32[]{:S(2)}) copy-start(f32[128,80]{1,0:T(8,128)} %constant.11.clone.table) | copy-start | bytes 122884
